TPU v7x, 32 devices: a whole 2x2x4 slice. The times are simulated.
32 devices in a mesh: dp: 4 (over x, core), seq: 8 (over z, y).
Axes of the slice: x: 2, y: 2, z: 4, core: 2. Of those that a mesh axis runs over, the one named last changes fastest.
Arguments:
- tokens: bfloat16 [4, 1024, 2048], P('dp', 'seq'), may hold values from -6 to 6
- segment_ids: int32 [4, 1024], P('dp', 'seq'), may hold values from 0 to 4, as said below
- gain_attn: bfloat16 [2048], P(('dp', 'seq')), may hold values from 0.25 to 1.75
- w_query: bfloat16 [2048, 2048], P(('dp', 'seq')), may hold values from -0.125 to 0.125
- w_key: bfloat16 [2048, 256], P(('dp', 'seq')), may hold values from -0.125 to 0.125
- w_value: bfloat16 [2048, 256], P(('dp', 'seq')), may hold values from -0.125 to 0.125
- w_output: bfloat16 [2048, 2048], P(('dp', 'seq')), may hold values from -2 to 2
- gain_mlp: bfloat16 [2048], P(('dp', 'seq')), may hold values from 0.25 to 1.75
- w_gate: bfloat16 [2048, 5632], P(('dp', 'seq')), may hold values from -0.125 to 0.125
- w_up: bfloat16 [2048, 5632], P(('dp', 'seq')), may hold values from -0.125 to 0.125
- w_down: bfloat16 [5632, 2048], P(('dp', 'seq')), may hold values from -0.078125 to 0.078125
- cotangent: bfloat16 [4, 1024, 2048], P('dp', 'seq'), may hold values from -6 to 6
Outputs:
- out_tokens: bfloat16 [4, 1024, 2048], P('dp', 'seq')
- grad_tokens: float32 [4, 1024, 2048], P('dp', 'seq')
- grad_gain_attn: float32 [2048], P(('dp', 'seq'))
- grad_query: float32 [2048, 2048], P(('dp', 'seq'))
- grad_key: float32 [2048, 256], P(('dp', 'seq'))
- grad_value: float32 [2048, 256], P(('dp', 'seq'))
- grad_output: float32 [2048, 2048], P(('dp', 'seq'))
- grad_gain_mlp: float32 [2048], P(('dp', 'seq'))
- grad_gate: float32 [2048, 5632], P(('dp', 'seq'))
- grad_up: float32 [2048, 5632], P(('dp', 'seq'))
- grad_down: float32 [5632, 2048], P(('dp', 'seq'))
Inputs may be any that keep to these rules, and one draw needn't show every extreme that they name: `segment_ids`: ids never fall along a row; in each row one document starts within the first 128 positions and ends within the last 128.
All inputs are finite; a program needn't handle non-finite values.
Results may differ from a plain program's by a relative error of at most 0.015.
Values may be sent and summed in bfloat16 or wider, within the bound.
A program may use at most 384 MiB of HBM per device.

v0:
```python
import functools
import math

import jax
import jax.numpy as jnp
from jax import lax
from jax.sharding import PartitionSpec as P

HEADS = 32
HEAD_DIM = 64
KV_HEADS = 4


EPS = 1e-05
ROPE_BASE = 10000.0
MASK_VALUE = -1e30


def for_sending(value):

    def short(part):
        return part.astype(jnp.bfloat16) if part.dtype == jnp.float32 else part

    return jax.tree.map(short, value)


def matmul(left, right):
    return jnp.dot(left, right, preferred_element_type=jnp.float32)


def angles(positions):
    freqs = ROPE_BASE ** (-jnp.arange(0, HEAD_DIM, 2).astype(jnp.float32) / HEAD_DIM)
    turned = positions.astype(jnp.float32)[:, None] * freqs[None, :]
    return (jnp.cos(turned)[:, None, :], jnp.sin(turned)[:, None, :])


def rotate(values, cosines, sines):
    half = values.shape[-1] // 2
    first = values[..., :half]
    second = values[..., half:]
    return jnp.concatenate([first * cosines - second * sines, second * cosines + first * sines], -1)


def row_positions(segments):
    index = jnp.arange(segments.shape[0], dtype=jnp.int32)
    fresh = jnp.concatenate([jnp.ones((1,), dtype=jnp.bool_), segments[1:] != segments[:-1]])
    starts = lax.cummax(jnp.where(fresh, index, jnp.zeros_like(index)), axis=0)
    return index - starts


def gather_weights(pieces):
    return jax.tree.map(
        lambda part, own: part.astype(own.dtype),
        lax.all_gather(for_sending(pieces), ("dp", "seq"), axis=0, tiled=True),
        pieces,
    )


def scatter_grads(terms):
    return lax.psum_scatter(terms, ("dp", "seq"), scatter_dimension=0, tiled=True)


def norm_back(grad_normed, normed, scale):
    return scale * (grad_normed - normed * jnp.mean(grad_normed * normed, -1, keepdims=True))


def body(
    tokens,
    segment_ids,
    gain_attn,
    w_query,
    w_key,
    w_value,
    w_output,
    gain_mlp,
    w_gate,
    w_up,
    w_down,
    cotangent,
):
    rows = tokens.shape[0]
    local = tokens.shape[1]
    width = tokens.shape[2]
    flat = rows * local
    group = HEADS // KV_HEADS
    kv_width = KV_HEADS * HEAD_DIM
    factor = HEAD_DIM ** (-0.5)
    row_segs = lax.all_gather(segment_ids, "seq", axis=1, tiled=True)
    length = row_segs.shape[1]
    offset = lax.axis_index("seq") * local
    my_index = offset + jnp.arange(local, dtype=jnp.int32)
    my_segs = lax.dynamic_slice_in_dim(row_segs, offset, local, 1)
    my_places = lax.dynamic_slice_in_dim(jax.vmap(row_positions)(row_segs), offset, local, 1)
    cosines, sines = angles(my_places.reshape(flat))
    attn_set = gather_weights((gain_attn, w_query, w_key, w_value, w_output))
    attn_gain, query_w, key_w, value_w, output_w = attn_set
    inputs = tokens.reshape(flat, width).astype(jnp.float32)
    scale_one = lax.rsqrt(jnp.mean(inputs * inputs, -1, keepdims=True) + EPS)
    norm_one = inputs * scale_one
    normed = (norm_one * attn_gain.astype(jnp.float32)).astype(jnp.bfloat16)
    query_rot = rotate(matmul(normed, query_w).reshape(flat, HEADS, HEAD_DIM), cosines, sines)
    queries = (
        (query_rot * factor).astype(jnp.bfloat16).reshape(rows, local, KV_HEADS, group, HEAD_DIM)
    )
    keys = rotate(matmul(normed, key_w).reshape(flat, KV_HEADS, HEAD_DIM), cosines, sines).astype(
        jnp.bfloat16
    )
    values = matmul(normed, value_w).astype(jnp.bfloat16)
    paired = jnp.concatenate([keys.reshape(flat, kv_width), values], 1).reshape(
        rows, local, 2 * kv_width
    )
    row_pairs = lax.all_gather(paired, "seq", axis=1, tiled=True)
    block = math.gcd(length, 512)
    last_block = (offset + local - 1) // block + 1

    def scores_at(row, number):
        start = number * block
        piece = lax.dynamic_slice_in_dim(row_pairs[row], start, block, 0)
        key_block = piece[:, :kv_width].reshape(block, KV_HEADS, HEAD_DIM)
        value_block = piece[:, kv_width:].reshape(block, KV_HEADS, HEAD_DIM)
        raw = jnp.einsum(
            "qgrd,kgd->grqk", queries[row], key_block, preferred_element_type=jnp.float32
        )
        key_index = start + jnp.arange(block, dtype=jnp.int32)
        key_segs = lax.dynamic_slice_in_dim(row_segs[row], start, block)
        allowed = (key_segs[None, :] == my_segs[row][:, None]) & (
            key_index[None, :] <= my_index[:, None]
        )
        return (raw, allowed, key_block, value_block, start)

    def max_step(row, number, carry):
        top, total = carry
        raw, allowed, key_block, value_block, start = scores_at(row, number)
        new_top = jnp.maximum(top, jnp.max(jnp.where(allowed, raw, MASK_VALUE), -1))
        fresh = jnp.sum(jnp.where(allowed, jnp.exp(raw - new_top[..., None]), 0.0), -1)
        return (new_top, total * jnp.exp(top - new_top) + fresh)

    def probs_at(raw, allowed, log_total):
        return jnp.where(allowed, jnp.exp(raw - log_total[..., None]), 0.0)

    def out_step(row, log_total, number, accum):
        raw, allowed, key_block, value_block, start = scores_at(row, number)
        probs = probs_at(raw, allowed, log_total).astype(jnp.bfloat16)
        return accum + jnp.einsum(
            "grqk,kgd->qgrd", probs, value_block, preferred_element_type=jnp.float32
        )

    stat_shape = (KV_HEADS, group, local)
    head_shape = (local, KV_HEADS, group, HEAD_DIM)
    row = 0
    top, total = lax.fori_loop(
        0,
        last_block,
        functools.partial(max_step, row),
        (jnp.full(stat_shape, MASK_VALUE, jnp.float32), jnp.zeros(stat_shape, jnp.float32)),
    )
    log_total = top + jnp.log(total)
    log_totals = [log_total]
    accum = lax.fori_loop(
        0,
        last_block,
        functools.partial(out_step, row, log_total),
        jnp.zeros(head_shape, jnp.float32),
    )
    attended_rows = accum.reshape(local, width)
    attended = attended_rows.astype(jnp.bfloat16)
    middle = inputs + matmul(attended, output_w)
    mlp_set = gather_weights((gain_mlp, w_gate, w_up, w_down))
    mlp_gain, gate_w, up_w, down_w = mlp_set
    scale_two = lax.rsqrt(jnp.mean(middle * middle, -1, keepdims=True) + EPS)
    norm_two = middle * scale_two
    second = (norm_two * mlp_gain.astype(jnp.float32)).astype(jnp.bfloat16)
    gate = matmul(second, gate_w)
    upward = matmul(second, up_w)
    sigma = jax.nn.sigmoid(gate)
    hidden = (gate * sigma * upward).astype(jnp.bfloat16)
    result = (middle + matmul(hidden, down_w)).astype(jnp.bfloat16).reshape(rows, local, width)
    attn_gain, query_w, key_w, value_w, output_w = gather_weights(
        (gain_attn, w_query, w_key, w_value, w_output)
    )
    mlp_gain, gate_w, up_w, down_w = gather_weights((gain_mlp, w_gate, w_up, w_down))
    grad_out = cotangent.reshape(flat, width)
    grad_down = jnp.einsum("tf,td->fd", hidden, grad_out, preferred_element_type=jnp.float32)
    grad_hidden = jnp.einsum("td,fd->tf", grad_out, down_w, preferred_element_type=jnp.float32)
    grad_gate = (grad_hidden * upward * sigma * (1.0 + gate * (1.0 - sigma))).astype(jnp.bfloat16)
    grad_up = (grad_hidden * gate * sigma).astype(jnp.bfloat16)
    grad_gate_w = jnp.einsum("td,tf->df", second, grad_gate, preferred_element_type=jnp.float32)
    grad_up_w = jnp.einsum("td,tf->df", second, grad_up, preferred_element_type=jnp.float32)
    grad_second = jnp.einsum("tf,df->td", grad_gate, gate_w, preferred_element_type=jnp.float32)
    grad_second = grad_second + jnp.einsum(
        "tf,df->td", grad_up, up_w, preferred_element_type=jnp.float32
    )
    grad_mlp_gain = jnp.sum(grad_second * norm_two, 0)
    grad_middle = grad_out.astype(jnp.float32) + norm_back(
        grad_second * mlp_gain.astype(jnp.float32), norm_two, scale_two
    )
    mlp_grads = scatter_grads((grad_mlp_gain, grad_gate_w, grad_up_w, grad_down))
    middle_low = grad_middle.astype(jnp.bfloat16)
    grad_output_w = jnp.einsum(
        "td,te->de", attended, middle_low, preferred_element_type=jnp.float32
    )
    grad_attended = jnp.einsum(
        "te,de->td", middle_low, output_w, preferred_element_type=jnp.float32
    )
    grad_attended = grad_attended.astype(jnp.bfloat16).reshape(
        rows, local, KV_HEADS, group, HEAD_DIM
    )

    def delta_step(row, log_total, number, accum):
        raw, allowed, key_block, value_block, start = scores_at(row, number)
        probs = probs_at(raw, allowed, log_total)
        grad_probs = jnp.einsum(
            "qgrd,kgd->grqk", grad_attended[row], value_block, preferred_element_type=jnp.float32
        )
        return accum + jnp.sum(probs * grad_probs, -1)

    def grad_step(row, log_total, delta, number, carry):
        grad_queries, row_grads = carry
        raw, allowed, key_block, value_block, start = scores_at(row, number)
        probs = probs_at(raw, allowed, log_total)
        grad_probs = jnp.einsum(
            "qgrd,kgd->grqk", grad_attended[row], value_block, preferred_element_type=jnp.float32
        )
        grad_raw = (probs * (grad_probs - delta[..., None])).astype(jnp.bfloat16)
        grad_queries = grad_queries + jnp.einsum(
            "grqk,kgd->qgrd", grad_raw, key_block, preferred_element_type=jnp.float32
        )
        grad_keys = jnp.einsum(
            "grqk,qgrd->kgd", grad_raw, queries[row], preferred_element_type=jnp.float32
        )
        grad_values = jnp.einsum(
            "grqk,qgrd->kgd",
            probs.astype(jnp.bfloat16),
            grad_attended[row],
            preferred_element_type=jnp.float32,
        )
        piece = jnp.concatenate(
            [grad_keys.reshape(block, kv_width), grad_values.reshape(block, kv_width)], 1
        )
        return (grad_queries, lax.dynamic_update_slice_in_dim(row_grads, piece, start, 0))

    row = 0
    delta = lax.fori_loop(
        0,
        last_block,
        functools.partial(delta_step, row, log_totals[row]),
        jnp.zeros(stat_shape, jnp.float32),
    )
    grad_queries, row_grads = lax.fori_loop(
        0,
        last_block,
        functools.partial(grad_step, row, log_totals[row], delta),
        (jnp.zeros(head_shape, jnp.float32), jnp.zeros((length, 2 * kv_width), jnp.float32)),
    )
    query_grad_rows = grad_queries.reshape(local, HEADS, HEAD_DIM)
    key_grad_rows = [row_grads]
    grad_queries = query_grad_rows
    own_grads = (
        lax.psum_scatter(
            jnp.stack(key_grad_rows, 0).astype(jnp.bfloat16), "seq", scatter_dimension=1, tiled=True
        )
        .astype(jnp.float32)
        .reshape(flat, 2 * kv_width)
    )
    grad_key_pre = rotate(
        own_grads[:, :kv_width].reshape(flat, KV_HEADS, HEAD_DIM), cosines, -sines
    )
    grad_key_pre = grad_key_pre.reshape(flat, kv_width).astype(jnp.bfloat16)
    grad_value_pre = own_grads[:, kv_width:].astype(jnp.bfloat16)
    grad_query_pre = rotate(grad_queries * factor, cosines, -sines)
    grad_query_pre = grad_query_pre.reshape(flat, width).astype(jnp.bfloat16)
    grad_query_w = jnp.einsum(
        "td,te->de", normed, grad_query_pre, preferred_element_type=jnp.float32
    )
    grad_key_w = jnp.einsum("td,te->de", normed, grad_key_pre, preferred_element_type=jnp.float32)
    grad_value_w = jnp.einsum(
        "td,te->de", normed, grad_value_pre, preferred_element_type=jnp.float32
    )
    grad_normed = jnp.einsum(
        "te,de->td", grad_query_pre, query_w, preferred_element_type=jnp.float32
    )
    grad_normed = grad_normed + jnp.einsum(
        "te,de->td", grad_key_pre, key_w, preferred_element_type=jnp.float32
    )
    grad_normed = grad_normed + jnp.einsum(
        "te,de->td", grad_value_pre, value_w, preferred_element_type=jnp.float32
    )
    grad_attn_gain = jnp.sum(grad_normed * norm_one, 0)
    grad_inputs = grad_middle + norm_back(
        grad_normed * attn_gain.astype(jnp.float32), norm_one, scale_one
    )
    attn_grads = scatter_grads(
        (grad_attn_gain, grad_query_w, grad_key_w, grad_value_w, grad_output_w)
    )
    return (
        result,
        grad_inputs.reshape(rows, local, width),
        attn_grads[0],
        attn_grads[1],
        attn_grads[2],
        attn_grads[3],
        attn_grads[4],
        mlp_grads[0],
        mlp_grads[1],
        mlp_grads[2],
        mlp_grads[3],
    )


def solution(mesh):
    return jax.shard_map(
        body,
        mesh=mesh,
        in_specs=(
            P("dp", "seq", None),
            P("dp", "seq"),
            P(("dp", "seq")),
            P(("dp", "seq"), None),
            P(("dp", "seq"), None),
            P(("dp", "seq"), None),
            P(("dp", "seq"), None),
            P(("dp", "seq")),
            P(("dp", "seq"), None),
            P(("dp", "seq"), None),
            P(("dp", "seq"), None),
            P("dp", "seq", None),
        ),
        out_specs=(
            P("dp", "seq", None),
            P("dp", "seq", None),
            P(("dp", "seq")),
            P(("dp", "seq"), None),
            P(("dp", "seq"), None),
            P(("dp", "seq"), None),
            P(("dp", "seq"), None),
            P(("dp", "seq")),
            P(("dp", "seq"), None),
            P(("dp", "seq"), None),
            P(("dp", "seq"), None),
        ),
        check_vma=False,
    )
```

profile of v0, /device:TPU:0, one launch (start us, length us, event | category | flops | bytes accessed | tf_op | source)
XLA Modules:
  0.0 4824.5 jit_solution(5235300983261720969)
XLA Ops:
  8.7 22.3 all_gather.44
  32.8 37.1 all-reduce.5
  76.0 47.6 all-gather.12.cloned.1.call-done
  129.3 36.0 all-gather.24.cloned.1.call-done
  166.8 77.5 %all-gather.14.cloned.1.call-done = bf16[2048,2048]{1,0:T(8,128)(2,1)} async-done(((bf16[64,2048]{1,0:T(8,128)(2,1)}), bf16[2048,2048]{1,0:T(8,128)(2,1)}) %all-gather.14.cloned.1.call-update) | async-done | bytes 8388624 | tf_op jit(solution)/shard_map/all_gather | solution.py:54
  244.4 12.4 copy.55
  274.2 49.1 %all-gather.16.cloned.1.call-done = bf16[2048,2048]{1,0:T(8,128)(2,1)} async-done(((bf16[64,2048]{1,0:T(8,128)(2,1)}), bf16[2048,2048]{1,0:T(8,128)(2,1)}) %all-gather.16.cloned.1.call-update) | async-done | bytes 8388624 | tf_op jit(solution)/shard_map/all_gather | solution.py:54
  328.3 140.9 %all-gather.18.cloned.1.call-done = bf16[2048,5632]{1,0:T(8,128)(2,1)} async-done(((bf16[64,5632]{1,0:T(8,128)(2,1)}), bf16[2048,5632]{1,0:T(8,128)(2,1)}) %all-gather.18.cloned.1.call-update) | async-done | bytes 23068688 | tf_op jit(solution)/shard_map/all_gather | solution.py:54
  469.2 12.3 fusion.94
  481.6 133.4 %all-gather.20.cloned.1.call-done = bf16[2048,5632]{1,0:T(8,128)(2,1)} async-done(((bf16[64,5632]{1,0:T(8,128)(2,1)}), bf16[2048,5632]{1,0:T(8,128)(2,1)}) %all-gather.20.cloned.1.call-update) | async-done | bytes 23068688 | tf_op jit(solution)/shard_map/all_gather | solution.py:54
  615.0 12.3 fusion.95
  627.2 133.5 %all-gather.22.cloned.1.call-done = bf16[5632,2048]{1,0:T(8,128)(2,1)} async-done(((bf16[176,2048]{1,0:T(8,128)(2,1)}), bf16[5632,2048]{1,0:T(8,128)(2,1)}) %all-gather.22.cloned.1.call-update) | async-done | bytes 23068688 | tf_op jit(solution)/shard_map/all_gather | solution.py:54
  760.7 15.8 multiply_convert_fusion
  776.5 13.1 fusion.96
  789.6 14.1 multiply_reduce_fusion
  806.1 6.3 convolution_convert_fusion
  818.8 9.2 while.51
  837.0 74.8 %reduce-scatter.25.cloned.1.call-done = bf16[128,512]{1,0:T(8,128)(2,1)} async-done(((bf16[1024,512]{1,0:T(8,128)(2,1)}), bf16[128,512]{1,0:T(8,128)(2,1)}) %reduce-scatter.25.cloned.1.call-update) | async-done | bytes 131088
  917.4 8.3 fusion.71
  927.0 8.2 fusion.73
  936.2 19.2 fusion.98
  955.5 19.3 fusion.99
  975.8 19.2 fusion.61
  995.1 6.5 fusion.97
  1001.6 11.8 fusion.43
  1015.5 40.3 all-reduce.4
  1059.6 130.3 %reduce-scatter.15.cloned.1.call-done = f32[64,256]{1,0:T(8,128)} async-done(((f32[2048,256]{1,0:T(8,128)}), f32[64,256]{1,0:T(8,128)}) %reduce-scatter.15.cloned.1.call-update) | async-done | bytes 65552 | tf_op jit(solution)/shard_map/reduce_scatter | solution.py:60
  1189.9 357.5 %reduce-scatter.11.cloned.1.call-done = f32[64,2048]{1,0:T(8,128)} async-done(((f32[2048,2048]{1,0:T(8,128)}), f32[64,2048]{1,0:T(8,128)}) %reduce-scatter.11.cloned.1.call-update) | async-done | bytes 524304 | tf_op jit(solution)/shard_map/reduce_scatter | solution.py:60
  1547.4 360.3 %reduce-scatter.17.cloned.1.call-done = f32[64,2048]{1,0:T(8,128)} async-done(((f32[2048,2048]{1,0:T(8,128)}), f32[64,2048]{1,0:T(8,128)}) %reduce-scatter.17.cloned.1.call-update) | async-done | bytes 524304 | tf_op jit(solution)/shard_map/reduce_scatter | solution.py:60
  1907.7 969.4 %reduce-scatter.19.cloned.1.call-done = f32[64,5632]{1,0:T(8,128)} async-done(((f32[2048,5632]{1,0:T(8,128)}), f32[64,5632]{1,0:T(8,128)}) %reduce-scatter.19.cloned.1.call-update) | async-done | bytes 1441808 | tf_op jit(solution)/shard_map/reduce_scatter | solution.py:60
  2877.2 970.2 %reduce-scatter.21.cloned.1.call-done = f32[64,5632]{1,0:T(8,128)} async-done(((f32[2048,5632]{1,0:T(8,128)}), f32[64,5632]{1,0:T(8,128)}) %reduce-scatter.21.cloned.1.call-update) | async-done | bytes 1441808 | tf_op jit(solution)/shard_map/reduce_scatter | solution.py:60
  3847.3 970.2 %reduce-scatter.23.cloned.1.call-done = f32[176,2048]{1,0:T(8,128)} async-done(((f32[5632,2048]{1,0:T(8,128)}), f32[176,2048]{1,0:T(8,128)}) %reduce-scatter.23.cloned.1.call-update) | async-done | bytes 1441808 | tf_op jit(solution)/shard_map/reduce_scatter | solution.py:60
  (194 shorter events, 92.1 us)
Async XLA Ops:
  7.2 65.6 %all-gather.10.cloned.1.call-start = ((), (), s32[]{:S(2)}) async-start(), calls=%async_computation.8 | async-start | bytes 1081344 | tf_op jit(solution)/shard_map/all_gather | solution.py:54
  7.9 115.7 %all-gather.12.cloned.1.call-start = ((), (), s32[]{:S(2)}) async-start(), calls=%async_computation.9 | async-start | bytes 1081344 | tf_op jit(solution)/shard_map/all_gather | solution.py:54
  8.7 156.7 %all-gather.24.cloned.1.call-start = ((), (), s32[]{:S(2)}) async-start(), calls=%async_computation.22 | async-start | bytes 1179648 | tf_op jit(solution)/shard_map/all_gather | solution.py:112
  69.9 186.8 %copy-start.19 = (f32[2048]{0:T(1024)}, f32[2048]{0:T(1024)S(1)}, u32[]{:S(2)}) copy-start(f32[2048]{0:T(1024)S(1)} %convert_element_type.135) | copy-start | bytes 24580
  72.0 184.7 %copy-start.25 = (f32[128]{0:T(128)}, f32[128]{0:T(128)S(1)}, u32[]{:S(2)}) copy-start(f32[128]{0:T(128)S(1)} %add_rsqrt_fusion.1) | copy-start | bytes 1540
  72.8 189.8 %copy-start.21 = (f32[128,32]{0,1:T(8,128)}, f32[128,32]{0,1:T(8,128)S(1)}, u32[]{:S(2)}) copy-start(f32[128,32]{0,1:T(8,128)S(1)} %get-tuple-element.556) | copy-start | bytes 49156
  126.0 118.3 %all-gather.14.cloned.1.call-start = ((), (), s32[]{:S(2)}) async-start(), calls=%async_computation.10 | async-start | bytes 8650752 | tf_op jit(solution)/shard_map/all_gather | solution.py:54
  126.6 196.6 %all-gather.16.cloned.1.call-start = ((), (), s32[]{:S(2)}) async-start(), calls=%async_computation.11 | async-start | bytes 8650752 | tf_op jit(solution)/shard_map/all_gather | solution.py:54
  127.2 342.0 %all-gather.18.cloned.1.call-start = ((), (), s32[]{:S(2)}) async-start(), calls=%async_computation.12 | async-start | bytes 23789568 | tf_op jit(solution)/shard_map/all_gather | solution.py:54
  127.8 487.2 %all-gather.20.cloned.1.call-start = ((), (), s32[]{:S(2)}) async-start(), calls=%async_computation.13 | async-start | bytes 23789568 | tf_op jit(solution)/shard_map/all_gather | solution.py:54
  128.5 632.2 %all-gather.22.cloned.1.call-start = ((), (), s32[]{:S(2)}) async-start(), calls=%async_computation.14 | async-start | bytes 23789568 | tf_op jit(solution)/shard_map/all_gather | solution.py:54
  129.3 782.5 %reduce-scatter.25.cloned.1.call-start = ((), (), s32[]{:S(2)}) async-start(), calls=%async_computation.23 | async-start | bytes 1179648
  244.4 12.4 copy-start
  328.1 475.5 %copy-start.2 = (f32[128,2048]{1,0:T(8,128)}, f32[128,2048]{1,0:T(8,128)S(1)}, u32[]{:S(2)}) copy-start(f32[128,2048]{1,0:T(8,128)S(1)} %get-tuple-element.558) | copy-start | bytes 3145732
  328.3 286.6 %copy-start.6 = (bf16[128,2048]{1,0:T(8,128)(2,1)}, bf16[128,2048]{1,0:T(8,128)(2,1)S(1)}, u32[]{:S(2)}) copy-start(bf16[128,2048]{1,0:T(8,128)(2,1)S(1)} %multiply_convert_fusion.3) | copy-start | bytes 1572868
  776.5 13.1 copy-start.8
  789.5 14.1 copy-start.14
  828.0 85.0 %copy-start.22 = (f32[128,32]{0,1:T(8,128)S(1)}, f32[128,32]{0,1:T(8,128)}, u32[]{:S(2)}) copy-start(f32[128,32]{0,1:T(8,128)} %copy-done.21) | copy-start | bytes 49156
  828.0 85.0 %copy-start.23 = (f32[128,32]{0,1:T(8,128)S(1)}, f32[128,32]{0,1:T(8,128)}, u32[]{:S(2)}) copy-start(f32[128,32]{0,1:T(8,128)} %get-tuple-element.554) | copy-start | bytes 49156
  828.1 85.1 %copy-start.1 = (bf16[1,128,2048]{2,1,0:T(8,128)(2,1)S(1)}, bf16[1,128,2048]{2,1,0:T(8,128)(2,1)}, u32[]{:S(2)}) copy-start(bf16[1,128,2048]{2,1,0:T(8,128)(2,1)} %param.20) | copy-start | bytes 1572868
  828.1 85.1 %copy-start.20 = (f32[2048]{0:T(1024)S(1)}, f32[2048]{0:T(1024)}, u32[]{:S(2)}) copy-start(f32[2048]{0:T(1024)} %copy-done.19) | copy-start | bytes 24580
  828.1 85.1 %copy-start.26 = (f32[128]{0:T(128)S(1)}, f32[128]{0:T(128)}, u32[]{:S(2)}) copy-start(f32[128]{0:T(128)} %copy-done.25) | copy-start | bytes 1540
  837.0 222.6 %reduce-scatter.13.cloned.1.call-start = ((), (), s32[]{:S(2)}) async-start(), calls=%async_computation.16 | async-start | bytes 2162688 | tf_op jit(solution)/shard_map/reduce_scatter | solution.py:60
  915.0 274.9 %reduce-scatter.15.cloned.1.call-start = ((), (), s32[]{:S(2)}) async-start(), calls=%async_computation.17 | async-start | bytes 2162688 | tf_op jit(solution)/shard_map/reduce_scatter | solution.py:60
  917.0 630.4 %reduce-scatter.11.cloned.1.call-start = ((), (), s32[]{:S(2)}) async-start(), calls=%async_computation.15 | async-start | bytes 17301504 | tf_op jit(solution)/shard_map/reduce_scatter | solution.py:60
  925.7 982.0 %reduce-scatter.17.cloned.1.call-start = ((), (), s32[]{:S(2)}) async-start(), calls=%async_computation.18 | async-start | bytes 17301504 | tf_op jit(solution)/shard_map/reduce_scatter | solution.py:60
  935.2 1942.0 %reduce-scatter.19.cloned.1.call-start = ((), (), s32[]{:S(2)}) async-start(), calls=%async_computation.19 | async-start | bytes 47579136 | tf_op jit(solution)/shard_map/reduce_scatter | solution.py:60
  955.5 2891.9 %reduce-scatter.21.cloned.1.call-start = ((), (), s32[]{:S(2)}) async-start(), calls=%async_computation.20 | async-start | bytes 47579136 | tf_op jit(solution)/shard_map/reduce_scatter | solution.py:60
  974.8 3842.7 %reduce-scatter.23.cloned.1.call-start = ((), (), s32[]{:S(2)}) async-start(), calls=%async_computation.21 | async-start | bytes 47579136 | tf_op jit(solution)/shard_map/reduce_scatter | solution.py:60
  1001.6 11.9 copy-start.11
  1001.6 12.3 copy-start.16
  1001.6 13.9 copy-start.24
  (11 other events, 24.9 us)
Sparse Core Ops, SparseCore 0:
  11.1 56.5 all-gather.9
  70.8 52.7 all-gather.11
  126.3 38.9 all-gather.23
  168.2 76.1 all-gather.13
  247.2 75.9 all-gather.15
  326.0 143.1 all-gather.17
  472.1 142.7 all-gather.19
  617.9 142.7 all-gather.21
  837.1 74.6 reduce-scatter.24
  915.1 136.9 reduce-scatter.12
  1055.0 134.8 reduce-scatter.14
  1192.7 354.5 reduce-scatter.10
  1550.4 357.3 reduce-scatter.16
  1910.6 966.5 reduce-scatter.18
  2880.0 967.3 reduce-scatter.20
  3850.2 967.3 reduce-scatter.22
where the time goes:
time: 4830 us; the launch traced here: 4820 us
  waiting for transfers between devices  4460 us (92%)
  matrix products  203 us (4%)
  blocking collectives  99.7 us (2%)
    reduce_scatter x7, waiting for transfers between devices, scatter_grads(): lax.psum_scatter(terms, ('dp', 'seq'), scatter_dimension=0, tiled=True)  3760 us
    all_gather x7, waiting for transfers between devices, gather_weights(): lax.all_gather(for_sending(pieces), ('dp', 'seq'), axis=0, tiled=True)  582 us
  transfers between devices with their start and end apart: 16, of which 14 were waited for; matrix products, arithmetic and copies ran while one was open for 3% of the time, Pallas kernels for 0%

commit v1 on v0

v1 whole, which is shorter than its diff:
```python
import functools

import jax
import jax.numpy as jnp
from jax import lax
from jax.experimental import pallas as pl
from jax.experimental.pallas import tpu as pltpu
from jax.sharding import PartitionSpec as P

HEADS = 32
HEAD_DIM = 64
KV_HEADS = 4
GROUP = HEADS // KV_HEADS

EPS = 1e-05
ROPE_BASE = 10000.0
MASK_VALUE = -1e30
MESH = pl.DeviceIdType.MESH
LOW = jnp.bfloat16
FULL = jnp.float32
VMEM_BYTES = 56 * 1024 * 1024


def matmul(left, right):
    return jnp.dot(left, right, preferred_element_type=FULL)


def matmul_nt(left, right):
    return lax.dot_general(left, right, (((1,), (1,)), ((), ())), preferred_element_type=FULL)


def matmul_tn(left, right):
    return lax.dot_general(left, right, (((0,), (0,)), ((), ())), preferred_element_type=FULL)


def ring_at(place, n):
    upper = lax.div(place, n // 2)
    return (1 - upper) * 2 * place + upper * (2 * (n - place) - 1)


def ring_place(index, n):
    odd = lax.rem(index, 2)
    return (1 - odd) * lax.div(index, 2) + odd * (n - lax.div(index + 1, 2))


class Where:
    def __init__(self, n_dp, n_seq):
        self.n_dp, self.n_seq = n_dp, n_seq
        self.chips = n_dp // 2
        self.dp = lax.axis_index("dp")
        self.seq = lax.axis_index("seq")
        self.core = lax.rem(self.dp, 2)
        self.chip = lax.div(self.dp, 2)
        self.place = ring_place(self.seq, n_seq)

    def ring(self, step):
        return ring_at(lax.rem(self.place + step + self.n_seq, self.n_seq), self.n_seq)

    def ring_ids(self):
        return [(self.dp, self.ring(1)), (self.dp, self.ring(-1))]

    def seq_ids(self):
        return [
            (self.dp, lax.rem(self.seq + k, self.n_seq)) for k in range(1, self.n_seq)
        ]

    def core_id(self):
        return (self.dp + 1 - 2 * self.core, self.seq)

    def chip_ids(self):
        return [
            (2 * lax.rem(self.chip + k, self.chips) + self.core, self.seq)
            for k in range(1, self.chips)
        ]


def greet(ids):
    barrier = pltpu.get_barrier_semaphore()
    for one in ids:
        pl.semaphore_signal(barrier, inc=1, device_id=one, device_id_type=MESH)
    pl.semaphore_wait(barrier, len(ids))


def remote(src, dst, send, recv, target):
    return pltpu.make_async_remote_copy(
        src_ref=src,
        dst_ref=dst,
        send_sem=send,
        recv_sem=recv,
        device_id=target,
        device_id_type=MESH,
    )


class RingGather:
    def __init__(self, at, own, everything, send, recv, local):
        self.at, self.own, self.everything = at, own, everything
        self.send, self.recv = send, recv
        self.steps = at.n_seq // 2
        self.half = own.shape[0] // 2
        self.copies = {}
        self.kept = pltpu.make_async_copy(own, everything.at[at.seq], local)

    @staticmethod
    def scratch(n_seq):
        shape = (2, n_seq // 2, 2)
        return [pltpu.SemaphoreType.DMA(shape), pltpu.SemaphoreType.DMA(shape)]

    def step(self, t):
        at = self.at
        if t == 0:
            self.kept.start()
        for h in (0, 1):
            for d in (0, 1):
                if t == self.steps - 1 and h != d:
                    continue
                if t > 0:
                    self.copies[(d, t - 1, h)].wait_recv()
                origin = at.ring(-t if d == 0 else t)
                rows = pl.ds(h * self.half, self.half)
                dst = self.everything.at[origin, rows]
                src = self.own.at[rows] if t == 0 else dst
                copy = remote(
                    src, dst, self.send.at[d, t, h], self.recv.at[d, t, h], at.ring_ids()[d]
                )
                copy.start()
                self.copies[(d, t, h)] = copy

    def finish(self):
        last = self.steps - 1
        for (d, t, h), copy in self.copies.items():
            if t == last or (t == last - 1 and h != d):
                copy.wait_recv()
        for copy in self.copies.values():
            copy.wait_send()
        self.kept.wait()


class RingScatter:
    def __init__(self, at, parts, slots, send, recv):
        self.at, self.parts, self.slots = at, parts, slots
        self.send, self.recv = send, recv
        self.steps = at.n_seq // 2
        self.half = parts.shape[1] // 2
        self.copies = {}

    @staticmethod
    def scratch(n_seq, rows, columns):
        shape = (2, n_seq // 2, 2)
        return [
            pltpu.VMEM((2, n_seq // 2, rows, columns), LOW),
            pltpu.SemaphoreType.DMA(shape),
            pltpu.SemaphoreType.DMA(shape),
        ]

    def step(self, t):
        at = self.at
        for h in (0, 1):
            for d in (0, 1):
                if t == 0 and h != d:
                    continue
                there = at.ring(self.steps - t if d == 0 else t - self.steps)
                rows = pl.ds(h * self.half, self.half)
                src = self.parts.at[there, rows]
                if t > 1 or (t == 1 and h == d):
                    self.copies[(d, t - 1, h)].wait_recv()
                    held = self.slots.at[d, t - 1, rows]
                    held[...] = (held[...].astype(FULL) + src[...].astype(FULL)).astype(LOW)
                    src = held
                copy = remote(
                    src,
                    self.slots.at[d, t, rows],
                    self.send.at[d, t, h],
                    self.recv.at[d, t, h],
                    at.ring_ids()[d],
                )
                copy.start()
                self.copies[(d, t, h)] = copy

    def finish(self, out):
        last = self.steps - 1
        for h in (0, 1):
            rows = pl.ds(h * self.half, self.half)
            total = self.parts[self.at.seq, rows].astype(FULL)
            for d in (0, 1):
                if last == 0 and h != d:
                    continue
                self.copies[(d, last, h)].wait_recv()
                total = total + self.slots[d, last, rows].astype(FULL)
            out[rows] = total
        for copy in self.copies.values():
            copy.wait_send()


class SeqExchange:
    def __init__(self, at, packed, landing, send, recv, local):
        self.kept = pltpu.make_async_copy(packed.at[at.seq], landing.at[at.seq], local)
        self.copies = [
            remote(packed.at[one[1]], landing.at[at.seq], send.at[k], recv.at[k], one)
            for k, one in enumerate(at.seq_ids())
        ]

    @staticmethod
    def scratch(n_seq):
        return [pltpu.SemaphoreType.DMA((n_seq - 1,)), pltpu.SemaphoreType.DMA((n_seq - 1,))]

    def start(self):
        self.kept.start()
        for copy in self.copies:
            copy.start()

    def arrived(self):
        self.kept.wait()
        for copy in self.copies:
            copy.wait_recv()

    def finish(self):
        for copy in self.copies:
            copy.wait_send()


class DpGather:
    def __init__(self, at, everything, send, recv):
        self.at, self.everything, self.send, self.recv = at, everything, send, recv
        own = everything.at[at.dp]
        self.out = [
            remote(own, own, send.at[k], recv.at[k], one) for k, one in enumerate(at.chip_ids())
        ]
        base = at.chips - 1
        self.mate = remote(own, own, send.at[base], recv.at[base], at.core_id())
        self.handed = []
        for k in range(1, at.chips):
            origin = 2 * lax.rem(at.chip + at.chips - k, at.chips) + at.core
            there = everything.at[origin]
            self.handed.append(
                remote(there, there, send.at[base + k], recv.at[base + k], at.core_id())
            )

    @staticmethod
    def scratch(n_dp):
        return [pltpu.SemaphoreType.DMA((n_dp - 1,)), pltpu.SemaphoreType.DMA((n_dp - 1,))]

    def start(self):
        for copy in self.out:
            copy.start()
        self.mate.start()

    def hand(self):
        for copy, onward in zip(self.out, self.handed):
            copy.wait_recv()
            onward.start()

    def finish(self):
        self.mate.wait_recv()
        for copy in self.handed:
            copy.wait_recv()
        for copy in self.out + [self.mate] + self.handed:
            copy.wait_send()


def add_rows(rows, chunk, one):
    def step(r, carry):
        one(pl.ds(pl.multiple_of(r * chunk, chunk), chunk))
        return carry

    lax.fori_loop(0, rows // chunk, step, 0)


def chunk_of(rows, columns):
    chunk = rows
    while chunk % 32 == 0 and chunk * columns > 65536:
        chunk //= 2
    return chunk


class DpScatter:
    def __init__(self, at, parts, core, other, send, recv):
        self.at, self.parts, self.core, self.other = at, parts, core, other
        self.send, self.recv = send, recv
        self.rows, self.columns = parts.shape[1], parts.shape[2]

    @staticmethod
    def scratch(n_dp, rows, columns):
        chips = n_dp // 2
        return [
            pltpu.VMEM((chips, rows, columns), LOW),
            pltpu.VMEM((max(chips - 1, 1), rows, columns), LOW),
            pltpu.SemaphoreType.DMA((2 * chips - 1,)),
            pltpu.SemaphoreType.DMA((2 * chips - 1,)),
        ]

    def to_core(self, k):
        at = self.at
        return remote(
            self.parts.at[2 * k + 1 - at.core],
            self.core.at[k],
            self.send.at[k],
            self.recv.at[k],
            at.core_id(),
        )

    def to_chip(self, k):
        at = self.at
        sem = at.chips + k - 1
        return remote(
            self.core.at[lax.rem(at.chip + k, at.chips)],
            self.other.at[k - 1],
            self.send.at[sem],
            self.recv.at[sem],
            at.chip_ids()[k - 1],
        )

    def start(self):
        for k in range(self.at.chips):
            self.to_core(k).start()

    def add_core(self, k):
        held = self.core.at[k]
        mine = self.parts.at[2 * k + self.at.core]

        def one(rows):
            held[rows] = (held[rows].astype(FULL) + mine[rows].astype(FULL)).astype(LOW)

        add_rows(self.rows, chunk_of(self.rows, self.columns), one)

    def across(self):
        at = self.at
        for k in range(1, at.chips):
            there = lax.rem(at.chip + k, at.chips)
            self.to_core(there).wait_recv()
            self.add_core(there)
            self.to_chip(k).start()

    def finish(self, out):
        at = self.at
        self.to_core(at.chip).wait_recv()
        for k in range(1, at.chips):
            self.to_chip(k).wait_recv()
        held = self.core.at[at.chip]
        mine = self.parts.at[2 * at.chip + at.core]

        def one(rows):
            total = held[rows].astype(FULL) + mine[rows].astype(FULL)
            for k in range(1, at.chips):
                total = total + self.other[k - 1, rows].astype(FULL)
            out[rows] = total.astype(out.dtype)

        add_rows(self.rows, chunk_of(self.rows, self.columns), one)
        for k in range(at.chips):
            self.to_core(k).wait_send()
        for k in range(1, at.chips):
            self.to_chip(k).wait_send()


def comm_params(number):
    return pltpu.CompilerParams(
        collective_id=number, has_side_effects=True, vmem_limit_bytes=VMEM_BYTES
    )


ANY = pl.BlockSpec(memory_space=pl.ANY)
VMEM = pl.BlockSpec(memory_space=pltpu.VMEM)


def shape_of(dims, kind):
    return jax.ShapeDtypeStruct(dims, kind)


def spread_kernel(
    n_dp, n_seq, x, dy, seg, pq, pgu, wd, wo,
    x_all, dy_all, seg_all, q_all, gu_all, wd_all, wo_all,
    local, seg_s, seg_r, pq_s, pq_r, pgu_s, pgu_r, x_s, x_r, dy_s, dy_r,
    gq_s, gq_r, ggu_s, ggu_r, gd_s, gd_r, go_s, go_r,
):
    at = Where(n_dp, n_seq)
    greet(at.seq_ids() + [at.core_id()] + at.chip_ids())
    put_d = pltpu.make_async_copy(wd, wd_all.at[at.dp], local.at[0])
    put_o = pltpu.make_async_copy(wo, wo_all.at[at.dp], local.at[1])
    put_d.start()
    put_o.start()
    swap_q = SeqExchange(at, pq, q_all.at[at.dp], pq_s, pq_r, local.at[2])
    swap_seg = SeqExchange(at, seg, seg_all, seg_s, seg_r, local.at[3])
    swap_gu = SeqExchange(at, pgu, gu_all.at[at.dp], pgu_s, pgu_r, local.at[4])
    ring_x = RingGather(at, x, x_all, x_s, x_r, local.at[5])
    ring_dy = RingGather(at, dy, dy_all, dy_s, dy_r, local.at[6])
    dp_q = DpGather(at, q_all, gq_s, gq_r)
    dp_gu = DpGather(at, gu_all, ggu_s, ggu_r)
    dp_d = DpGather(at, wd_all, gd_s, gd_r)
    dp_o = DpGather(at, wo_all, go_s, go_r)
    swap_q.start()
    swap_seg.start()
    ring_x.step(0)
    put_o.wait()
    dp_o.start()
    put_d.wait()
    dp_d.start()
    swap_gu.start()
    swap_q.arrived()
    dp_q.start()
    for t in range(1, ring_x.steps):
        ring_x.step(t)
    dp_o.hand()
    dp_q.hand()
    dp_d.hand()
    ring_dy.step(0)
    swap_gu.arrived()
    dp_gu.start()
    for t in range(1, ring_dy.steps):
        ring_dy.step(t)
    dp_gu.hand()
    for one in (ring_x, swap_q, swap_seg, dp_o, dp_d, dp_q, swap_gu, ring_dy, dp_gu):
        if one is swap_seg:
            one.arrived()
        one.finish()


def spread(n_dp, n_seq, x, dy, seg, pq, pgu, wd, wo):
    scratch = [pltpu.SemaphoreType.DMA((7,))]
    for _ in range(3):
        scratch += SeqExchange.scratch(n_seq)
    for _ in range(2):
        scratch += RingGather.scratch(n_seq)
    for _ in range(4):
        scratch += DpGather.scratch(n_dp)
    return pl.pallas_call(
        functools.partial(spread_kernel, n_dp, n_seq),
        name="spread_inputs",
        out_shape=[
            shape_of((n_seq,) + x.shape, x.dtype),
            shape_of((n_seq,) + dy.shape, dy.dtype),
            shape_of(seg.shape, seg.dtype),
            shape_of((n_dp,) + pq.shape, LOW),
            shape_of((n_dp,) + pgu.shape, LOW),
            shape_of((n_dp,) + wd.shape, LOW),
            shape_of((n_dp,) + wo.shape, LOW),
        ],
        in_specs=[ANY] * 7,
        out_specs=[ANY] * 7,
        scratch_shapes=scratch,
        compiler_params=comm_params(1),
    )(x, dy, seg, pq, pgu, wd, wo)


def gather_kernel(n_dp, n_seq, own, everything, local, send, recv):
    at = Where(n_dp, n_seq)
    greet(at.ring_ids())
    ring = RingGather(at, own, everything, send, recv, local.at[0])
    for t in range(ring.steps):
        ring.step(t)
    ring.finish()


def gather(n_dp, n_seq, number, own):
    return pl.pallas_call(
        functools.partial(gather_kernel, n_dp, n_seq),
        name="ring_gather",
        out_shape=shape_of((n_seq,) + own.shape, own.dtype),
        in_specs=[ANY],
        out_specs=ANY,
        scratch_shapes=[pltpu.SemaphoreType.DMA((1,))] + RingGather.scratch(n_seq),
        compiler_params=comm_params(number),
    )(own)


def scatter_kernel(n_dp, n_seq, parts, out, slots, send, recv):
    at = Where(n_dp, n_seq)
    greet(at.ring_ids())
    ring = RingScatter(at, parts, slots, send, recv)
    for t in range(ring.steps):
        ring.step(t)
    ring.finish(out)


def scatter(n_dp, n_seq, number, parts):
    return pl.pallas_call(
        functools.partial(scatter_kernel, n_dp, n_seq),
        name="ring_scatter",
        out_shape=shape_of(parts.shape[1:], FULL),
        in_specs=[VMEM],
        out_specs=VMEM,
        scratch_shapes=RingScatter.scratch(n_seq, *parts.shape[1:]),
        compiler_params=comm_params(number),
    )(parts)


def reduce_kernel(
    n_dp, n_seq, cols, rows, got, total, total_v,
    c_core, c_other, c_s, c_r, r_core, r_other, r_s, r_r, fin, a_s, a_r, local,
):
    at = Where(n_dp, n_seq)
    greet(at.seq_ids() + [at.core_id()] + at.chip_ids())
    down = DpScatter(at, rows, r_core, r_other, r_s, r_r)
    side = DpScatter(at, cols, c_core, c_other, c_s, c_r)
    side.start()
    down.start()
    side.across()
    down.across()
    side.finish(fin)
    n, width = got.shape[1], got.shape[2]
    copies = []
    kept = pltpu.make_async_copy(
        fin.at[pl.ds(pl.multiple_of(at.seq * n, n), n)], got.at[at.seq], local.at[0]
    )
    kept.start()
    for k, one in enumerate(at.seq_ids()):
        src = fin.at[pl.ds(pl.multiple_of(one[1] * n, n), n)]
        copy = remote(src, got.at[at.seq], a_s.at[k], a_r.at[k], one)
        copy.start()
        copies.append(copy)
    down.finish(total_v)
    store = pltpu.make_async_copy(total_v, total, local.at[1])
    store.start()
    for copy in copies:
        copy.wait()
    kept.wait()
    store.wait()


def reduce(n_dp, n_seq, number, cols, rows, kind):
    _, deep, wide = cols.shape
    return pl.pallas_call(
        functools.partial(reduce_kernel, n_dp, n_seq),
        name="reduce_grads",
        out_shape=[
            shape_of((n_seq, deep // n_seq, wide), LOW),
            shape_of(rows.shape[1:], kind),
        ],
        in_specs=[VMEM, VMEM],
        out_specs=[ANY, ANY],
        scratch_shapes=[pltpu.VMEM(rows.shape[1:], kind)]
        + DpScatter.scratch(n_dp, deep, wide)
        + DpScatter.scratch(n_dp, *rows.shape[1:])
        + [pltpu.VMEM((deep, wide), LOW)]
        + SeqExchange.scratch(n_seq)
        + [pltpu.SemaphoreType.DMA((2,))],
        compiler_params=comm_params(number),
    )(cols, rows)


def allowed_at(start_ref, begin, count, stop):
    query = lax.broadcasted_iota(jnp.int32, (count, stop), 0) + begin
    key = lax.broadcasted_iota(jnp.int32, (count, stop), 1)
    return (key <= query) & (key >= start_ref[begin : begin + count])


def attend_kernel(block, start_ref, q_ref, k_ref, v_ref, o_ref, lse_ref):
    for begin in range(0, q_ref.shape[1], block):
        stop = begin + block
        allowed = allowed_at(start_ref, begin, block, stop)
        raw = matmul_nt(q_ref[0, begin:stop], k_ref[0, :stop])
        raw = jnp.where(allowed, raw, MASK_VALUE)
        top = jnp.max(raw, -1, keepdims=True)
        probs = jnp.where(allowed, jnp.exp(raw - top), 0.0)
        total = jnp.sum(probs, -1, keepdims=True)
        probs = (probs * (1.0 / total)).astype(LOW)
        o_ref[0, begin:stop] = matmul(probs, v_ref[0, :stop]).astype(LOW)
        lse_ref[0, begin:stop] = top + jnp.log(total)


def attend(starts, queries, keys, values):
    heads, length, dim = queries.shape
    block = min(256, length)
    per_kv = heads // keys.shape[0]
    one = pl.BlockSpec((1, length, dim), lambda h: (h, 0, 0))
    shared = pl.BlockSpec((1, length, dim), lambda h: (h // per_kv, 0, 0))
    stat = pl.BlockSpec((1, length, 1), lambda h: (h, 0, 0))
    return pl.pallas_call(
        functools.partial(attend_kernel, block),
        name="attend",
        grid=(heads,),
        out_shape=[
            shape_of((heads, length, dim), LOW),
            shape_of((heads, length, 1), FULL),
        ],
        in_specs=[pl.BlockSpec((length, 1), lambda h: (0, 0)), one, shared, shared],
        out_specs=[one, stat],
        compiler_params=pltpu.CompilerParams(vmem_limit_bytes=VMEM_BYTES),
    )(starts, queries, keys, values)


def attend_back_kernel(
    block, per_kv, start_ref, q_ref, k_ref, v_ref, do_ref, lse_ref, dq_ref, dk_ref, dv_ref
):
    @pl.when(lax.rem(pl.program_id(0), per_kv) == 0)
    def _():
        dk_ref[...] = jnp.zeros_like(dk_ref)
        dv_ref[...] = jnp.zeros_like(dv_ref)

    for begin in range(0, q_ref.shape[1], block):
        stop = begin + block
        allowed = allowed_at(start_ref, begin, block, stop)
        q = q_ref[0, begin:stop]
        do = do_ref[0, begin:stop]
        k = k_ref[0, :stop]
        raw = matmul_nt(q, k)
        probs = jnp.where(allowed, jnp.exp(raw - lse_ref[0, begin:stop]), 0.0)
        grad_probs = matmul_nt(do, v_ref[0, :stop])
        delta = jnp.sum(probs * grad_probs, -1, keepdims=True)
        grad_raw = (probs * (grad_probs - delta)).astype(LOW)
        dq_ref[0, begin:stop] = matmul(grad_raw, k)
        dk_ref[0, :stop] += matmul_tn(grad_raw, q)
        dv_ref[0, :stop] += matmul_tn(probs.astype(LOW), do)


def attend_back(starts, queries, keys, values, grads, lse):
    heads, length, dim = queries.shape
    block = min(256, length)
    per_kv = heads // keys.shape[0]
    one = pl.BlockSpec((1, length, dim), lambda h: (h, 0, 0))
    shared = pl.BlockSpec((1, length, dim), lambda h: (h // per_kv, 0, 0))
    stat = pl.BlockSpec((1, length, 1), lambda h: (h, 0, 0))
    return pl.pallas_call(
        functools.partial(attend_back_kernel, block, per_kv),
        name="attend_back",
        grid=(heads,),
        out_shape=[
            shape_of((heads, length, dim), FULL),
            shape_of(keys.shape, FULL),
            shape_of(keys.shape, FULL),
        ],
        in_specs=[pl.BlockSpec((length, 1), lambda h: (0, 0)), one, shared, shared, one, stat],
        out_specs=[one, shared, shared],
        compiler_params=pltpu.CompilerParams(vmem_limit_bytes=VMEM_BYTES),
    )(starts, queries, keys, values, grads, lse)


def rotate(values, cosines, sines):
    half = values.shape[-1] // 2
    first = values[..., :half]
    second = values[..., half:]
    return jnp.concatenate([first * cosines - second * sines, second * cosines + first * sines], -1)


def norm_back(grad_normed, normed, scale):
    return scale * (grad_normed - normed * jnp.mean(grad_normed * normed, -1, keepdims=True))


def body(
    n_dp,
    n_seq,
    tokens,
    segment_ids,
    gain_attn,
    w_query,
    w_key,
    w_value,
    w_output,
    gain_mlp,
    w_gate,
    w_up,
    w_down,
    cotangent,
):
    local, width = tokens.shape[1], tokens.shape[2]
    length = n_seq * local
    own_rows = w_query.shape[0]
    own_ff = w_down.shape[0]
    part_ff = n_dp * own_ff
    heads = HEADS // n_seq
    q_width = heads * HEAD_DIM
    kv_heads = max(heads // GROUP, 1)
    kv_width = kv_heads * HEAD_DIM
    factor = HEAD_DIM ** (-0.5)
    dtype = tokens.dtype
    x_own = tokens.reshape(local, width)
    dy_own = cotangent.reshape(local, width)

    gain_one = gain_attn.astype(FULL)[:, None]
    gain_two = gain_mlp.astype(FULL)[:, None]

    def gained(gain, weight):
        return (gain * weight.astype(FULL)).astype(LOW)

    def for_kv(weight):
        return jnp.stack(
            [
                weight[:, first * HEAD_DIM : first * HEAD_DIM + kv_width]
                for first in [s * heads // GROUP for s in range(n_seq)]
            ]
        )

    pack_q = jnp.concatenate(
        [
            gained(gain_one, w_query).reshape(own_rows, n_seq, q_width).transpose(1, 0, 2),
            for_kv(gained(gain_one, w_key)),
            for_kv(gained(gain_one, w_value)),
        ],
        -1,
    )

    def ff_split(weight):
        return (
            weight.reshape(own_rows, n_dp, n_seq, own_ff)
            .transpose(2, 0, 1, 3)
            .reshape(n_seq, own_rows, part_ff)
        )

    pack_gu = jnp.concatenate(
        [ff_split(gained(gain_two, w_gate)), ff_split(gained(gain_two, w_up))], -1
    )
    there = [(l, (l % n_dp) * n_seq + l // n_dp) for l in range(n_dp * n_seq)]
    back = [(b, a) for a, b in there]
    wo_block = lax.ppermute(w_output, ("dp", "seq"), there)
    seg_block = jnp.broadcast_to(
        segment_ids.reshape(1, 1, local), (n_seq, 8, local)
    )
    down_block = w_down if own_ff % 16 == 0 else w_down.reshape(16, own_ff * width // 16)

    x_all, dy_all, seg_all, q_all, gu_all, wd_all, wo_all = spread(
        n_dp, n_seq, x_own, dy_own, seg_block, pack_q, pack_gu, down_block, wo_block
    )
    inputs = x_all.reshape(length, width).astype(FULL)
    dy = dy_all.reshape(length, width)
    weight_q = q_all.reshape(width, q_width + 2 * kv_width)
    weight_gu = gu_all.reshape(width, 2 * part_ff)
    weight_d = wd_all.reshape(part_ff, width)
    weight_o = wo_all.reshape(q_width, width)
    segs = seg_all[:, 0, :].reshape(length)

    starts = jnp.sum((segs[None, :] < segs[:, None]).astype(jnp.int32), 1)
    places = (jnp.arange(length, dtype=jnp.int32) - starts).astype(FULL)
    freqs = ROPE_BASE ** (-jnp.arange(0, HEAD_DIM, 2).astype(FULL) / HEAD_DIM)
    turned = places[:, None] * freqs[None, :]
    cosines, sines = jnp.cos(turned)[:, None, :], jnp.sin(turned)[:, None, :]
    starts = starts[:, None]

    scale_one = lax.rsqrt(jnp.mean(inputs * inputs, -1, keepdims=True) + EPS)
    norm_one = (inputs * scale_one).astype(LOW)
    qkv = matmul(norm_one, weight_q)

    def to_heads(values):
        return values.astype(LOW).transpose(1, 0, 2)

    queries = to_heads(
        rotate(qkv[:, :q_width].reshape(length, heads, HEAD_DIM), cosines, sines) * factor
    )
    keys = to_heads(
        rotate(
            qkv[:, q_width : q_width + kv_width].reshape(length, kv_heads, HEAD_DIM),
            cosines,
            sines,
        )
    )
    values = to_heads(qkv[:, q_width + kv_width :].reshape(length, kv_heads, HEAD_DIM))
    attended, lse = attend(starts, queries, keys, values)
    attended = attended.transpose(1, 0, 2).reshape(length, q_width)
    part = matmul(attended, weight_o).astype(LOW).reshape(n_seq, local, width)
    middle = x_own.astype(FULL) + scatter(n_dp, n_seq, 2, part)

    scale_two = lax.rsqrt(jnp.mean(middle * middle, -1, keepdims=True) + EPS)
    norm_two = middle * scale_two
    second = gather(n_dp, n_seq, 3, norm_two.astype(LOW)).reshape(length, width)
    both = matmul(second, weight_gu)
    gate, upward = both[:, :part_ff], both[:, part_ff:]
    sigma = jax.nn.sigmoid(gate)
    hidden = (gate * sigma * upward).astype(LOW)
    part = matmul(hidden, weight_d).astype(LOW).reshape(n_seq, local, width)
    result = (middle + scatter(n_dp, n_seq, 4, part)).astype(dtype)

    grad_hidden = matmul_nt(dy, weight_d)
    grad_gate = (grad_hidden * upward * sigma * (1.0 + gate * (1.0 - sigma))).astype(LOW)
    grad_up = (grad_hidden * gate * sigma).astype(LOW)
    grad_both = jnp.concatenate([grad_gate, grad_up], 1)
    part = matmul_nt(grad_both, weight_gu).astype(LOW).reshape(n_seq, local, width)
    grad_second = scatter(n_dp, n_seq, 5, part)
    grad_middle = dy_own.astype(FULL) + norm_back(grad_second, norm_two, scale_two)
    grad_gu = matmul_tn(second, grad_both).astype(LOW)
    grad_d = matmul_tn(hidden, dy).astype(LOW)

    middle_low = gather(n_dp, n_seq, 6, grad_middle.astype(LOW)).reshape(length, width)
    grad_o = matmul_tn(attended, middle_low).astype(LOW)
    grad_attended = (
        matmul_nt(middle_low, weight_o).astype(LOW).reshape(length, heads, HEAD_DIM)
    ).transpose(1, 0, 2)
    dq, dk, dv = attend_back(starts, queries, keys, values, grad_attended, lse)

    def from_heads(grads):
        return grads.transpose(1, 0, 2)

    def flat(grads):
        return grads.reshape(length, grads.shape[1] * HEAD_DIM).astype(LOW)

    grad_qkv = jnp.concatenate(
        [
            flat(rotate(from_heads(dq) * factor, cosines, -sines)),
            flat(rotate(from_heads(dk), cosines, -sines)),
            flat(from_heads(dv)),
        ],
        1,
    )
    part = matmul_nt(grad_qkv, weight_q).astype(LOW).reshape(n_seq, local, width)
    grad_normed = scatter(n_dp, n_seq, 7, part)
    own_inputs = x_own.astype(FULL)
    own_scale = lax.rsqrt(jnp.mean(own_inputs * own_inputs, -1, keepdims=True) + EPS)
    grad_inputs = grad_middle + norm_back(grad_normed, own_inputs * own_scale, own_scale)
    grad_q = matmul_tn(norm_one, grad_qkv).astype(LOW)

    got_gu, got_d = reduce(
        n_dp,
        n_seq,
        8,
        grad_gu.reshape(n_dp, n_seq * own_rows, 2 * part_ff),
        grad_d.reshape((n_dp,) + down_block.shape),
        FULL,
    )
    got_q, got_o = reduce(
        n_dp,
        n_seq,
        9,
        grad_q.reshape(n_dp, n_seq * own_rows, q_width + 2 * kv_width),
        grad_o.reshape((n_dp,) + w_output.shape),
        LOW,
    )
    grad_output_w = lax.ppermute(got_o, ("dp", "seq"), back).astype(FULL)
    grad_down_w = got_d.reshape(own_ff, width)

    def ff_join(grads):
        return (
            grads.astype(FULL)
            .reshape(n_seq, own_rows, n_dp, own_ff)
            .transpose(1, 2, 0, 3)
            .reshape(own_rows, n_dp * n_seq * own_ff)
        )

    raw_gate = ff_join(got_gu[:, :, :part_ff])
    raw_up = ff_join(got_gu[:, :, part_ff:])
    raw_query = (
        got_q[:, :, :q_width].astype(FULL).transpose(1, 0, 2).reshape(own_rows, width)
    )

    def kv_join(grads):
        firsts = [s * heads // GROUP for s in range(n_seq)]
        columns = []
        for head in range(KV_HEADS):
            terms = [
                grads[s, :, (head - first) * HEAD_DIM : (head - first + 1) * HEAD_DIM].astype(FULL)
                for s, first in enumerate(firsts)
                if first <= head < first + kv_heads
            ]
            columns.append(functools.reduce(jnp.add, terms))
        return jnp.concatenate(columns, 1)

    raw_key = kv_join(got_q[:, :, q_width : q_width + kv_width])
    raw_value = kv_join(got_q[:, :, q_width + kv_width :])

    def gain_grad(*pairs):
        return sum(jnp.sum(weight.astype(FULL) * raw, 1) for weight, raw in pairs)

    grad_attn_gain = gain_grad((w_query, raw_query), (w_key, raw_key), (w_value, raw_value))
    grad_mlp_gain = gain_grad((w_gate, raw_gate), (w_up, raw_up))
    return (
        result.reshape(tokens.shape),
        grad_inputs.reshape(tokens.shape),
        grad_attn_gain,
        gain_one * raw_query,
        gain_one * raw_key,
        gain_one * raw_value,
        grad_output_w,
        grad_mlp_gain,
        gain_two * raw_gate,
        gain_two * raw_up,
        grad_down_w,
    )


def solution(mesh):
    rows = P(("dp", "seq"), None)
    vector = P(("dp", "seq"))
    row = P("dp", "seq", None)
    return jax.shard_map(
        functools.partial(body, mesh.shape["dp"], mesh.shape["seq"]),
        mesh=mesh,
        in_specs=(row, P("dp", "seq"), vector, rows, rows, rows, rows, vector, rows, rows, rows, row),
        out_specs=(row, row, vector, rows, rows, rows, rows, vector, rows, rows, rows),
        check_vma=False,
    )
```

time: 4830 us -> 742 us (0.15)
  waiting for transfers between devices: 4460 us -> 0.01 us
  Pallas kernels: 0 us -> 550 us
  matrix products: 203 us -> 68.5 us
  blocking collectives: 99.7 us -> 0 us
    reduce_scatter x7 -> x0, waiting for transfers between devices: 3760 us -> none  [scatter_grads(): lax.psum_scatter(terms, ('dp', 'seq'), scatter_dimension=0, tiled=True)]
    all_gather x8 -> x0, waiting for transfers between devices: 618 us -> none  [the longest x7 582 us: gather_weights(): lax.all_gather(for_sending(pieces), ('dp', 'seq'), axis=0, tiled=True)]
    pallas_call x0 -> x11, Pallas kernels: none -> 550 us  [the longest x4 206 us: scatter(): pl.pallas_call(functools.partial(scatter_kernel, n_dp, n_seq), name='ring...]
    dot_general x30 -> x12, matrix products: 203 us -> 68.5 us  [the longest x4 24.8 us: matmul_nt(): lax.dot_general(left, right, (((1,), (1,)), ((), ())), preferred_element_...]
    unnamed x17 -> x0, waiting for transfers between devices: 79.3 us -> none
    unnamed x2 -> x0, blocking collectives: 77.4 us -> none
  transfers between devices with their start and end apart: 16 -> 2, of which waited for: 14 -> 0; matrix products, arithmetic and copies ran while one was open for 3% -> 4% of each run, Pallas kernels for 0% -> 9%
where the time goes in v1:
time: 742 us; the launch traced here: 738 us
  Pallas kernels  550 us (74%)
  matrix products  68.5 us (9%)
  other arithmetic  60 us (8%)
  local copies, waits for them, and re-layouts  53.8 us (7%)
    pallas_call x4, Pallas kernels, scatter(): pl.pallas_call(functools.partial(scatter_kernel, n_dp, n_seq), name='ring...  206 us
    pallas_call x1, Pallas kernels, spread(): pl.pallas_call(functools.partial(spread_kernel, n_dp, n_seq), name='sprea...  142 us
    pallas_call x2, Pallas kernels, reduce(): pl.pallas_call(functools.partial(reduce_kernel, n_dp, n_seq), name='reduc...  91.9 us
    pallas_call x2, Pallas kernels, gather(): pl.pallas_call(functools.partial(gather_kernel, n_dp, n_seq), name='ring_...  83.7 us
    dot_general x4, matrix products, matmul_nt(): lax.dot_general(left, right, (((1,), (1,)), ((), ())), preferred_element_...  24.8 us
    reshape x6, local copies, waits for them, and re-layouts, ff_join(): return grads.astype(FULL).reshape(n_seq, own_rows, n_dp, own_ff).transpos...  22.9 us
    dot_general x4, matrix products, matmul(): return jnp.dot(left, right, preferred_element_type=FULL)  22.1 us
    dot_general x4, matrix products, matmul_tn(): lax.dot_general(left, right, (((0,), (0,)), ((), ())), preferred_element_...  21.5 us
  transfers between devices with their start and end apart: 2, of which 0 were waited for; matrix products, arithmetic and copies ran while one was open for 4% of the time, Pallas kernels for 9%

profile of v1, /device:TPU:0, one launch (start us, length us, event | category | flops | bytes accessed | tf_op | source)
XLA Modules:
  0.0 737.6 jit_solution(15144907060908851851)
XLA Ops:
  16.2 3.2 reshape.419
  25.5 141.7 %spread_inputs.1 = (bf16[8,128,2048]{2,1,0:T(8,128)(2,1)}, bf16[8,128,2048]{2,1,0:T(8,128)(2,1)}, s32[8,8,128]{2,1,0:T(8,128)}, bf16[4,8,64,384]{3,2,1,0:T(8,128...) custom-call(bf16[128,2048]{1,0:T(8,128)(2,1)} %bitcast.187, ...), custom_call_target="tpu_custom_call" | custom-call | tf_op jit(solution)/shard_map/spread_inputs/pallas_call | solution.py:425
  167.2 3.2 multiply_reduce_fusion
  181.5 3.2 fusion.36
  194.8 12.1 %attend.1 = (bf16[4,1024,64]{2,1,0:T(8,128)(2,1)}, f32[4,1024,1]{2,1,0:T(8,128)}) custom-call(s32[1024,1]{1,0:T(8,128)} %copy.80.start_ref, bf16[4,1024,64]{2,1,0:T(8,128)(2,1)} %fusion.14.q_ref, bf16[1,1024,64]{2,1,0:T(8,128)(2,1)} %pad_maximum_fusion.9.k_ref, bf16[1,1024,64]{2,1,0:T(8,128)(2,1)} %bitcast.207), custom_call_target="tpu_custom_call" | custom-call | tf_op jit(solution)/shard_map/attend/pallas_call | solution.py:567
  206.9 4.5 bitcast_convert_fusion
  211.4 45.5 %ring_scatter.4 = f32[128,2048]{1,0:T(8,128)} custom-call(bf16[8,128,2048]{2,1,0:T(8,128)(2,1)} %bitcast.196), custom_call_target="tpu_custom_call" | custom-call | tf_op jit(solution)/shard_map/ring_scatter/pallas_call | solution.py:475
  260.5 43.8 %ring_gather.2 = bf16[8,128,2048]{2,1,0:T(8,128)(2,1)} custom-call(bf16[128,2048]{1,0:T(8,128)(2,1)} %multiply_convert_fusion.4.own), custom_call_target="tpu_custom_call" | custom-call | tf_op jit(solution)/shard_map/ring_gather/pallas_call | solution.py:454
  304.3 10.6 %fusion.51 = f32[1024,1408]{1,0:T(8,128)S(1)} fusion(bf16[1024,2048]{1,0:T(8,128)(2,1)} %bitcast.198, bf16[2048,1408]{1,0:T(8,128)(2,1)} %bitcast.223), kind=kOutput, calls=%fused_computation.158 | convolution fusion | flops 5905580032 | bytes 15728640 | tf_op jit(solution)/shard_map/dot_general | solution.py:25
  315.0 6.0 multiply_convert_fusion.2
  321.0 9.9 %convolution_convert_fusion.2 = bf16[1024,2048]{1,0:T(8,128)(2,1)} fusion(bf16[2048,1408]{1,0:T(8,128)(2,1)S(1)} %bitcast.226, bf16[1024,704]{1,0:T(8,128)(2,1)} %get-tuple-element.46, bf16[1024,704]{1,0:T(8,128)(2,1)S(1)} %get-tuple-element.45), kind=kOutput, calls=%fused_computation.8 | convolution fusion | flops 5913444352 | bytes 12845056 | tf_op jit(solution)/shard_map/dot_general | solution.py:29
  330.9 8.8 %convolution_convert_fusion = bf16[2048,1408]{1,0:T(8,128)(2,1)} fusion(bf16[1024,2048]{1,0:T(8,128)(2,1)S(1)} %bitcast.199, bf16[1024,704]{1,0:T(8,128)(2,1)S(1)} %copy-done.38, bf16[1024,704]{1,0:T(8,128)(2,1)S(1)} %get-tuple-element.45), kind=kOutput, calls=%fused_computation.5 | convolution fusion | flops 5914230784 | bytes 12845056 | tf_op jit(solution)/shard_map/dot_general | solution.py:33
  339.7 4.6 convolution_convert_fusion.4
  344.3 5.2 convolution_convert_fusion.3
  353.4 42.4 %ring_scatter.6 = f32[128,2048]{1,0:T(8,128)} custom-call(bf16[8,128,2048]{2,1,0:T(8,128)(2,1)} %bitcast.195), custom_call_target="tpu_custom_call" | custom-call | tf_op jit(solution)/shard_map/ring_scatter/pallas_call | solution.py:475
  399.2 39.9 %ring_gather.3 = bf16[8,128,2048]{2,1,0:T(8,128)(2,1)} custom-call(bf16[128,2048]{1,0:T(8,128)(2,1)} %fusion.48.own), custom_call_target="tpu_custom_call" | custom-call | tf_op jit(solution)/shard_map/ring_gather/pallas_call | solution.py:454
  439.1 4.4 convolution_convert_fusion.7
  448.2 14.9 %attend_back.1 = (f32[4,1024,64]{2,1,0:T(8,128)}, f32[1,1024,64]{2,1,0:T(8,128)}, f32[1,1024,64]{2,1,0:T(8,128)}) custom-call(s32[1024,1]{1,0:T(8,128)} %copy.80.start_ref, bf16[4,1024,64]{2,1,0:T(8,128)(2,1)} %fusion.14.q_ref, bf16[1,1024,64]{2,1,0:T(8,128)(2,1)} %pad_maximum_fusion.9.k_ref, bf16[1,1024,64]{2,1,0:T(8,128)(2,1)} %bitcast.208, ...), custom_call_target="tpu_custom_call" | custom-call | tf_op jit(solution)/shard_map/attend_back/pallas_call | solution.py:612
  473.6 5.9 convolution_convert_fusion.5
  479.5 25.1 %reduce_grads.2 = (bf16[8,64,384]{2,1,0:T(8,128)(2,1)}, bf16[64,2048]{1,0:T(8,128)(2,1)}) custom-call(bf16[4,512,384]{2,1,0:T(8,128)(2,1)} %bitcast.211, bf16[4,64,2048]{2,1,0:T(8,128)(2,1)} %bitcast.215), custom_call_target="tpu_custom_call" | custom-call | tf_op jit(solution)/shard_map/reduce_grads/pallas_call | solution.py:521
  507.3 4.5 convolution_convert_fusion.1
  512.3 50.6 %ring_scatter.5 = f32[128,2048]{1,0:T(8,128)} custom-call(bf16[8,128,2048]{2,1,0:T(8,128)(2,1)} %bitcast.193), custom_call_target="tpu_custom_call" | custom-call | tf_op jit(solution)/shard_map/ring_scatter/pallas_call | solution.py:475
  562.9 66.8 %reduce_grads.3 = (bf16[8,64,1408]{2,1,0:T(8,128)(2,1)}, f32[176,2048]{1,0:T(8,128)}) custom-call(bf16[4,512,1408]{2,1,0:T(8,128)(2,1)} %bitcast.190, bf16[4,176,2048]{2,1,0:T(8,128)(2,1)} %bitcast.206), custom_call_target="tpu_custom_call" | custom-call | tf_op jit(solution)/shard_map/reduce_grads/pallas_call | solution.py:521
  629.7 3.5 slice_convert_fusion
  633.2 3.9 reshape.463
  637.1 4.1 copy.92
  641.3 3.3 reshape.456
  644.5 4.2 reshape.461
  648.7 4.1 copy.91
  652.8 3.3 reshape.454
  659.0 67.6 %ring_scatter.7 = f32[128,2048]{1,0:T(8,128)} custom-call(bf16[8,128,2048]{2,1,0:T(8,128)(2,1)} %bitcast.194), custom_call_target="tpu_custom_call" | custom-call | tf_op jit(solution)/shard_map/ring_scatter/pallas_call | solution.py:475
  728.2 3.4 broadcast_multiply_fusion
  (168 shorter events, 81.9 us)
Async XLA Ops:
  0.6 24.2 %collective-permute-start = (bf16[64,2048]{1,0:T(8,128)(2,1)}, bf16[64,2048]{1,0:T(8,128)(2,1)S(1)}, u32[]{:S(2)}, u32[]{:S(2)}) collective-permute-start(bf16[64,2048]{1,0:T(8,128)(2,1)} %param.18), channel_id=1, source_target_pairs={{0,0},{1,8},{2,16},{3,24},{4,1},{5,9},{6,17},{7,25},{8,2},{9,10},{... | collective-permute-start | bytes 786440 | tf_op jit(solution)/shard_map/ppermute | solution.py:703
  4.7 3.8 copy-start.22
  19.8 5.0 copy-start.30
  167.2 3.5 copy-start.1
  193.2 13.7 %copy-start.36 = (bf16[4,64,2048]{2,1,0:T(8,128)(2,1)S(1)}, bf16[4,64,2048]{2,1,0:T(8,128)(2,1)}, u32[]{:S(2)}) copy-start(bf16[4,64,2048]{2,1,0:T(8,128)(2,1)} %get-tuple-element.31) | copy-start | bytes 3145732
  211.4 45.5 %copy-start.3 = (bf16[1,128,2048]{2,1,0:T(8,128)(2,1)S(1)}, bf16[1,128,2048]{2,1,0:T(8,128)(2,1)}, u32[]{:S(2)}) copy-start(bf16[1,128,2048]{2,1,0:T(8,128)(2,1)} %param.12) | copy-start | bytes 1572868
  304.3 10.6 %copy-start.32 = (bf16[8,128,2048]{2,1,0:T(8,128)(2,1)S(1)}, bf16[8,128,2048]{2,1,0:T(8,128)(2,1)}, u32[]{:S(2)}) copy-start(bf16[8,128,2048]{2,1,0:T(8,128)(2,1)} %get-tuple-element.34) | copy-start | bytes 12582916
  304.3 10.6 %copy-start.33 = (bf16[4,176,2048]{2,1,0:T(8,128)(2,1)S(1)}, bf16[4,176,2048]{2,1,0:T(8,128)(2,1)}, u32[]{:S(2)}) copy-start(bf16[4,176,2048]{2,1,0:T(8,128)(2,1)} %get-tuple-element.33) | copy-start | bytes 8650756
  304.3 16.6 %slice-start = ((s8[5767168]{0:T(1024)(128)(4,1)}), s8[4194304]{0:T(1024)(128)(4,1)S(1)}, s32[]{:S(2)}) async-start(s8[5767168]{0:T(1024)(128)(4,1)} %bitcast.224), calls=%async_computation | async-start | bytes 8388608
  314.9 6.0 slice-start.1
  320.9 9.9 %copy-start.11 = (bf16[8,128,2048]{2,1,0:T(8,128)(2,1)S(1)}, bf16[8,128,2048]{2,1,0:T(8,128)(2,1)}, u32[]{:S(2)}) copy-start(bf16[8,128,2048]{2,1,0:T(8,128)(2,1)} %ring_gather.2) | copy-start | bytes 12582916
  320.9 9.9 %copy-start.38 = (bf16[1024,704]{1,0:T(8,128)(2,1)S(1)}, bf16[1024,704]{1,0:T(8,128)(2,1)}, u32[]{:S(2)}) copy-start(bf16[1024,704]{1,0:T(8,128)(2,1)} %get-tuple-element.46) | copy-start | bytes 4325380
  344.3 5.2 copy-start.2
  353.4 42.4 %copy-start = (f32[128,2048]{1,0:T(8,128)S(1)}, f32[128,2048]{1,0:T(8,128)}, u32[]{:S(2)}) copy-start(f32[128,2048]{1,0:T(8,128)} %ring_scatter.4) | copy-start | bytes 3145732
  353.4 44.6 %copy-start.8 = (bf16[1,128,2048]{2,1,0:T(8,128)(2,1)S(1)}, bf16[1,128,2048]{2,1,0:T(8,128)(2,1)}, u32[]{:S(2)}) copy-start(bf16[1,128,2048]{2,1,0:T(8,128)(2,1)} %param.23) | copy-start | bytes 1572868
  399.2 39.9 %copy-start.37 = (bf16[4,64,2048]{2,1,0:T(8,128)(2,1)S(1)}, bf16[4,64,2048]{2,1,0:T(8,128)(2,1)}, u32[]{:S(2)}) copy-start(bf16[4,64,2048]{2,1,0:T(8,128)(2,1)} %get-tuple-element.31) | copy-start | bytes 3145732
  439.1 4.4 copy-start.12
  439.1 4.4 copy-start.20
  465.6 3.9 copy-start.15
  479.5 27.8 %copy-start.19 = (bf16[1024,4,64]{0,2,1:T(8,128)(2,1)S(1)}, bf16[1024,4,64]{0,2,1:T(8,128)(2,1)}, u32[]{:S(2)}) copy-start(bf16[1024,4,64]{0,2,1:T(8,128)(2,1)} %copy.86) | copy-start | bytes 1572868
  479.5 27.8 %copy-start.35 = (bf16[4,8,64,384]{3,2,1,0:T(8,128)(2,1)S(1)}, bf16[4,8,64,384]{3,2,1,0:T(8,128)(2,1)}, u32[]{:S(2)}) copy-start(bf16[4,8,64,384]{3,2,1,0:T(8,128)(2,1)} %get-tuple-element.29) | copy-start | bytes 4718596
  507.3 4.5 copy-start.31
  652.8 3.4 copy-start.18
  657.2 69.4 %copy-start.29 = (f32[128]{0:T(128)S(1)}, f32[128]{0:T(128)}, u32[]{:S(2)}) copy-start(f32[128]{0:T(128)} %add_rsqrt_fusion.1) | copy-start | bytes 1540
  657.2 78.2 %collective-permute-start.1 = (bf16[64,2048]{1,0:T(8,128)(2,1)}, bf16[64,2048]{1,0:T(8,128)(2,1)S(1)}, u32[]{:S(2)}, u32[]{:S(2)}) collective-permute-start(bf16[64,2048]{1,0:T(8,128)(2,1)} %get-tuple-element.40), channel_id=1, source_target_pairs={{0,0},{8,1},{16,2},{24,3},{1,4},{9,5},{17,6},{25,7},{2,8},{10,9},{... | collective-permute-start | bytes 786440 | tf_op jit(solution)/shard_map/ppermute | solution.py:814
  659.0 69.2 %copy-start.6 = (f32[64,5632]{1,0:T(8,128)S(1)}, f32[64,5632]{1,0:T(8,128)}, u32[]{:S(2)}) copy-start(f32[64,5632]{1,0:T(8,128)} %reshape.456) | copy-start | bytes 4325380
  659.0 69.2 %copy-start.7 = (f32[64,5632]{1,0:T(8,128)S(1)}, f32[64,5632]{1,0:T(8,128)}, u32[]{:S(2)}) copy-start(f32[64,5632]{1,0:T(8,128)} %reshape.454) | copy-start | bytes 4325380
  659.0 69.2 %copy-start.13 = (bf16[64,5632]{1,0:T(8,128)(2,1)S(1)}, bf16[64,5632]{1,0:T(8,128)(2,1)}, u32[]{:S(2)}) copy-start(bf16[64,5632]{1,0:T(8,128)(2,1)} %param.20) | copy-start | bytes 2162692
  728.2 3.4 copy-start.5
  728.2 3.4 copy-start.9
  728.2 3.4 copy-start.10
  731.7 4.6 copy-start.16
  (11 other events, 20.0 us)

commit v2 on v1

v2 whole, which is shorter than its diff:
```python
import functools

import jax
import jax.numpy as jnp
from jax import lax
from jax.experimental import pallas as pl
from jax.experimental.pallas import tpu as pltpu
from jax.sharding import PartitionSpec as P

HEADS = 32
HEAD_DIM = 64
KV_HEADS = 4
GROUP = HEADS // KV_HEADS

EPS = 1e-05
ROPE_BASE = 10000.0
MASK_VALUE = -1e30
MESH = pl.DeviceIdType.MESH
LOW = jnp.bfloat16
FULL = jnp.float32
VMEM_BYTES = 60 * 1024 * 1024


def matmul(left, right):
    return jnp.dot(left, right, preferred_element_type=FULL)


def matmul_nt(left, right):
    return lax.dot_general(left, right, (((1,), (1,)), ((), ())), preferred_element_type=FULL)


def matmul_tn(left, right):
    return lax.dot_general(left, right, (((0,), (0,)), ((), ())), preferred_element_type=FULL)


def ring_at(place, n):
    upper = lax.div(place, n // 2)
    return (1 - upper) * 2 * place + upper * (2 * (n - place) - 1)


def ring_place(index, n):
    odd = lax.rem(index, 2)
    return (1 - odd) * lax.div(index, 2) + odd * (n - lax.div(index + 1, 2))


class Where:
    def __init__(self, n_dp, n_seq):
        self.n_dp, self.n_seq = n_dp, n_seq
        self.chips = n_dp // 2
        self.dp = lax.axis_index("dp")
        self.seq = lax.axis_index("seq")
        self.core = lax.rem(self.dp, 2)
        self.chip = lax.div(self.dp, 2)
        self.place = ring_place(self.seq, n_seq)

    def ring(self, step):
        return ring_at(lax.rem(self.place + step + self.n_seq, self.n_seq), self.n_seq)

    def ring_ids(self):
        return [(self.dp, self.ring(1)), (self.dp, self.ring(-1))]

    def seq_ids(self):
        return [
            (self.dp, lax.rem(self.seq + k, self.n_seq)) for k in range(1, self.n_seq)
        ]

    def dp_ids(self):
        return [(lax.rem(self.dp + k, self.n_dp), self.seq) for k in range(1, self.n_dp)]

    def core_id(self):
        return (self.dp + 1 - 2 * self.core, self.seq)

    def chip_ids(self):
        return [
            (2 * lax.rem(self.chip + k, self.chips) + self.core, self.seq)
            for k in range(1, self.chips)
        ]


def greet(ids):
    barrier = pltpu.get_barrier_semaphore()
    for one in ids:
        pl.semaphore_signal(barrier, inc=1, device_id=one, device_id_type=MESH)
    pl.semaphore_wait(barrier, len(ids))


def remote(src, dst, send, recv, target):
    return pltpu.make_async_remote_copy(
        src_ref=src,
        dst_ref=dst,
        send_sem=send,
        recv_sem=recv,
        device_id=target,
        device_id_type=MESH,
    )


class Ring:
    def __init__(self, at, shape, send, recv):
        self.at, self.send, self.recv = at, send, recv
        self.steps = at.n_seq // 2
        self.halves = 2 if len(shape) > 2 or shape[0] % 32 == 0 else 1
        self.half = shape[0] // self.halves
        self.copies = {}

    @staticmethod
    def semaphores(n_seq):
        shape = (2, n_seq // 2, 2)
        return [pltpu.SemaphoreType.DMA(shape), pltpu.SemaphoreType.DMA(shape)]

    def opposite(self, h, d):
        return d == h if self.halves == 2 else d == 0

    def rows(self, h):
        return pl.ds(h * self.half, self.half)

    def go(self, src, dst, d, t, h):
        target = self.at.ring_ids()[d]
        copy = remote(src, dst, self.send.at[d, t, h], self.recv.at[d, t, h], target)
        copy.start()
        self.copies[(d, t, h)] = copy

    def pieces(self):
        return [(h, d) for h in range(self.halves) for d in (0, 1)]


class RingGather(Ring):
    def __init__(self, at, own, everything, send, recv, local):
        super().__init__(at, own.shape, send, recv)
        self.own, self.everything = own, everything
        self.kept = pltpu.make_async_copy(own, everything.at[at.seq], local)
        self.waited = set()

    @staticmethod
    def scratch(n_seq):
        return Ring.semaphores(n_seq)

    def wait(self, key):
        self.copies[key].wait_recv()
        self.waited.add(key)

    def step(self, t):
        if t == 0:
            self.kept.start()
        for h, d in self.pieces():
            if t == self.steps - 1 and not self.opposite(h, d):
                continue
            if t > 0:
                self.wait((d, t - 1, h))
            origin = self.at.ring(-t if d == 0 else t)
            dst = self.everything.at[origin, self.rows(h)]
            self.go(self.own.at[self.rows(h)] if t == 0 else dst, dst, d, t, h)

    def finish(self):
        for key in self.copies:
            if key not in self.waited:
                self.wait(key)
        for copy in self.copies.values():
            copy.wait_send()
        self.kept.wait()


class RingScatter(Ring):
    def __init__(self, at, parts, slots, send, recv, staged=None, loads=None):
        super().__init__(at, parts.shape[1:], send, recv)
        self.parts, self.slots, self.staged, self.loads = parts, slots, staged, loads

    @staticmethod
    def scratch(n_seq, *block):
        return [pltpu.VMEM((2, n_seq // 2) + block, LOW)] + Ring.semaphores(n_seq)

    @staticmethod
    def staging(*block):
        return [pltpu.VMEM((2,) + block, LOW), pltpu.SemaphoreType.DMA((2, 2))]

    def there(self, t, d):
        return self.at.ring(self.steps - t if d == 0 else t - self.steps)

    def adds(self, t, h, d):
        return t > 1 or (t == 1 and self.opposite(h, d))

    def load(self, t, h, d):
        rows = self.rows(h)
        block = self.parts.at[self.there(t, d), rows]
        return pltpu.make_async_copy(block, self.staged.at[d, rows], self.loads.at[d, h])

    def load_all(self, t):
        if self.staged is not None:
            for h, d in self.pieces():
                if t < self.steps and self.adds(t, h, d):
                    self.load(t, h, d).start()
                elif t == self.steps and d == 0:
                    self.load(t, h, d).start()

    def step(self, t):
        if t == 0:
            self.load_all(1)
        for h, d in self.pieces():
            if t == 0 and not self.opposite(h, d):
                continue
            rows = self.rows(h)
            src = self.parts.at[self.there(t, d), rows]
            if self.adds(t, h, d):
                if self.staged is not None:
                    self.load(t, h, d).wait()
                    src = self.staged.at[d, rows]
                self.copies[(d, t - 1, h)].wait_recv()
                held = self.slots.at[d, t - 1, rows]
                held[...] = (held[...].astype(FULL) + src[...].astype(FULL)).astype(LOW)
                src = held
            self.go(src, self.slots.at[d, t, rows], d, t, h)
        if t > 0:
            self.load_all(t + 1)

    def finish(self, out):
        last = self.steps - 1
        if last == 0:
            self.load_all(1)
        for h in range(self.halves):
            rows = self.rows(h)
            if self.staged is None:
                total = self.parts[self.at.seq, rows].astype(FULL)
            else:
                self.load(self.steps, h, 0).wait()
                total = self.staged[0, rows].astype(FULL)
            for d in (0, 1):
                if last == 0 and not self.opposite(h, d):
                    continue
                self.copies[(d, last, h)].wait_recv()
                total = total + self.slots[d, last, rows].astype(FULL)
            out[rows] = total.astype(out.dtype)
        for copy in self.copies.values():
            copy.wait_send()


class Exchange:
    def __init__(self, me, ids, axis, packed, landing, send, recv, local):
        self.kept = pltpu.make_async_copy(packed.at[me], landing.at[me], local)
        self.copies = [
            remote(packed.at[one[axis]], landing.at[me], send.at[k], recv.at[k], one)
            for k, one in enumerate(ids)
        ]

    @staticmethod
    def scratch(n):
        return [pltpu.SemaphoreType.DMA((n - 1,)), pltpu.SemaphoreType.DMA((n - 1,))]

    def start(self):
        self.kept.start()
        for copy in self.copies:
            copy.start()

    def arrived(self):
        self.kept.wait()
        for copy in self.copies:
            copy.wait_recv()

    def finish(self):
        for copy in self.copies:
            copy.wait_send()


def seq_exchange(at, *refs):
    return Exchange(at.seq, at.seq_ids(), 1, *refs)


def dp_exchange(at, *refs):
    return Exchange(at.dp, at.dp_ids(), 0, *refs)


class DpGather:
    def __init__(self, at, own, everything, send, recv, local):
        self.kept = pltpu.make_async_copy(own, everything.at[at.dp], local)
        slot = everything.at[at.dp]
        self.out = [
            remote(own, slot, send.at[k], recv.at[k], one) for k, one in enumerate(at.chip_ids())
        ]
        base = at.chips - 1
        self.mate = remote(own, slot, send.at[base], recv.at[base], at.core_id())
        self.handed = []
        for k in range(1, at.chips):
            origin = 2 * lax.rem(at.chip + at.chips - k, at.chips) + at.core
            there = everything.at[origin]
            self.handed.append(
                remote(there, there, send.at[base + k], recv.at[base + k], at.core_id())
            )

    @staticmethod
    def scratch(n_dp):
        return [pltpu.SemaphoreType.DMA((n_dp - 1,)), pltpu.SemaphoreType.DMA((n_dp - 1,))]

    def start(self):
        for copy in self.out:
            copy.start()
        self.mate.start()
        self.kept.start()

    def hand(self):
        for copy, onward in zip(self.out, self.handed):
            copy.wait_recv()
            onward.start()

    def arrived(self):
        self.kept.wait()
        self.mate.wait_recv()
        for copy in self.handed:
            copy.wait_recv()

    def finish(self):
        for copy in self.out + [self.mate] + self.handed:
            copy.wait_send()


def add_rows(rows, chunk, one):
    def step(r, carry):
        one(pl.ds(pl.multiple_of(r * chunk, chunk), chunk))
        return carry

    lax.fori_loop(0, rows // chunk, step, 0)


def chunk_of(rows, columns):
    chunk = rows
    while chunk % 32 == 0 and chunk * columns > 65536:
        chunk //= 2
    return chunk


class DpScatter:
    def __init__(self, at, parts, core, other, send, recv):
        self.at, self.parts, self.core, self.other = at, parts, core, other
        self.send, self.recv = send, recv
        self.rows, self.columns = parts.shape[1], parts.shape[2]

    @staticmethod
    def scratch(n_dp, rows, columns):
        chips = n_dp // 2
        return [
            pltpu.VMEM((chips, rows, columns), LOW),
            pltpu.VMEM((max(chips - 1, 1), rows, columns), LOW),
            pltpu.SemaphoreType.DMA((2 * chips - 1,)),
            pltpu.SemaphoreType.DMA((2 * chips - 1,)),
        ]

    def to_core(self, k):
        at = self.at
        return remote(
            self.parts.at[2 * k + 1 - at.core],
            self.core.at[k],
            self.send.at[k],
            self.recv.at[k],
            at.core_id(),
        )

    def to_chip(self, k):
        at = self.at
        sem = at.chips + k - 1
        return remote(
            self.core.at[lax.rem(at.chip + k, at.chips)],
            self.other.at[k - 1],
            self.send.at[sem],
            self.recv.at[sem],
            at.chip_ids()[k - 1],
        )

    def start(self):
        for k in range(self.at.chips):
            self.to_core(k).start()

    def add_core(self, k):
        held = self.core.at[k]
        mine = self.parts.at[2 * k + self.at.core]

        def one(rows):
            held[rows] = (held[rows].astype(FULL) + mine[rows].astype(FULL)).astype(LOW)

        add_rows(self.rows, chunk_of(self.rows, self.columns), one)

    def across(self):
        at = self.at
        for k in range(1, at.chips):
            there = lax.rem(at.chip + k, at.chips)
            self.to_core(there).wait_recv()
            self.add_core(there)
            self.to_chip(k).start()

    def finish(self, out):
        at = self.at
        self.to_core(at.chip).wait_recv()
        for k in range(1, at.chips):
            self.to_chip(k).wait_recv()
        held = self.core.at[at.chip]
        mine = self.parts.at[2 * at.chip + at.core]

        def one(rows):
            total = held[rows].astype(FULL) + mine[rows].astype(FULL)
            for k in range(1, at.chips):
                total = total + self.other[k - 1, rows].astype(FULL)
            out[rows] = total.astype(out.dtype)

        add_rows(self.rows, chunk_of(self.rows, self.columns), one)
        for k in range(at.chips):
            self.to_core(k).wait_send()
        for k in range(1, at.chips):
            self.to_chip(k).wait_send()


def comm_params(number):
    return pltpu.CompilerParams(
        collective_id=number, has_side_effects=True, vmem_limit_bytes=VMEM_BYTES
    )


ANY = pl.BlockSpec(memory_space=pl.ANY)
VMEM = pl.BlockSpec(memory_space=pltpu.VMEM)


def shape_of(dims, kind):
    return jax.ShapeDtypeStruct(dims, kind)


class Refs:
    def __init__(self, names, refs):
        refs = list(refs)
        for name, count in names:
            taken, refs = refs[: max(count, 1)], refs[max(count, 1) :]
            setattr(self, name, taken if count else taken[0])


def run(kernel, name, number, ins, outs, scratch):
    names = [(key, 0) for key in ins] + [(key, 0) for key in outs]
    shapes = []
    for key, value in scratch.items():
        if isinstance(value, list):
            names.append((key, len(value)))
            shapes += value
        else:
            names.append((key, 0))
            shapes.append(value)
    found = pl.pallas_call(
        lambda *refs: kernel(Refs(names, refs)),
        name=name,
        out_shape=[shape for shape, _ in outs.values()],
        in_specs=[spec for _, spec in ins.values()],
        out_specs=[spec for _, spec in outs.values()],
        scratch_shapes=shapes,
        compiler_params=comm_params(number),
    )(*[array for array, _ in ins.values()])
    return dict(zip(outs, found))


def dma(*dims):
    return pltpu.SemaphoreType.DMA(dims)


def vm(kind, *dims):
    return pltpu.VMEM(dims, kind)


def lanes(rows):
    return lax.broadcasted_iota(jnp.int32, (rows, 2 * HEAD_DIM), 1)


def low_head(rows):
    return lanes(rows) < HEAD_DIM


def swapped(pair):
    half = HEAD_DIM // 2
    first = lax.rem(lanes(pair.shape[0]), HEAD_DIM) < half
    return jnp.where(
        first, pltpu.roll(pair, 2 * HEAD_DIM - half, 1), pltpu.roll(pair, half, 1)
    )


def split_heads(pair):
    wide = pair.astype(FULL)
    low = low_head(pair.shape[0])
    return jnp.concatenate(
        [jnp.where(low, wide, 0.0), jnp.where(low, 0.0, wide)], 0
    ).astype(LOW)


def join_heads(both):
    rows = both.shape[0] // 2
    return jnp.where(low_head(rows), both[:rows], both[rows:])


def spread_kv(kv):
    wide = kv.astype(FULL)
    turned = pltpu.roll(wide, HEAD_DIM, 1)
    low = low_head(kv.shape[0])
    return jnp.where(low, wide, turned).astype(LOW), jnp.where(low, turned, wide).astype(LOW)


def mask_of(position, start, length):
    key = lax.broadcasted_iota(jnp.int32, (start.shape[0], length), 1)
    return jnp.where((key <= position) & (key >= start), 0.0, MASK_VALUE)


def own_positions(at, tok):
    return at.seq * tok + lax.broadcasted_iota(jnp.int32, (tok, 1), 0)


def rows_of(r, count):
    return pl.ds(pl.multiple_of(r * count, count), count)


def interleave(ring, jobs):
    jobs = list(jobs)
    for t in range(1, ring.steps):
        if jobs:
            jobs.pop(0)()
        ring.step(t)
    for job in jobs:
        job()


def front_kernel(n_dp, n_seq, own_ff, m):
    at = Where(n_dp, n_seq)
    tok, width = m.x.shape
    q_width = m.q.shape[1]
    groups = q_width // (2 * HEAD_DIM)
    rank = n_seq * m.pq.shape[1]
    length = n_seq * tok
    greet(at.seq_ids() + at.dp_ids())
    swap_q = dp_exchange(at, m.pq, m.landed, *m.swap_q_sem, m.local.at[0])
    x_g = DpGather(at, m.x, m.xs, *m.x_sem, m.local.at[1])
    row_x = seq_exchange(at, m.seg_rows, m.seg_row, *m.row_x_sem, m.local.at[2])
    row_g = DpGather(at, m.seg_row, m.segs, *m.row_g_sem, m.local.at[3])
    col_g = DpGather(at, m.seg_col, m.seg_cols, *m.col_g_sem, m.local.at[4])
    ring_q = RingGather(at, m.landed, m.wq_all, *m.ring_q_sem, m.local.at[5])
    ring_o = RingGather(at, m.wo, m.wo_all, *m.ring_o_sem, m.local.at[6])
    ring_kv = RingGather(at, m.kv_own, m.kv_all, *m.ring_kv_sem, m.local.at[7])
    swap_gu = seq_exchange(at, m.pgu, m.gu, *m.swap_gu_sem, m.local.at[8])
    stores = []

    def store(src, dst):
        copy = pltpu.make_async_copy(src, dst, m.local.at[9 + len(stores)])
        copy.start()
        stores.append(copy)

    swap_q.start()
    x_g.start()
    row_x.start()
    col_g.start()

    def pack(weight, first):
        for s in range(n_seq):
            for i in range(n_dp):
                piece = weight[:, (i * n_seq + s) * own_ff : (i * n_seq + s + 1) * own_ff]
                m.pgu[s, :, first + i * own_ff : first + (i + 1) * own_ff] = (
                    m.gain[:, :1] * piece.astype(FULL)
                ).astype(LOW)

    swap_q.arrived()
    ring_q.step(0)
    row_x.arrived()
    row_g.start()

    def hand():
        x_g.hand()
        row_g.hand()
        col_g.hand()

    def norm():
        x_g.arrived()
        for r in range(n_dp):
            x = m.xs[r].astype(FULL)
            scale = lax.rsqrt(jnp.mean(x * x, -1, keepdims=True) + EPS)
            m.n1[r] = (x * scale).astype(LOW)
        store(m.n1, m.n1_out)

    def place():
        row_g.arrived()
        col_g.arrived()
        position = own_positions(at, tok)
        first = lax.rem(lanes(tok), HEAD_DIM) < HEAD_DIM // 2
        for r in range(n_dp):
            segs = jnp.concatenate([m.segs[r, s, :1] for s in range(n_seq)], 1)
            own = m.seg_cols[r][:, :1]
            start = jnp.sum((segs < own).astype(jnp.int32), 1, keepdims=True)
            turned = (position - start).astype(FULL) * m.freqs[:1]
            rows = slice(r * tok, (r + 1) * tok)
            m.cos[rows] = jnp.cos(turned)
            sines = jnp.sin(turned)
            m.sin[rows] = jnp.where(first, -sines, sines)
            m.starts[rows] = jnp.broadcast_to(start, (tok, 2 * HEAD_DIM))
        store(m.cos, m.cos_out)
        store(m.sin, m.sin_out)
        store(m.starts, m.starts_out)

    interleave(
        ring_q,
        [lambda: pack(m.wg, 0), hand, norm, place, lambda: pack(m.wu, n_dp * own_ff)],
    )
    ring_q.finish()
    ring_o.step(0)
    store(m.wq_all, m.wq_out)

    m.qkv[...] = sum(
        matmul(
            m.n1[:, :, i * rank : (i + 1) * rank].reshape(n_dp * tok, rank),
            m.wq_all[:, i].reshape(rank, q_width + 2 * HEAD_DIM),
        )
        for i in range(n_dp)
    )
    factor = HEAD_DIM ** (-0.5)
    for g in range(groups + 1):
        cols = slice(g * 2 * HEAD_DIM, (g + 1) * 2 * HEAD_DIM)
        pair = m.qkv[:, cols]
        turned = pair * m.cos[...] + swapped(pair) * m.sin[...]
        if g < groups:
            m.q[:, cols] = (turned * factor).astype(LOW)
        else:
            m.kv_own[...] = jnp.where(low_head(pair.shape[0]), turned, pair).astype(LOW)
    ring_kv.step(0)
    store(m.q, m.q_out)
    ring_o.step(1)
    for t in range(1, ring_kv.steps):
        ring_kv.step(t)
    ring_kv.finish()
    store(m.kv_all, m.kv_out)
    swap_gu.start()

    later = list(range(2, ring_o.steps))
    for r in range(n_dp):
        rows = slice(r * tok, (r + 1) * tok)
        k, v = spread_kv(m.kv_all[:, rows].reshape(length, 2 * HEAD_DIM))
        m.k2[...] = k
        m.v2[...] = v
        m.mask[...] = mask_of(own_positions(at, tok), m.starts[rows, :1], length)

        def group(g, carry):
            cols = rows_of(g, 2 * HEAD_DIM)
            raw = matmul_nt(split_heads(m.q[rows, cols]), m.k2[...])
            raw = raw + jnp.concatenate([m.mask[...]] * 2, 0)
            top = jnp.max(raw, -1, keepdims=True)
            probs = jnp.exp(raw - top)
            total = jnp.sum(probs, -1, keepdims=True)
            probs = (probs * (1.0 / total)).astype(LOW)
            m.o[rows, cols] = join_heads(matmul(probs, m.v2[...])).astype(LOW)
            m.lse[r * groups + g] = top + jnp.log(total)
            return carry

        lax.fori_loop(0, groups, group, 0)
        if later:
            ring_o.step(later.pop(0))
    for t in later:
        ring_o.step(t)
    store(m.o, m.o_out)
    store(m.lse, m.lse_out)
    ring_o.finish()
    store(m.wo_all, m.wo_out)
    full = m.wo_all[...].reshape(q_width, width)
    for r in range(n_dp):
        m.parts[r] = matmul(m.o[r * tok : (r + 1) * tok], full).astype(LOW)
    back = DpScatter(at, m.parts, *m.back)
    back.start()
    back.across()
    back.finish(m.middle)
    middle = m.x[...].astype(FULL) + m.middle[...]
    m.middle[...] = middle
    scale = lax.rsqrt(jnp.mean(middle * middle, -1, keepdims=True) + EPS)
    m.second[...] = (middle * scale).astype(LOW)
    swap_gu.arrived()
    for one in (swap_q, x_g, row_x, row_g, col_g, swap_gu):
        one.finish()
    for copy in stores:
        copy.wait()


def front(n_dp, n_seq, own_ff, x, seg_rows, seg_col, freqs, pq, wg, wu, gain, wo):
    tok, width = x.shape
    rank, columns = pq.shape[1:]
    q_width = columns - 2 * HEAD_DIM
    groups = q_width // (2 * HEAD_DIM)
    pair = 2 * HEAD_DIM
    length = n_seq * tok
    every = n_dp * tok
    gu_width = 2 * n_dp * own_ff
    ins = {
        "x": x, "seg_rows": seg_rows, "seg_col": seg_col, "freqs": freqs, "pq": pq, "wg": wg, "wu": wu, "gain": gain, "wo": wo,
    }
    ins = {key: (value, VMEM) for key, value in ins.items()}
    kept = {
        "n1": (LOW, n_dp, tok, width),
        "q": (LOW, every, q_width),
        "kv_all": (LOW, n_seq, every, pair),
        "o": (LOW, every, q_width),
        "lse": (FULL, n_dp * groups, 2 * tok, 1),
        "cos": (FULL, every, pair),
        "sin": (FULL, every, pair),
        "starts": (jnp.int32, every, pair),
        "wq_all": (LOW, n_seq, n_dp, rank, columns),
        "wo_all": (LOW, n_seq, rank, width),
    }
    outs = {
        key.replace("_all", "") + "_out": (shape_of(dims[1:], dims[0]), ANY)
        for key, dims in kept.items()
    }
    outs["gu"] = (shape_of((n_seq, rank, gu_width), LOW), ANY)
    outs["middle"] = (shape_of((tok, width), FULL), VMEM)
    outs["second"] = (shape_of((tok, width), LOW), VMEM)
    scratch = {key: vm(*dims) for key, dims in kept.items()}
    scratch |= {
        "landed": vm(LOW, n_dp, rank, columns),
        "xs": vm(LOW, n_dp, tok, width),
        "seg_row": vm(jnp.int32, n_seq, 8, tok),
        "segs": vm(jnp.int32, n_dp, n_seq, 8, tok),
        "seg_cols": vm(jnp.int32, n_dp, tok, pair),
        "kv_own": vm(LOW, every, pair),
        "mask": vm(FULL, tok, length),
        "pgu": vm(LOW, n_seq, rank, gu_width),
        "qkv": vm(FULL, every, columns),
        "k2": vm(LOW, length, pair),
        "v2": vm(LOW, length, pair),
        "parts": vm(LOW, n_dp, tok, width),
        "back": DpScatter.scratch(n_dp, tok, width),
        "local": dma(9 + len(kept)),
        "swap_q_sem": Exchange.scratch(n_dp),
        "x_sem": DpGather.scratch(n_dp),
        "row_x_sem": Exchange.scratch(n_seq),
        "row_g_sem": DpGather.scratch(n_dp),
        "col_g_sem": DpGather.scratch(n_dp),
        "ring_q_sem": Ring.semaphores(n_seq),
        "ring_o_sem": Ring.semaphores(n_seq),
        "ring_kv_sem": Ring.semaphores(n_seq),
        "swap_gu_sem": Exchange.scratch(n_seq),
    }
    return run(
        functools.partial(front_kernel, n_dp, n_seq, own_ff), "attention_forward", 1, ins, outs, scratch
    )


def feed_kernel(n_dp, n_seq, m):
    at = Where(n_dp, n_seq)
    greet(at.ring_ids() + at.dp_ids())
    ring_n = RingGather(at, m.second, m.second_all, *m.ring_n, m.local.at[0])
    ring_dy = RingGather(at, m.dy, m.dy_all, *m.ring_dy, m.local.at[1])
    gu = DpGather(at, m.gu, m.gu_all, *m.gu_sem, m.local.at[2])
    down = DpGather(at, m.wd, m.wd_all, *m.wd_sem, m.local.at[3])
    ring_n.step(0)
    gu.start()
    down.start()
    for t in range(1, ring_n.steps):
        ring_n.step(t)
    ring_dy.step(0)
    gu.hand()
    down.hand()
    for t in range(1, ring_dy.steps):
        ring_dy.step(t)
    for one in (gu, down):
        one.arrived()
    for one in (ring_n, ring_dy, gu, down):
        one.finish()


def feed(n_dp, n_seq, second, dy, gu, wd):
    ins = {"second": second, "dy": dy, "gu": gu, "wd": wd}
    outs = {
        "second_all": (shape_of((n_seq,) + second.shape, LOW), ANY),
        "dy_all": (shape_of((n_seq,) + dy.shape, LOW), ANY),
        "gu_all": (shape_of((n_dp,) + gu.shape, LOW), ANY),
        "wd_all": (shape_of((n_dp,) + wd.shape, LOW), ANY),
    }
    scratch = {
        "local": dma(4),
        "ring_n": Ring.semaphores(n_seq),
        "ring_dy": Ring.semaphores(n_seq),
        "gu_sem": DpGather.scratch(n_dp),
        "wd_sem": DpGather.scratch(n_dp),
    }
    return run(
        functools.partial(feed_kernel, n_dp, n_seq),
        "gather_feed_forward",
        2,
        {key: (value, ANY) for key, value in ins.items()},
        outs,
        scratch,
    )


def back_kernel(n_dp, n_seq, m):
    at = Where(n_dp, n_seq)
    tok, width = m.x.shape
    q_width = m.q.shape[1]
    groups = q_width // (2 * HEAD_DIM)
    rank = n_seq * m.wq.shape[2]
    length = n_seq * tok
    pair = 2 * HEAD_DIM
    greet(at.ring_ids() + at.dp_ids())
    ring_h = RingScatter(at, m.part_h, *m.ring_h, *m.staged)
    ring_y = RingScatter(at, m.part_y, m.ring_h[0], *m.ring_y, *m.staged)
    d_g = DpGather(at, m.d_own, m.d_all, *m.d_sem, m.local.at[0])
    ring_kv = RingScatter(at, m.part_kv, *m.ring_kv)
    ring_q = RingScatter(at, m.part_q, *m.ring_q)
    ring_o = RingScatter(at, m.part_o, *m.ring_o)
    back = DpScatter(at, m.d_all, *m.back)
    swap_q = dp_exchange(at, m.sum_q, m.got_q, *m.swap_q, m.local.at[1])
    for t in range(ring_h.steps):
        ring_h.step(t)
    ring_h.finish(m.dmid)
    for one in at.ring_ids():
        pl.semaphore_signal(m.free, inc=1, device_id=one, device_id_type=MESH)

    def norm_back(grad, value):
        scale = lax.rsqrt(jnp.mean(value * value, -1, keepdims=True) + EPS)
        normed = value * scale
        return scale * (grad - normed * jnp.mean(grad * normed, -1, keepdims=True))

    m.dmid[...] = m.dy[...].astype(FULL) + norm_back(m.dmid[...], m.middle[...])
    m.d_own[...] = m.dmid[...].astype(LOW)
    d_g.start()
    pl.semaphore_wait(m.free, 2)
    ring_y.step(0)
    d_g.hand()
    d_g.arrived()
    m.do[...] = matmul_nt(
        m.d_all[...].reshape(n_dp * tok, width), m.wo[...].reshape(q_width, width)
    ).astype(LOW)
    later = list(range(1, ring_y.steps))
    for r in range(n_dp):
        rows = slice(r * tok, (r + 1) * tok)
        k, v = spread_kv(m.kv[:, rows].reshape(length, pair))
        m.k2[...] = k
        m.v2[...] = v
        m.mask[...] = mask_of(own_positions(at, tok), m.starts[rows, :1], length)
        m.dk2[...] = jnp.zeros_like(m.dk2)
        m.dv2[...] = jnp.zeros_like(m.dv2)

        def group(g, carry):
            cols = rows_of(g, pair)
            q2 = split_heads(m.q[rows, cols])
            do2 = split_heads(m.do[rows, cols])
            raw = matmul_nt(q2, m.k2[...])
            raw = raw + jnp.concatenate([m.mask[...]] * 2, 0)
            probs = jnp.exp(raw - m.lse[r * groups + g])
            grad_probs = matmul_nt(do2, m.v2[...])
            delta = jnp.sum(probs * grad_probs, -1, keepdims=True)
            grad_raw = (probs * (grad_probs - delta)).astype(LOW)
            m.dq[rows, cols] = join_heads(matmul(grad_raw, m.k2[...]))
            m.dk2[...] += matmul_tn(grad_raw, q2)
            m.dv2[...] += matmul_tn(probs.astype(LOW), do2)
            return carry

        lax.fori_loop(0, groups, group, 0)
        dk = m.dk2[...]
        dv = m.dv2[...]
        dkv = jnp.where(
            low_head(length), dk + pltpu.roll(dk, HEAD_DIM, 1), dv + pltpu.roll(dv, HEAD_DIM, 1)
        )
        m.part_kv[:, rows] = dkv.astype(LOW).reshape(n_seq, tok, pair)
        if later:
            ring_y.step(later.pop(0))
    for t in later:
        ring_y.step(t)
    ring_kv.step(0)
    m.part_o[...] = (
        matmul_tn(m.o[...], m.d_all[...].reshape(n_dp * tok, width))
        .astype(LOW)
        .reshape(m.part_o.shape)
    )
    d_g.finish()
    for t in range(1, ring_kv.steps):
        ring_kv.step(t)
    ring_kv.finish(m.dkv)
    ring_y.finish(m.sum_y)
    n1 = m.ring_h[0].at[0, pl.ds(0, n_dp)]
    fetch = pltpu.make_async_copy(m.n1, n1, m.local.at[2])
    fetch.start()
    ring_o.step(0)
    m.out[...] = (m.middle[...] + m.sum_y[...]).astype(m.out.dtype)
    factor = HEAD_DIM ** (-0.5)
    for g in range(groups + 1):
        cols = slice(g * pair, (g + 1) * pair)
        grad = m.dq[:, cols] * factor if g < groups else m.dkv[...]
        turned = grad * m.cos[...] - swapped(grad) * m.sin[...]
        if g == groups:
            turned = jnp.where(low_head(grad.shape[0]), turned, grad)
        m.dqkv[:, cols] = turned.astype(LOW)
    for i in range(n_dp):
        cols = slice(i * rank, (i + 1) * rank)
        weight = m.wq[:, i].reshape(rank, q_width + pair)
        m.d_all[:, :, cols] = (
            matmul_nt(m.dqkv[...], weight).astype(LOW).reshape(n_dp, tok, rank)
        )
    back.start()
    fetch.wait()
    for i in range(n_dp):
        cols = slice(i * rank, (i + 1) * rank)
        m.part_q[:, i] = (
            matmul_tn(n1[:, :, cols].reshape(n_dp * tok, rank), m.dqkv[...]).astype(LOW).reshape(n_seq, rank // n_seq, q_width + pair)
        )
    ring_q.step(0)
    back.across()
    for t in range(1, ring_q.steps):
        ring_q.step(t)
        ring_o.step(t)
    back.finish(m.dn1)
    m.grad_x[...] = m.dmid[...] + norm_back(m.dn1[...], m.x[...].astype(FULL))
    ring_q.finish(m.sum_q)
    swap_q.start()
    ring_o.finish(m.grad_o)
    swap_q.arrived()
    swap_q.finish()


def back(n_dp, n_seq, dtype, ins):
    tok, width = ins["x"].shape
    every = n_dp * tok
    q_width = ins["q"].shape[1]
    pair = 2 * HEAD_DIM
    length = n_seq * tok
    rank, columns = ins["wq"].shape[2:]
    outs = {
        "out": (shape_of((tok, width), dtype), VMEM),
        "grad_x": (shape_of((tok, width), FULL), VMEM),
        "grad_o": (shape_of((rank, width), FULL), VMEM),
        "got_q": (shape_of((n_dp, rank, columns), LOW), ANY),
    }
    scratch = {
        "local": dma(3),
        "free": pltpu.SemaphoreType.REGULAR,
        "dmid": vm(FULL, tok, width),
        "d_own": vm(LOW, tok, width),
        "d_all": vm(LOW, n_dp, tok, width),
        "d_sem": DpGather.scratch(n_dp),
        "do": vm(LOW, every, q_width),
        "k2": vm(LOW, length, pair),
        "v2": vm(LOW, length, pair),
        "mask": vm(FULL, tok, length),
        "dk2": vm(FULL, length, pair),
        "dv2": vm(FULL, length, pair),
        "dq": vm(FULL, every, q_width),
        "dkv": vm(FULL, every, pair),
        "dqkv": vm(LOW, every, columns),
        "dn1": vm(FULL, tok, width),
        "sum_y": vm(FULL, tok, width),
        "sum_q": vm(LOW, n_dp, rank, columns),
        "part_kv": vm(LOW, n_seq, every, pair),
        "part_q": vm(LOW, n_seq, n_dp, rank, columns),
        "part_o": vm(LOW, n_seq, rank, width),
        "back": DpScatter.scratch(n_dp, tok, width),
        "ring_h": RingScatter.scratch(n_seq, tok, width),
        "ring_y": Ring.semaphores(n_seq),
        "staged": RingScatter.staging(tok, width),
        "ring_kv": RingScatter.scratch(n_seq, every, pair),
        "ring_q": RingScatter.scratch(n_seq, n_dp, rank, columns),
        "ring_o": RingScatter.scratch(n_seq, rank, width),
        "swap_q": Exchange.scratch(n_dp),
    }
    return run(
        functools.partial(back_kernel, n_dp, n_seq),
        "attention_backward",
        3,
        {key: (value, ANY if key in ("part_h", "part_y", "n1") else VMEM) for key, value in ins.items()},
        outs,
        scratch,
    )


def reduce_kernel(n_dp, n_seq, m):
    at = Where(n_dp, n_seq)
    greet(at.seq_ids() + at.dp_ids())
    down = DpScatter(at, m.rows, *m.down)
    side = DpScatter(at, m.cols, *m.side)
    side.start()
    down.start()
    side.across()
    down.across()
    side.finish(m.fin)
    n = m.got.shape[1]
    copies = []
    kept = pltpu.make_async_copy(m.fin.at[rows_of(at.seq, n)], m.got.at[at.seq], m.local.at[0])
    kept.start()
    for k, one in enumerate(at.seq_ids()):
        src = m.fin.at[rows_of(one[1], n)]
        copy = remote(src, m.got.at[at.seq], m.swap[0].at[k], m.swap[1].at[k], one)
        copy.start()
        copies.append(copy)
    down.finish(m.total)
    for copy in copies:
        copy.wait()
    kept.wait()


def reduce(n_dp, n_seq, cols, rows):
    _, deep, wide = cols.shape
    return run(
        functools.partial(reduce_kernel, n_dp, n_seq),
        "reduce_feed_forward_grads",
        4,
        {"cols": (cols, VMEM), "rows": (rows, VMEM)},
        {
            "got": (shape_of((n_seq, deep // n_seq, wide), LOW), ANY),
            "total": (shape_of(rows.shape[1:], FULL), VMEM),
        },
        {
            "local": dma(1),
            "side": DpScatter.scratch(n_dp, deep, wide),
            "down": DpScatter.scratch(n_dp, *rows.shape[1:]),
            "fin": vm(LOW, deep, wide),
            "swap": Exchange.scratch(n_seq),
        },
    )


def body(
    n_dp,
    n_seq,
    tokens,
    segment_ids,
    gain_attn,
    w_query,
    w_key,
    w_value,
    w_output,
    gain_mlp,
    w_gate,
    w_up,
    w_down,
    cotangent,
):
    local, width = tokens.shape[1], tokens.shape[2]
    length = n_seq * local
    own_rows = w_query.shape[0]
    own_ff = w_down.shape[0]
    part_ff = n_dp * own_ff
    heads = HEADS // n_dp
    q_width = heads * HEAD_DIM
    x_own = tokens.reshape(local, width)
    dy_own = cotangent.reshape(local, width)

    gain_one = gain_attn.astype(FULL)[:, None]
    gain_two = gain_mlp.astype(FULL)[:, None]
    kv_of = [i * heads // GROUP for i in range(n_dp)]

    def gained(weight):
        return (gain_one * weight.astype(FULL)).astype(LOW)

    pack_q = jnp.stack(
        [
            jnp.concatenate(
                [
                    gained(w_query[:, i * q_width : (i + 1) * q_width]),
                    gained(w_key[:, kv * HEAD_DIM : (kv + 1) * HEAD_DIM]),
                    gained(w_value[:, kv * HEAD_DIM : (kv + 1) * HEAD_DIM]),
                ],
                1,
            )
            for i, kv in enumerate(kv_of)
        ]
    )
    freqs = ROPE_BASE ** (-jnp.arange(0, HEAD_DIM, 2).astype(FULL) / HEAD_DIM)
    ids = segment_ids.reshape(local)
    pair = 2 * HEAD_DIM
    got = front(
        n_dp,
        n_seq,
        own_ff,
        x_own,
        jnp.broadcast_to(ids, (n_seq, 8, local)),
        jnp.broadcast_to(ids[:, None], (local, pair)),
        jnp.broadcast_to(jnp.tile(freqs, 4), (8, pair)),
        pack_q,
        w_gate,
        w_up,
        jnp.broadcast_to(gain_two, (own_rows, pair)),
        w_output,
    )
    down_block = w_down if own_ff % 16 == 0 else w_down.reshape(16, own_ff * width // 16)
    fed = feed(n_dp, n_seq, got["second"], dy_own, got["gu"], down_block)
    second = fed["second_all"].reshape(length, width)
    dy = fed["dy_all"].reshape(length, width)
    weight_gu = fed["gu_all"].reshape(width, 2 * part_ff)
    weight_d = fed["wd_all"].reshape(part_ff, width)

    both = matmul(second, weight_gu)
    gate, upward = both[:, :part_ff], both[:, part_ff:]
    sigma = jax.nn.sigmoid(gate)
    hidden = (gate * sigma * upward).astype(LOW)
    part_y = matmul(hidden, weight_d).astype(LOW).reshape(n_seq, local, width)
    grad_hidden = matmul_nt(dy, weight_d)
    grad_gate = (grad_hidden * upward * sigma * (1.0 + gate * (1.0 - sigma))).astype(LOW)
    grad_up = (grad_hidden * gate * sigma).astype(LOW)
    grad_both = jnp.concatenate([grad_gate, grad_up], 1)
    part_h = matmul_nt(grad_both, weight_gu).astype(LOW).reshape(n_seq, local, width)
    grad_gu = matmul_tn(second, grad_both).astype(LOW)
    grad_d = matmul_tn(hidden, dy).astype(LOW)

    ins = {
        "part_h": part_h,
        "part_y": part_y,
        "x": x_own,
        "dy": dy_own,
        "middle": got["middle"],
    }
    for name in ("n1", "q", "kv", "o", "lse", "cos", "sin", "starts", "wq", "wo"):
        ins[name] = got[name + "_out"]
    done = back(n_dp, n_seq, tokens.dtype, ins)
    reduced = reduce(
        n_dp,
        n_seq,
        grad_gu.reshape(n_dp, n_seq * own_rows, 2 * part_ff),
        grad_d.reshape((n_dp,) + down_block.shape),
    )
    got_q, got_gu = done["got_q"], reduced["got"]

    def ff_join(grads):
        return (
            grads.astype(FULL)
            .reshape(n_seq, own_rows, n_dp, own_ff)
            .transpose(1, 2, 0, 3)
            .reshape(own_rows, n_dp * n_seq * own_ff)
        )

    raw_gate = ff_join(got_gu[:, :, :part_ff])
    raw_up = ff_join(got_gu[:, :, part_ff:])
    raw_query = jnp.concatenate([got_q[i, :, :q_width] for i in range(n_dp)], 1).astype(FULL)

    def kv_join(first):
        terms = [got_q[i, :, first : first + HEAD_DIM].astype(FULL) for i in range(n_dp)]
        return jnp.concatenate(
            [
                sum(term for term, kv in zip(terms, kv_of) if kv == head)
                for head in range(KV_HEADS)
            ],
            1,
        )

    raw_key = kv_join(q_width)
    raw_value = kv_join(q_width + HEAD_DIM)

    def gain_grad(*pairs):
        return sum(jnp.sum(weight.astype(FULL) * raw, 1) for weight, raw in pairs)

    return (
        done["out"].reshape(tokens.shape),
        done["grad_x"].reshape(tokens.shape),
        gain_grad((w_query, raw_query), (w_key, raw_key), (w_value, raw_value)),
        gain_one * raw_query,
        gain_one * raw_key,
        gain_one * raw_value,
        done["grad_o"],
        gain_grad((w_gate, raw_gate), (w_up, raw_up)),
        gain_two * raw_gate,
        gain_two * raw_up,
        reduced["total"].reshape(own_ff, width),
    )


def solution(mesh):
    rows = P(("dp", "seq"), None)
    vector = P(("dp", "seq"))
    row = P("dp", "seq", None)
    return jax.shard_map(
        functools.partial(body, mesh.shape["dp"], mesh.shape["seq"]),
        mesh=mesh,
        in_specs=(row, P("dp", "seq"), vector, rows, rows, rows, rows, vector, rows, rows, rows, row),
        out_specs=(row, row, vector, rows, rows, rows, rows, vector, rows, rows, rows),
        check_vma=False,
    )
```

time: 742 us -> 574 us (0.77)
  Pallas kernels: 550 us -> 479 us
  other arithmetic: 60 us -> 13.6 us
  local copies, waits for them, and re-layouts: 53.8 us -> 27.6 us
  matrix products: 68.5 us -> 43.3 us
    pallas_call x11 -> x4, Pallas kernels: 550 us -> 479 us  [run(): pl.pallas_call(lambda *refs: kernel(Refs(names, refs)), name=name, out_sh...]
    dot_general x4 -> x2, matrix products: 24.8 us -> 12.7 us  [matmul_nt(): lax.dot_general(left, right, (((1,), (1,)), ((), ())), preferred_element_...]
    convert_element_type x11 -> x2, other arithmetic: 13.3 us -> 1.98 us  [gained(): return (gain_one * weight.astype(FULL)).astype(LOW)]
    reshape x9 -> x0, local copies, waits for them, and re-layouts: 10.3 us -> none  [the longest x4 6.05 us: ff_split(): weight.reshape(own_rows, n_dp, n_seq, own_ff).transpose(2, 0, 1, 3)]
    concatenate x5 -> x0, other arithmetic: 9.93 us -> none  [the longest x3 6.57 us: rotate(): jnp.concatenate([first * cosines - second * sines, second * cosines + fir...]
    reduce_sum x5 -> x0, other arithmetic: 8.89 us -> none  [the longest x1 3.22 us: body(): scale_one = lax.rsqrt(jnp.mean(inputs * inputs, -1, keepdims=True) + EPS)]
    dot_general x4 -> x2, matrix products: 21.5 us -> 13.1 us  [matmul_tn(): lax.dot_general(left, right, (((0,), (0,)), ((), ())), preferred_element_...]
    unnamed x101 -> x40, local copies, waits for them, and re-layouts: 12.6 us -> 4.82 us
  transfers between devices with their start and end apart: 2 -> 0, of which waited for: 0 -> 0; matrix products, arithmetic and copies ran while one was open for 4% -> 0% of each run, Pallas kernels for 9% -> 0%
where the time goes in v2:
time: 574 us; the launch traced here: 565 us
  Pallas kernels  479 us (83%)
  matrix products  43.3 us (8%)
  local copies, waits for them, and re-layouts  27.6 us (5%)
  other arithmetic  13.6 us (2%)
    pallas_call x4, Pallas kernels, run(): pl.pallas_call(lambda *refs: kernel(Refs(names, refs)), name=name, out_sh...  479 us
    dot_general x2, matrix products, matmul(): return jnp.dot(left, right, preferred_element_type=FULL)  17.5 us
    reshape x6, local copies, waits for them, and re-layouts, ff_join(): return grads.astype(FULL).reshape(n_seq, own_rows, n_dp, own_ff).transpos...  16.1 us
    dot_general x2, matrix products, matmul_tn(): lax.dot_general(left, right, (((0,), (0,)), ((), ())), preferred_element_...  13.1 us
    dot_general x2, matrix products, matmul_nt(): lax.dot_general(left, right, (((1,), (1,)), ((), ())), preferred_element_...  12.7 us

profile of v2, /device:TPU:0, one launch (start us, length us, event | category | flops | bytes accessed | tf_op | source)
XLA Modules:
  0.0 564.9 jit_solution(10094161124940662594)
XLA Ops:
  1.3 0.9 multiply_convert_fusion.14
  2.2 1.1 multiply_convert_fusion.6
  3.5 0.8 pad_maximum_fusion.3.refs_4_
  4.3 1.4 broadcast_in_dim.9.refs_2_
  5.6 1.3 broadcast_in_dim.8.refs_1_
  6.9 1.3 broadcast_in_dim.21.refs_7_
  8.9 124.7 %attention_forward.1 = (bf16[4,128,2048]{2,1,0:T(8,128)(2,1)}, bf16[512,512]{1,0:T(8,128)(2,1)}, bf16[8,512,128]{2,1,0:T(8,128)(2,1)}, bf16[512,512]{1,0:T(8,128...) custom-call(bf16[128,2048]{1,0:T(8,128)(2,1)} %bitcast.69, ...), custom_call_target="tpu_custom_call" | custom-call | tf_op jit(solution)/shard_map/attention_forward/pallas_call | solution.py:440
  133.7 103.1 %gather_feed_forward.1 = (bf16[8,128,2048]{2,1,0:T(8,128)(2,1)}, bf16[8,128,2048]{2,1,0:T(8,128)(2,1)}, bf16[4,8,64,1408]{3,2,1,0:T(8,128)(2,1)}, bf16[4,176,2048]{2,1,0:T(8,128)(2,1)}) custom-call(bf16[128,2048]{1,0:T(8,128)(2,1)} %get-tuple-element.34.refs_0_, bf16[128,2048]{1,0:T(8,128)(2,1)} %bitcast.67, bf16[8,64,1408]{2,1,0:T(8,128)(2,1)} %get-tuple-element.35.refs_2_, ...), custom_call_target="tpu_custom_call" | custom-call | tf_op jit(solution)/shard_map/gather_feed_forward/pallas_call | solution.py:440
  236.8 10.9 %fusion.5 = f32[1024,1408]{0,1:T(8,128)S(1)} fusion(bf16[1024,2048]{1,0:T(8,128)(2,1)} %bitcast.79, bf16[2048,1408]{1,0:T(8,128)(2,1)} %bitcast.75), kind=kOutput, calls=%fused_computation.60 | convolution fusion | flops 5905580032 | bytes 15728640 | tf_op jit(solution)/shard_map/dot_general | solution.py:25
  247.7 4.2 multiply_convert_fusion.2
  251.9 4.5 convolution_convert_fusion.3
  256.5 8.6 %convolution_convert_fusion = bf16[2048,1408]{1,0:T(8,128)(2,1)} fusion(bf16[1024,2048]{1,0:T(8,128)(2,1)S(1)} %bitcast.80, bf16[1024,704]{0,1:T(8,128)(2,1)S(1)} %get-tuple-element.58, bf16[1024,704]{0,1:T(8,128)(2,1)S(1)} %get-tuple-element.57), kind=kOutput, calls=%fused_computation | convolution fusion | flops 5914230784 | bytes 12845056 | tf_op jit(solution)/shard_map/dot_general | solution.py:33
  265.0 69.8 %reduce_feed_forward_grads.1 = (bf16[8,64,1408]{2,1,0:T(8,128)(2,1)}, f32[176,2048]{1,0:T(8,128)}) custom-call(bf16[4,512,1408]{2,1,0:T(8,128)(2,1)} %bitcast.63, bf16[4,176,2048]{2,1,0:T(8,128)(2,1)} %bitcast.66), custom_call_target="tpu_custom_call" | custom-call | tf_op jit(solution)/shard_map/reduce_feed_forward_grads/pallas_call | solution.py:440
  334.8 3.5 slice_convert_fusion
  338.3 3.0 reshape.134
  341.4 2.6 copy.25
  343.9 2.5 reshape.128
  346.4 3.0 reshape.136
  349.5 2.6 copy.26
  352.0 2.5 reshape.130
  354.5 3.6 broadcast_multiply_fusion
  358.7 6.6 %convolution_convert_fusion.1 = bf16[1024,2048]{1,0:T(8,128)(2,1)} fusion(bf16[1024,704]{0,1:T(8,128)(2,1)} %copy-done.11, bf16[704,2048]{1,0:T(8,128)(2,1)S(1)} %bitcast.84), kind=kOutput, calls=%fused_computation.1 | convolution fusion | flops 2954887168 | bytes 8519680 | tf_op jit(solution)/shard_map/dot_general | solution.py:25
  365.3 8.5 %convolution_convert_fusion.2 = bf16[1024,2048]{1,0:T(8,128)(2,1)} fusion(bf16[2048,1408]{1,0:T(8,128)(2,1)S(1)} %bitcast.78, bf16[1024,704]{0,1:T(8,128)(2,1)S(1)} %copy-done.15, bf16[1024,704]{0,1:T(8,128)(2,1)S(1)} %copy-done.13), kind=kOutput, calls=%fused_computation.2 | convolution fusion | flops 5913444352 | bytes 12845056 | tf_op jit(solution)/shard_map/dot_general | solution.py:29
  373.8 181.4 %attention_backward.1 = (bf16[128,2048]{1,0:T(8,128)(2,1)}, f32[128,2048]{1,0:T(8,128)}, f32[64,2048]{1,0:T(8,128)}, bf16[4,64,640]{2,1,0:T(8,128)(2,1)}) custom-call(bf16[8,128,2048]{2,1,0:T(8,128)(2,1)} %bitcast.65, bf16[8,128,2048]{2,1,0:T(8,128)(2,1)} %bitcast.64, bf16[128,2048]{1,0:T(8,128)(2,1)} %bitcast.70, bf16[128,2048]{1,0:T(8,128)(2,1)} %bitcast.68, ...), custom_call_target="tpu_custom_call" | custom-call | tf_op jit(solution)/shard_map/attention_backward/pallas_call | solution.py:440
  555.2 1.1 slice_bitcast_fusion.3
  556.3 1.0 convert_multiply_fusion
  557.3 1.0 slice_bitcast_fusion.11
  558.3 0.9 convert_multiply_fusion.2
  559.7 1.9 copy.32
  561.6 1.0 copy.33
  562.6 0.8 copy.34
  563.4 1.1 copy.35
  (47 shorter events, 2.7 us)
Async XLA Ops:
  236.8 10.9 %copy-start.8 = (bf16[8,128,2048]{2,1,0:T(8,128)(2,1)S(1)}, bf16[8,128,2048]{2,1,0:T(8,128)(2,1)}, u32[]{:S(2)}) copy-start(bf16[8,128,2048]{2,1,0:T(8,128)(2,1)} %get-tuple-element.36) | copy-start | bytes 12582916
  236.8 10.9 %copy-start.9 = (bf16[4,176,2048]{2,1,0:T(8,128)(2,1)S(1)}, bf16[4,176,2048]{2,1,0:T(8,128)(2,1)}, u32[]{:S(2)}) copy-start(bf16[4,176,2048]{2,1,0:T(8,128)(2,1)} %get-tuple-element.37) | copy-start | bytes 8650756
  251.9 4.5 copy-start.11
  251.9 4.5 copy-start.12
  251.9 4.5 copy-start.14
  251.9 4.5 copy-start.7
  349.4 5.1 copy-start.6
  354.5 4.1 copy-start.10
  354.5 10.7 %slice-start = ((s8[5767168]{0:T(1024)(128)(4,1)}), s8[4194304]{0:T(1024)(128)(4,1)S(1)}, s32[]{:S(2)}) async-start(s8[5767168]{0:T(1024)(128)(4,1)} %bitcast.76), calls=%async_computation | async-start | bytes 8388608
  358.6 6.6 %slice-start.1 = ((s8[5767168]{0:T(1024)(128)(4,1)}), s8[1572864]{0:T(1024)(128)(4,1)S(1)}, s32[]{:S(2)}) async-start(s8[5767168]{0:T(1024)(128)(4,1)} %bitcast.76), calls=%async_computation.1 | async-start | bytes 3145728
  358.6 6.6 %copy-start.13 = (bf16[1024,704]{0,1:T(8,128)(2,1)S(1)}, bf16[1024,704]{0,1:T(8,128)(2,1)}, u32[]{:S(2)}) copy-start(bf16[1024,704]{0,1:T(8,128)(2,1)} %copy-done.12) | copy-start | bytes 4325380
  358.7 6.6 %copy-start.15 = (bf16[1024,704]{0,1:T(8,128)(2,1)S(1)}, bf16[1024,704]{0,1:T(8,128)(2,1)}, u32[]{:S(2)}) copy-start(bf16[1024,704]{0,1:T(8,128)(2,1)} %copy-done.14) | copy-start | bytes 4325380
  373.8 182.5 %copy-start.1 = (bf16[64,2048]{1,0:T(8,128)(2,1)S(1)}, bf16[64,2048]{1,0:T(8,128)(2,1)}, u32[]{:S(2)}) copy-start(bf16[64,2048]{1,0:T(8,128)(2,1)} %param.15) | copy-start | bytes 786436
  373.8 184.5 %copy-start.4 = (bf16[64,256]{1,0:T(8,128)(2,1)S(1)}, bf16[64,256]{1,0:T(8,128)(2,1)}, u32[]{:S(2)}) copy-start(bf16[64,256]{1,0:T(8,128)(2,1)} %param.16) | copy-start | bytes 98308
  373.8 184.5 %copy-start.5 = (bf16[64,256]{1,0:T(8,128)(2,1)S(1)}, bf16[64,256]{1,0:T(8,128)(2,1)}, u32[]{:S(2)}) copy-start(bf16[64,256]{1,0:T(8,128)(2,1)} %param.17) | copy-start | bytes 98308
  555.2 6.4 %copy-start.2 = (f32[128,2048]{1,0:T(8,128)S(1)}, f32[128,2048]{1,0:T(8,128)}, u32[]{:S(2)}) copy-start(f32[128,2048]{1,0:T(8,128)} %get-tuple-element.52) | copy-start | bytes 3145732
  555.2 7.4 %copy-start.3 = (f32[64,2048]{1,0:T(8,128)S(1)}, f32[64,2048]{1,0:T(8,128)}, u32[]{:S(2)}) copy-start(f32[64,2048]{1,0:T(8,128)} %get-tuple-element.125) | copy-start | bytes 1572868
  556.3 7.1 %copy-start = (f32[176,2048]{1,0:T(8,128)S(1)}, f32[176,2048]{1,0:T(8,128)}, u32[]{:S(2)}) copy-start(f32[176,2048]{1,0:T(8,128)} %get-tuple-element.129) | copy-start | bytes 4325380

commit v3 on v2

--- a/solution.py
+++ b/solution.py
@@ -142,6 +142,8 @@
     def step(self, t):
         if t == 0:
             self.kept.start()
+        if t == 1:
+            self.kept.wait()
         for h, d in self.pieces():
             if t == self.steps - 1 and not self.opposite(h, d):
                 continue
@@ -151,13 +153,17 @@
             dst = self.everything.at[origin, self.rows(h)]
             self.go(self.own.at[self.rows(h)] if t == 0 else dst, dst, d, t, h)
 
+    def rest(self, t):
+        for key in self.copies:
+            if key not in self.waited and key[1] <= t:
+                self.wait(key)
+
     def finish(self):
-        for key in self.copies:
-            if key not in self.waited:
-                self.wait(key)
+        self.rest(self.steps)
         for copy in self.copies.values():
             copy.wait_send()
-        self.kept.wait()
+        if self.steps == 1:
+            self.kept.wait()
 
 
 class RingScatter(Ring):
@@ -516,7 +522,7 @@
         job()
 
 
-def front_kernel(n_dp, n_seq, own_ff, m):
+def front_kernel(n_dp, n_seq, own_ff, ff, m):
     at = Where(n_dp, n_seq)
     tok, width = m.x.shape
     q_width = m.q.shape[1]
@@ -533,10 +539,11 @@
     ring_o = RingGather(at, m.wo, m.wo_all, *m.ring_o_sem, m.local.at[6])
     ring_kv = RingGather(at, m.kv_own, m.kv_all, *m.ring_kv_sem, m.local.at[7])
     swap_gu = seq_exchange(at, m.pgu, m.gu, *m.swap_gu_sem, m.local.at[8])
+    down = DpGather(at, m.wd, m.wd_all, *m.down_sem, m.local.at[9])
     stores = []
 
     def store(src, dst):
-        copy = pltpu.make_async_copy(src, dst, m.local.at[9 + len(stores)])
+        copy = pltpu.make_async_copy(src, dst, m.local.at[10 + len(stores)])
         copy.start()
         stores.append(copy)
 
@@ -546,15 +553,20 @@
     col_g.start()
 
     def pack(weight, first):
+        if ff > own_ff:
+            m.pgu[:, :, first : first + n_dp * ff] = jnp.zeros(
+                m.pgu.shape[:2] + (n_dp * ff,), LOW
+            )
         for s in range(n_seq):
             for i in range(n_dp):
                 piece = weight[:, (i * n_seq + s) * own_ff : (i * n_seq + s + 1) * own_ff]
-                m.pgu[s, :, first + i * own_ff : first + (i + 1) * own_ff] = (
+                m.pgu[s, :, first + i * ff : first + i * ff + own_ff] = (
                     m.gain[:, :1] * piece.astype(FULL)
                 ).astype(LOW)
 
     swap_q.arrived()
     ring_q.step(0)
+    down.start()
     row_x.arrived()
     row_g.start()
 
@@ -592,7 +604,7 @@
 
     interleave(
         ring_q,
-        [lambda: pack(m.wg, 0), hand, norm, place, lambda: pack(m.wu, n_dp * own_ff)],
+        [lambda: pack(m.wg, 0), hand, norm, place, lambda: pack(m.wu, n_dp * ff)],
     )
     ring_q.finish()
     ring_o.step(0)
@@ -619,6 +631,7 @@
     ring_o.step(1)
     for t in range(1, ring_kv.steps):
         ring_kv.step(t)
+    down.hand()
     ring_kv.finish()
     store(m.kv_all, m.kv_out)
     swap_gu.start()
@@ -664,13 +677,14 @@
     scale = lax.rsqrt(jnp.mean(middle * middle, -1, keepdims=True) + EPS)
     m.second[...] = (middle * scale).astype(LOW)
     swap_gu.arrived()
-    for one in (swap_q, x_g, row_x, row_g, col_g, swap_gu):
+    down.arrived()
+    for one in (swap_q, x_g, row_x, row_g, col_g, swap_gu, down):
         one.finish()
     for copy in stores:
         copy.wait()
 
 
-def front(n_dp, n_seq, own_ff, x, seg_rows, seg_col, freqs, pq, wg, wu, gain, wo):
+def front(n_dp, n_seq, own_ff, x, seg_rows, seg_col, freqs, pq, wg, wu, gain, wo, wd):
     tok, width = x.shape
     rank, columns = pq.shape[1:]
     q_width = columns - 2 * HEAD_DIM
@@ -678,11 +692,13 @@
     pair = 2 * HEAD_DIM
     length = n_seq * tok
     every = n_dp * tok
-    gu_width = 2 * n_dp * own_ff
+    ff = wd.shape[0]
+    gu_width = 2 * n_dp * ff
     ins = {
         "x": x, "seg_rows": seg_rows, "seg_col": seg_col, "freqs": freqs, "pq": pq, "wg": wg, "wu": wu, "gain": gain, "wo": wo,
     }
     ins = {key: (value, VMEM) for key, value in ins.items()}
+    ins["wd"] = (wd, ANY)
     kept = {
         "n1": (LOW, n_dp, tok, width),
         "q": (LOW, every, q_width),
@@ -700,6 +716,7 @@
         for key, dims in kept.items()
     }
     outs["gu"] = (shape_of((n_seq, rank, gu_width), LOW), ANY)
+    outs["wd_all"] = (shape_of((n_dp,) + wd.shape, LOW), ANY)
     outs["middle"] = (shape_of((tok, width), FULL), VMEM)
     outs["second"] = (shape_of((tok, width), LOW), VMEM)
     scratch = {key: vm(*dims) for key, dims in kept.items()}
@@ -717,7 +734,7 @@
         "v2": vm(LOW, length, pair),
         "parts": vm(LOW, n_dp, tok, width),
         "back": DpScatter.scratch(n_dp, tok, width),
-        "local": dma(9 + len(kept)),
+        "local": dma(10 + len(kept)),
         "swap_q_sem": Exchange.scratch(n_dp),
         "x_sem": DpGather.scratch(n_dp),
         "row_x_sem": Exchange.scratch(n_seq),
@@ -727,61 +744,171 @@
         "ring_o_sem": Ring.semaphores(n_seq),
         "ring_kv_sem": Ring.semaphores(n_seq),
         "swap_gu_sem": Exchange.scratch(n_seq),
+        "down_sem": DpGather.scratch(n_dp),
     }
     return run(
-        functools.partial(front_kernel, n_dp, n_seq, own_ff), "attention_forward", 1, ins, outs, scratch
+        functools.partial(front_kernel, n_dp, n_seq, own_ff, ff), "attention_forward", 1, ins, outs, scratch
     )
 
 
 def feed_kernel(n_dp, n_seq, m):
     at = Where(n_dp, n_seq)
+    tok, width = m.second.shape
+    wide = m.wgu.shape[2]
+    part = wide // 2
+    rank = width // n_dp
+    length = n_seq * tok
     greet(at.ring_ids() + at.dp_ids())
-    ring_n = RingGather(at, m.second, m.second_all, *m.ring_n, m.local.at[0])
-    ring_dy = RingGather(at, m.dy, m.dy_all, *m.ring_dy, m.local.at[1])
-    gu = DpGather(at, m.gu, m.gu_all, *m.gu_sem, m.local.at[2])
-    down = DpGather(at, m.wd, m.wd_all, *m.wd_sem, m.local.at[3])
+    gu = DpGather(at, m.gu, m.wgu, *m.gu_sem, m.local.at[0])
+    ring_n = RingGather(at, m.second, m.second_all, *m.ring_n, m.local.at[1])
+    ring_dy = RingGather(at, m.dy, m.dy_all, *m.ring_dy, m.local.at[2])
+    ring_h = RingScatter(at, m.part, *m.ring_h)
+    side = DpScatter(at, m.wgu, *m.side)
+    down = DpScatter(at, m.wd, *m.down)
+    gu.start()
+    held = pltpu.make_async_copy(m.wd_all, m.wd, m.local.at[3])
+    held.start()
     ring_n.step(0)
-    gu.start()
-    down.start()
     for t in range(1, ring_n.steps):
         ring_n.step(t)
     ring_dy.step(0)
     gu.hand()
-    down.hand()
+    ring_n.finish()
+    gu.arrived()
+    held.wait()
+    stores = []
+
+    def forward(c):
+        blocks = slice(2 * c, 2 * c + 2)
+        normed = m.second_all[blocks].reshape(2 * tok, width)
+        both = matmul(normed, m.wgu[...].reshape(width, wide))
+        gate, upward = both[:, :part], both[:, part:]
+        sigma = jax.nn.sigmoid(gate)
+        silu = gate * sigma
+        hidden = (silu * upward).astype(LOW)
+        m.by_up[blocks] = silu.reshape(2, tok, part)
+        m.by_gate[blocks] = (upward * sigma * (1.0 + gate * (1.0 - sigma))).reshape(2, tok, part)
+        m.hidden[blocks] = hidden.reshape(2, tok, part)
+        out = matmul(hidden, m.wd[...].reshape(part, width))
+        m.part[blocks] = out.astype(LOW).reshape(2, tok, width)
+        copy = pltpu.make_async_copy(m.part.at[blocks], m.part_y.at[blocks], m.store.at[c])
+        copy.start()
+        stores.append(copy)
+
+    def backward(blocks):
+        rows = len(blocks) * tok
+        dy = jnp.concatenate([m.dy_all[b] for b in blocks], 0)
+        grad = matmul_nt(dy, m.wd[...].reshape(part, width))
+        for k, b in enumerate(blocks):
+            one = grad[k * tok : (k + 1) * tok]
+            m.grads[b, :, :part] = (one * m.by_gate[b]).astype(LOW)
+            m.grads[b, :, part:] = (one * m.by_up[b]).astype(LOW)
+        both = jnp.concatenate([m.grads[b] for b in blocks], 0)
+        for i in range(n_dp):
+            cols = slice(i * rank, (i + 1) * rank)
+            out = matmul_nt(both, m.wgu[i]).astype(LOW)
+            for k, b in enumerate(blocks):
+                m.part[b, :, cols] = out[k * tok : (k + 1) * tok]
+
+    jobs = [functools.partial(forward, c) for c in range(n_seq // 2)]
+
+    def stored():
+        for copy in stores:
+            copy.wait()
+
+    jobs.append(stored)
+    jobs.append(lambda: backward([at.seq]))
     for t in range(1, ring_dy.steps):
+        for _ in range(2):
+            if jobs:
+                jobs.pop(0)()
         ring_dy.step(t)
-    for one in (gu, down):
-        one.arrived()
-    for one in (ring_n, ring_dy, gu, down):
-        one.finish()
+        if t < ring_dy.steps - 1:
+            jobs.append(functools.partial(backward, [at.ring(-t), at.ring(t)]))
+    for job in jobs:
+        job()
+    if ring_dy.steps > 1:
+        ring_dy.rest(ring_dy.steps - 2)
+        backward([at.ring(1 - ring_dy.steps), at.ring(ring_dy.steps - 1)])
+    ring_dy.finish()
+    backward([at.ring(ring_dy.steps)])
+    gu.finish()
+
+    ring_h.step(0)
+    grads = m.grads[...].reshape(length, wide)
+
+    def grad_gu(k):
+        chip = lax.rem(at.chip + 1 + k, at.chips)
+        for c in (0, 1):
+            normed = m.second_all[:, :, rows_of(2 * chip + c, rank)].reshape(length, rank)
+            m.wgu[2 * chip + c] = matmul_tn(normed, m.grads[...].reshape(length, wide)).astype(LOW)
+        side.to_core(chip).start()
+
+    def grad_down():
+        step = width // n_dp
+        for i in range(n_dp):
+            cols = slice(i * step, (i + 1) * step)
+            dy = m.dy_all[:, :, cols].reshape(length, step)
+            m.wd[:, :, cols] = (
+                matmul_tn(m.hidden[...].reshape(length, part), dy)
+                .astype(LOW)
+                .reshape(m.wd.shape[:2] + (step,))
+            )
+        down.start()
+
+    jobs = [functools.partial(grad_gu, 0)]
+    jobs += [functools.partial(grad_gu, k) for k in range(1, at.chips)]
+    jobs.insert(max(len(jobs) - 1, 1), side.across)
+    jobs.append(grad_down)
+    jobs.append(down.across)
+    per = -(-len(jobs) // (ring_h.steps))
+    for t in range(1, ring_h.steps):
+        for _ in range(per):
+            if jobs:
+                jobs.pop(0)()
+        ring_h.step(t)
+    for job in jobs:
+        job()
+    ring_h.finish(m.grad_h)
+    side.finish(m.fin)
+    down.finish(m.grad_d)
 
 
 def feed(n_dp, n_seq, second, dy, gu, wd):
-    ins = {"second": second, "dy": dy, "gu": gu, "wd": wd}
+    tok, width = second.shape
+    deep, wide = gu.shape
+    ff = wd.shape[1]
+    part = wide // 2
+    ins = {"second": (second, ANY), "dy": (dy, ANY), "gu": (gu, ANY), "wd_all": (wd, ANY)}
     outs = {
-        "second_all": (shape_of((n_seq,) + second.shape, LOW), ANY),
-        "dy_all": (shape_of((n_seq,) + dy.shape, LOW), ANY),
-        "gu_all": (shape_of((n_dp,) + gu.shape, LOW), ANY),
-        "wd_all": (shape_of((n_dp,) + wd.shape, LOW), ANY),
+        "part_y": (shape_of((n_seq, tok, width), LOW), ANY),
+        "grad_h": (shape_of((tok, width), FULL), VMEM),
+        "fin": (shape_of((deep, wide), LOW), VMEM),
+        "grad_d": (shape_of((ff, width), FULL), VMEM),
     }
     scratch = {
         "local": dma(4),
+        "wd": vm(LOW, *wd.shape),
+        "store": dma(n_seq // 2),
+        "second_all": vm(LOW, n_seq, tok, width),
+        "dy_all": vm(LOW, n_seq, tok, width),
+        "wgu": vm(LOW, n_dp, deep, wide),
+        "by_gate": vm(FULL, n_seq, tok, part),
+        "by_up": vm(FULL, n_seq, tok, part),
+        "hidden": vm(LOW, n_seq, tok, part),
+        "grads": vm(LOW, n_seq, tok, wide),
+        "part": vm(LOW, n_seq, tok, width),
+        "gu_sem": DpGather.scratch(n_dp),
         "ring_n": Ring.semaphores(n_seq),
         "ring_dy": Ring.semaphores(n_seq),
-        "gu_sem": DpGather.scratch(n_dp),
-        "wd_sem": DpGather.scratch(n_dp),
+        "ring_h": RingScatter.scratch(n_seq, tok, width),
+        "side": DpScatter.scratch(n_dp, deep, wide),
+        "down": DpScatter.scratch(n_dp, ff, width),
     }
-    return run(
-        functools.partial(feed_kernel, n_dp, n_seq),
-        "gather_feed_forward",
-        2,
-        {key: (value, ANY) for key, value in ins.items()},
-        outs,
-        scratch,
-    )
-
-
-def back_kernel(n_dp, n_seq, m):
+    return run(functools.partial(feed_kernel, n_dp, n_seq), "feed_forward", 2, ins, outs, scratch)
+
+
+def back_kernel(n_dp, n_seq, own_ff, ff, m):
     at = Where(n_dp, n_seq)
     tok, width = m.x.shape
     q_width = m.q.shape[1]
@@ -789,30 +916,26 @@
     rank = n_seq * m.wq.shape[2]
     length = n_seq * tok
     pair = 2 * HEAD_DIM
-    greet(at.ring_ids() + at.dp_ids())
-    ring_h = RingScatter(at, m.part_h, *m.ring_h, *m.staged)
-    ring_y = RingScatter(at, m.part_y, m.ring_h[0], *m.ring_y, *m.staged)
+    greet(at.seq_ids() + at.dp_ids())
+    swap_gu = [
+        remote(m.fin.at[one[1]], m.got_gu.at[at.seq], m.swap_gu[0].at[k], m.swap_gu[1].at[k], one)
+        for k, one in enumerate(at.seq_ids())
+    ]
+    ring_y = RingScatter(at, m.part_y, *m.ring_y, *m.staged)
     d_g = DpGather(at, m.d_own, m.d_all, *m.d_sem, m.local.at[0])
     ring_kv = RingScatter(at, m.part_kv, *m.ring_kv)
     ring_q = RingScatter(at, m.part_q, *m.ring_q)
     ring_o = RingScatter(at, m.part_o, *m.ring_o)
     back = DpScatter(at, m.d_all, *m.back)
     swap_q = dp_exchange(at, m.sum_q, m.got_q, *m.swap_q, m.local.at[1])
-    for t in range(ring_h.steps):
-        ring_h.step(t)
-    ring_h.finish(m.dmid)
-    for one in at.ring_ids():
-        pl.semaphore_signal(m.free, inc=1, device_id=one, device_id_type=MESH)
-
     def norm_back(grad, value):
         scale = lax.rsqrt(jnp.mean(value * value, -1, keepdims=True) + EPS)
         normed = value * scale
         return scale * (grad - normed * jnp.mean(grad * normed, -1, keepdims=True))
 
-    m.dmid[...] = m.dy[...].astype(FULL) + norm_back(m.dmid[...], m.middle[...])
+    m.dmid[...] = m.dy[...].astype(FULL) + norm_back(m.grad_h[...], m.middle[...])
     m.d_own[...] = m.dmid[...].astype(LOW)
     d_g.start()
-    pl.semaphore_wait(m.free, 2)
     ring_y.step(0)
     d_g.hand()
     d_g.arrived()
@@ -820,9 +943,18 @@
         m.d_all[...].reshape(n_dp * tok, width), m.wo[...].reshape(q_width, width)
     ).astype(LOW)
     later = list(range(1, ring_y.steps))
+
+    def load_kv(r):
+        block = m.kv.at[:, pl.ds(r * tok, tok)]
+        return pltpu.make_async_copy(block, m.kv_row.at[r % 2], m.load.at[r % 2])
+
+    load_kv(0).start()
     for r in range(n_dp):
         rows = slice(r * tok, (r + 1) * tok)
-        k, v = spread_kv(m.kv[:, rows].reshape(length, pair))
+        load_kv(r).wait()
+        if r + 1 < n_dp:
+            load_kv(r + 1).start()
+        k, v = spread_kv(m.kv_row[r % 2].reshape(length, pair))
         m.k2[...] = k
         m.v2[...] = v
         m.mask[...] = mask_of(own_positions(at, tok), m.starts[rows, :1], length)
@@ -865,12 +997,14 @@
     for t in range(1, ring_kv.steps):
         ring_kv.step(t)
     ring_kv.finish(m.dkv)
-    ring_y.finish(m.sum_y)
-    n1 = m.ring_h[0].at[0, pl.ds(0, n_dp)]
+    ring_y.finish(m.wide)
+    for copy in swap_gu:
+        copy.start()
+    n1 = m.ring_y[0].at[0, pl.ds(0, n_dp)]
     fetch = pltpu.make_async_copy(m.n1, n1, m.local.at[2])
     fetch.start()
     ring_o.step(0)
-    m.out[...] = (m.middle[...] + m.sum_y[...]).astype(m.out.dtype)
+    m.out[...] = (m.middle[...] + m.wide[...]).astype(m.out.dtype)
     factor = HEAD_DIM ** (-0.5)
     for g in range(groups + 1):
         cols = slice(g * pair, (g + 1) * pair)
@@ -897,16 +1031,29 @@
     for t in range(1, ring_q.steps):
         ring_q.step(t)
         ring_o.step(t)
-    back.finish(m.dn1)
-    m.grad_x[...] = m.dmid[...] + norm_back(m.dn1[...], m.x[...].astype(FULL))
+    back.finish(m.wide)
+    m.grad_x[...] = m.dmid[...] + norm_back(m.wide[...], m.x[...].astype(FULL))
     ring_q.finish(m.sum_q)
     swap_q.start()
     ring_o.finish(m.grad_o)
+    for copy in swap_gu:
+        copy.wait()
+    m.got_gu[at.seq] = m.fin[at.seq]
+    gain = m.gain[:, :1]
+    gain_grad = jnp.zeros(gain.shape, FULL)
+    for weight, grad, first in ((m.wg, m.grad_g, 0), (m.wu, m.grad_u, n_dp * ff)):
+        for s in range(n_seq):
+            for i in range(n_dp):
+                raw = m.got_gu[s, :, first + i * ff : first + i * ff + own_ff].astype(FULL)
+                cols = slice((i * n_seq + s) * own_ff, (i * n_seq + s + 1) * own_ff)
+                gain_grad += jnp.sum(weight[:, cols].astype(FULL) * raw, 1, keepdims=True)
+                grad[:, cols] = gain * raw
+    m.grad_gain[...] = jnp.broadcast_to(gain_grad, m.grad_gain.shape)
     swap_q.arrived()
     swap_q.finish()
 
 
-def back(n_dp, n_seq, dtype, ins):
+def back(n_dp, n_seq, own_ff, ff, dtype, ins):
     tok, width = ins["x"].shape
     every = n_dp * tok
     q_width = ins["q"].shape[1]
@@ -918,10 +1065,14 @@
         "grad_x": (shape_of((tok, width), FULL), VMEM),
         "grad_o": (shape_of((rank, width), FULL), VMEM),
         "got_q": (shape_of((n_dp, rank, columns), LOW), ANY),
+        "grad_g": (shape_of(ins["wg"].shape, FULL), VMEM),
+        "grad_u": (shape_of(ins["wg"].shape, FULL), VMEM),
+        "grad_gain": (shape_of((rank, pair), FULL), VMEM),
     }
     scratch = {
         "local": dma(3),
-        "free": pltpu.SemaphoreType.REGULAR,
+        "load": dma(2),
+        "kv_row": vm(LOW, 2, n_seq, tok, pair),
         "dmid": vm(FULL, tok, width),
         "d_own": vm(LOW, tok, width),
         "d_all": vm(LOW, n_dp, tok, width),
@@ -935,74 +1086,28 @@
         "dq": vm(FULL, every, q_width),
         "dkv": vm(FULL, every, pair),
         "dqkv": vm(LOW, every, columns),
-        "dn1": vm(FULL, tok, width),
-        "sum_y": vm(FULL, tok, width),
+        "wide": vm(FULL, tok, width),
         "sum_q": vm(LOW, n_dp, rank, columns),
         "part_kv": vm(LOW, n_seq, every, pair),
         "part_q": vm(LOW, n_seq, n_dp, rank, columns),
         "part_o": vm(LOW, n_seq, rank, width),
         "back": DpScatter.scratch(n_dp, tok, width),
-        "ring_h": RingScatter.scratch(n_seq, tok, width),
-        "ring_y": Ring.semaphores(n_seq),
+        "ring_y": RingScatter.scratch(n_seq, tok, width),
         "staged": RingScatter.staging(tok, width),
         "ring_kv": RingScatter.scratch(n_seq, every, pair),
         "ring_q": RingScatter.scratch(n_seq, n_dp, rank, columns),
         "ring_o": RingScatter.scratch(n_seq, rank, width),
         "swap_q": Exchange.scratch(n_dp),
+        "swap_gu": Exchange.scratch(n_seq),
+        "got_gu": vm(LOW, *ins["fin"].shape),
     }
     return run(
-        functools.partial(back_kernel, n_dp, n_seq),
+        functools.partial(back_kernel, n_dp, n_seq, own_ff, ff),
         "attention_backward",
         3,
-        {key: (value, ANY if key in ("part_h", "part_y", "n1") else VMEM) for key, value in ins.items()},
+        {key: (value, ANY if key in ("part_y", "n1", "kv") else VMEM) for key, value in ins.items()},
         outs,
         scratch,
-    )
-
-
-def reduce_kernel(n_dp, n_seq, m):
-    at = Where(n_dp, n_seq)
-    greet(at.seq_ids() + at.dp_ids())
-    down = DpScatter(at, m.rows, *m.down)
-    side = DpScatter(at, m.cols, *m.side)
-    side.start()
-    down.start()
-    side.across()
-    down.across()
-    side.finish(m.fin)
-    n = m.got.shape[1]
-    copies = []
-    kept = pltpu.make_async_copy(m.fin.at[rows_of(at.seq, n)], m.got.at[at.seq], m.local.at[0])
-    kept.start()
-    for k, one in enumerate(at.seq_ids()):
-        src = m.fin.at[rows_of(one[1], n)]
-        copy = remote(src, m.got.at[at.seq], m.swap[0].at[k], m.swap[1].at[k], one)
-        copy.start()
-        copies.append(copy)
-    down.finish(m.total)
-    for copy in copies:
-        copy.wait()
-    kept.wait()
-
-
-def reduce(n_dp, n_seq, cols, rows):
-    _, deep, wide = cols.shape
-    return run(
-        functools.partial(reduce_kernel, n_dp, n_seq),
-        "reduce_feed_forward_grads",
-        4,
-        {"cols": (cols, VMEM), "rows": (rows, VMEM)},
-        {
-            "got": (shape_of((n_seq, deep // n_seq, wide), LOW), ANY),
-            "total": (shape_of(rows.shape[1:], FULL), VMEM),
-        },
-        {
-            "local": dma(1),
-            "side": DpScatter.scratch(n_dp, deep, wide),
-            "down": DpScatter.scratch(n_dp, *rows.shape[1:]),
-            "fin": vm(LOW, deep, wide),
-            "swap": Exchange.scratch(n_seq),
-        },
     )
 
 
@@ -1026,14 +1131,14 @@
     length = n_seq * local
     own_rows = w_query.shape[0]
     own_ff = w_down.shape[0]
-    part_ff = n_dp * own_ff
+    ff = -(-own_ff // 16) * 16
     heads = HEADS // n_dp
     q_width = heads * HEAD_DIM
     x_own = tokens.reshape(local, width)
     dy_own = cotangent.reshape(local, width)
 
     gain_one = gain_attn.astype(FULL)[:, None]
-    gain_two = gain_mlp.astype(FULL)[:, None]
+    gain_two = jnp.broadcast_to(gain_mlp.astype(FULL)[:, None], (own_rows, 2 * HEAD_DIM))
     kv_of = [i * heads // GROUP for i in range(n_dp)]
 
     def gained(weight):
@@ -1066,57 +1171,33 @@
         pack_q,
         w_gate,
         w_up,
-        jnp.broadcast_to(gain_two, (own_rows, pair)),
+        gain_two,
         w_output,
+        jnp.pad(w_down, ((0, ff - own_ff), (0, 0))),
     )
-    down_block = w_down if own_ff % 16 == 0 else w_down.reshape(16, own_ff * width // 16)
-    fed = feed(n_dp, n_seq, got["second"], dy_own, got["gu"], down_block)
-    second = fed["second_all"].reshape(length, width)
-    dy = fed["dy_all"].reshape(length, width)
-    weight_gu = fed["gu_all"].reshape(width, 2 * part_ff)
-    weight_d = fed["wd_all"].reshape(part_ff, width)
-
-    both = matmul(second, weight_gu)
-    gate, upward = both[:, :part_ff], both[:, part_ff:]
-    sigma = jax.nn.sigmoid(gate)
-    hidden = (gate * sigma * upward).astype(LOW)
-    part_y = matmul(hidden, weight_d).astype(LOW).reshape(n_seq, local, width)
-    grad_hidden = matmul_nt(dy, weight_d)
-    grad_gate = (grad_hidden * upward * sigma * (1.0 + gate * (1.0 - sigma))).astype(LOW)
-    grad_up = (grad_hidden * gate * sigma).astype(LOW)
-    grad_both = jnp.concatenate([grad_gate, grad_up], 1)
-    part_h = matmul_nt(grad_both, weight_gu).astype(LOW).reshape(n_seq, local, width)
-    grad_gu = matmul_tn(second, grad_both).astype(LOW)
-    grad_d = matmul_tn(hidden, dy).astype(LOW)
-
+    fed = feed(
+        n_dp,
+        n_seq,
+        got["second"],
+        dy_own,
+        got["gu"].reshape(n_seq * own_rows, 2 * n_dp * ff),
+        got["wd_all"],
+    )
     ins = {
-        "part_h": part_h,
-        "part_y": part_y,
+        "part_y": fed["part_y"],
+        "grad_h": fed["grad_h"],
+        "fin": fed["fin"].reshape(got["gu"].shape),
+        "wg": w_gate,
+        "wu": w_up,
+        "gain": gain_two,
         "x": x_own,
         "dy": dy_own,
         "middle": got["middle"],
     }
     for name in ("n1", "q", "kv", "o", "lse", "cos", "sin", "starts", "wq", "wo"):
         ins[name] = got[name + "_out"]
-    done = back(n_dp, n_seq, tokens.dtype, ins)
-    reduced = reduce(
-        n_dp,
-        n_seq,
-        grad_gu.reshape(n_dp, n_seq * own_rows, 2 * part_ff),
-        grad_d.reshape((n_dp,) + down_block.shape),
-    )
-    got_q, got_gu = done["got_q"], reduced["got"]
-
-    def ff_join(grads):
-        return (
-            grads.astype(FULL)
-            .reshape(n_seq, own_rows, n_dp, own_ff)
-            .transpose(1, 2, 0, 3)
-            .reshape(own_rows, n_dp * n_seq * own_ff)
-        )
-
-    raw_gate = ff_join(got_gu[:, :, :part_ff])
-    raw_up = ff_join(got_gu[:, :, part_ff:])
+    done = back(n_dp, n_seq, own_ff, ff, tokens.dtype, ins)
+    got_q = done["got_q"]
     raw_query = jnp.concatenate([got_q[i, :, :q_width] for i in range(n_dp)], 1).astype(FULL)
 
     def kv_join(first):
@@ -1143,10 +1224,10 @@
         gain_one * raw_key,
         gain_one * raw_value,
         done["grad_o"],
-        gain_grad((w_gate, raw_gate), (w_up, raw_up)),
-        gain_two * raw_gate,
-        gain_two * raw_up,
-        reduced["total"].reshape(own_ff, width),
+        done["grad_gain"][:, 0],
+        done["grad_g"],
+        done["grad_u"],
+        fed["grad_d"][:own_ff],
     )
 
 

time: 574 us -> 489 us (0.85)
  matrix products: 43.3 us -> 0 us
  Pallas kernels: 479 us -> 456 us
  local copies, waits for them, and re-layouts: 27.6 us -> 15.6 us
  other arithmetic: 13.6 us -> 6 us
    dot_general x6 -> x0, matrix products: 43.3 us -> none  [the longest x2 17.5 us: matmul(): return jnp.dot(left, right, preferred_element_type=FULL)]
    pallas_call x4 -> x3, Pallas kernels: 479 us -> 456 us  [run(): pl.pallas_call(lambda *refs: kernel(Refs(names, refs)), name=name, out_sh...]
    reshape x6 -> x0, local copies, waits for them, and re-layouts: 16.1 us -> none  [ff_join(): return grads.astype(FULL).reshape(n_seq, own_rows, n_dp, own_ff).transpos...]
where the time goes in v3:
time: 489 us; the launch traced here: 479 us
  Pallas kernels  456 us (93%)
  local copies, waits for them, and re-layouts  15.6 us (3%)
  other arithmetic  6 us (1%)
    pallas_call x3, Pallas kernels, run(): pl.pallas_call(lambda *refs: kernel(Refs(names, refs)), name=name, out_sh...  456 us

profile of v3, /device:TPU:0, one launch (start us, length us, event | category | flops | bytes accessed | tf_op | source)
XLA Modules:
  0.0 479.0 jit_solution(4280982656200493666)
XLA Ops:
  0.6 0.7 convert_element_type.130
  1.3 0.1 tile.10
  1.4 0.6 broadcast_in_dim.20.refs_3_
  2.0 1.3 broadcast_in_dim.21.refs_7_.refs_5_
  3.3 1.3 broadcast_in_dim.8.refs_1_
  4.6 1.4 broadcast_in_dim.9.refs_2_
  6.0 0.9 multiply_convert_fusion.11
  6.9 1.1 multiply_convert_fusion.3
  8.0 0.1 maximum_bitcast_fusion
  8.1 0.1 maximum_bitcast_fusion.2
  8.2 0.8 pad_maximum_fusion.refs_4_
  8.9 137.3 %attention_forward.1 = (bf16[4,128,2048]{2,1,0:T(8,128)(2,1)}, bf16[512,512]{1,0:T(8,128)(2,1)}, bf16[8,512,128]{2,1,0:T(8,128)(2,1)}, bf16[512,512]{1,0:T(8,128...) custom-call(bf16[128,2048]{1,0:T(8,128)(2,1)} %bitcast.39, ...), custom_call_target="tpu_custom_call" | custom-call | tf_op jit(solution)/shard_map/attention_forward/pallas_call | solution.py:446
  146.2 150.7 %feed_forward.1 = (bf16[8,128,2048]{2,1,0:T(8,128)(2,1)}, f32[128,2048]{1,0:T(8,128)}, bf16[512,1408]{1,0:T(8,128)(2,1)}, f32[176,2048]{1,0:T(8,128)}) custom-call(bf16[128,2048]{1,0:T(8,128)(2,1)} %get-tuple-element.36.refs_0_, bf16[128,2048]{1,0:T(8,128)(2,1)} %bitcast.41, bf16[512,1408]{1,0:T(8,128)(2,1)} %bitcast.43, ...), custom_call_target="tpu_custom_call" | custom-call | tf_op jit(solution)/shard_map/feed_forward/pallas_call | solution.py:446
  297.0 0.0 copy-start.7
  297.0 0.0 copy-start.8
  297.0 0.0 copy-start.3
  297.0 168.2 %attention_backward.1 = (bf16[128,2048]{1,0:T(8,128)(2,1)}, f32[128,2048]{1,0:T(8,128)}, f32[64,2048]{1,0:T(8,128)}, bf16[4,64,640]{2,1,0:T(8,128)(2,1)}, f32[64...) custom-call(bf16[8,128,2048]{2,1,0:T(8,128)(2,1)} %get-tuple-element.39.refs_0_, ...), custom_call_target="tpu_custom_call" | custom-call | tf_op jit(solution)/shard_map/attention_backward/pallas_call | solution.py:446
  465.3 1.4 slice_reduce_fusion
  466.7 0.9 slice_bitcast_fusion.11
  467.7 1.0 slice_bitcast_fusion.3
  468.7 0.9 convert_multiply_fusion.2
  469.6 1.0 convert_multiply_fusion
  470.6 0.5 add_add_fusion
  471.2 0.8 copy.29
  472.0 1.0 copy.30
  472.9 0.8 copy.31
  473.7 0.0 copy-done.2
  473.7 1.1 copy.32
  474.8 0.8 copy-done.1
  475.6 1.1 copy.33
  476.7 0.8 copy-done
  477.5 1.1 copy.34
  (14 shorter events, 0.0 us)
Async XLA Ops:
  297.0 171.7 %copy-start.7 = (bf16[64,256]{1,0:T(8,128)(2,1)S(1)}, bf16[64,256]{1,0:T(8,128)(2,1)}, u32[]{:S(2)}) copy-start(bf16[64,256]{1,0:T(8,128)(2,1)} %param.16) | copy-start | bytes 98308
  297.0 171.7 %copy-start.8 = (bf16[64,256]{1,0:T(8,128)(2,1)S(1)}, bf16[64,256]{1,0:T(8,128)(2,1)}, u32[]{:S(2)}) copy-start(bf16[64,256]{1,0:T(8,128)(2,1)} %param.17) | copy-start | bytes 98308
  297.0 172.6 %copy-start.3 = (bf16[64,2048]{1,0:T(8,128)(2,1)S(1)}, bf16[64,2048]{1,0:T(8,128)(2,1)}, u32[]{:S(2)}) copy-start(bf16[64,2048]{1,0:T(8,128)(2,1)} %param.15) | copy-start | bytes 786436
  465.3 5.9 %copy-start.6 = (bf16[128,2048]{1,0:T(8,128)(2,1)S(1)}, bf16[128,2048]{1,0:T(8,128)(2,1)}, u32[]{:S(2)}) copy-start(bf16[128,2048]{1,0:T(8,128)(2,1)} %get-tuple-element.53) | copy-start | bytes 1572868
  467.7 4.3 copy-start.4
  471.2 1.8 copy-start.5
  472.0 1.8 copy-start.2
  473.7 1.9 copy-start.1
  475.6 1.9 copy-start

commit v4 on v3

--- a/solution.py
+++ b/solution.py
@@ -198,11 +198,17 @@
                 elif t == self.steps and d == 0:
                     self.load(t, h, d).start()
 
+    def early(self):
+        for h, d in self.pieces():
+            if self.steps > 1 and not self.opposite(h, d):
+                block = self.parts.at[self.there(1, d), self.rows(h)]
+                self.go(block, self.slots.at[d, 1, self.rows(h)], d, 1, h)
+
     def step(self, t):
         if t == 0:
             self.load_all(1)
         for h, d in self.pieces():
-            if t == 0 and not self.opposite(h, d):
+            if (t == 0 and not self.opposite(h, d)) or (d, t, h) in self.copies:
                 continue
             rows = self.rows(h)
             src = self.parts.at[self.there(t, d), rows]
@@ -512,17 +518,13 @@
     return pl.ds(pl.multiple_of(r * count, count), count)
 
 
-def interleave(ring, jobs):
-    jobs = list(jobs)
-    for t in range(1, ring.steps):
-        if jobs:
-            jobs.pop(0)()
-        ring.step(t)
-    for job in jobs:
-        job()
-
-
-def front_kernel(n_dp, n_seq, own_ff, ff, m):
+def to_column(row):
+    n = row.shape[1]
+    here = lax.broadcasted_iota(jnp.int32, (n, n), 0) == lax.broadcasted_iota(jnp.int32, (n, n), 1)
+    return jnp.sum(jnp.where(here, row.astype(FULL), 0.0), 1, keepdims=True)
+
+
+def front_kernel(n_dp, n_seq, own_ff, ff, kv_of, m):
     at = Where(n_dp, n_seq)
     tok, width = m.x.shape
     q_width = m.q.shape[1]
@@ -540,6 +542,10 @@
     ring_kv = RingGather(at, m.kv_own, m.kv_all, *m.ring_kv_sem, m.local.at[7])
     swap_gu = seq_exchange(at, m.pgu, m.gu, *m.swap_gu_sem, m.local.at[8])
     down = DpGather(at, m.wd, m.wd_all, *m.down_sem, m.local.at[9])
+    loads = [
+        pltpu.make_async_copy(src, dst, m.load.at[k])
+        for k, (src, dst) in enumerate(((m.wg_in, m.wg), (m.wu_in, m.wu), (m.x, m.x_own)))
+    ]
     stores = []
 
     def store(src, dst):
@@ -547,12 +553,30 @@
         copy.start()
         stores.append(copy)
 
+    ring_o.step(0)
+    for copy in loads:
+        copy.start()
+
+    gain = to_column(m.gain_one[...])
+    for i, kv in enumerate(kv_of):
+        m.pq[i, :, :q_width] = (
+            gain * m.wq[:, i * q_width : (i + 1) * q_width].astype(FULL)
+        ).astype(LOW)
+        for weight, first in ((m.wk, q_width), (m.wv, q_width + HEAD_DIM)):
+            m.pq[i, :, first : first + HEAD_DIM] = (
+                gain * weight[:, kv * HEAD_DIM : (kv + 1) * HEAD_DIM].astype(FULL)
+            ).astype(LOW)
     swap_q.start()
     x_g.start()
+    ids = m.ids[...]
+    m.seg_rows[...] = jnp.broadcast_to(ids[None], m.seg_rows.shape)
+    m.seg_col[...] = jnp.broadcast_to(to_column(ids).astype(jnp.int32), m.seg_col.shape)
     row_x.start()
     col_g.start()
 
-    def pack(weight, first):
+    def pack(k, weight, first):
+        loads[k].wait()
+        scale = to_column(m.gain_two[...])
         if ff > own_ff:
             m.pgu[:, :, first : first + n_dp * ff] = jnp.zeros(
                 m.pgu.shape[:2] + (n_dp * ff,), LOW
@@ -561,12 +585,11 @@
             for i in range(n_dp):
                 piece = weight[:, (i * n_seq + s) * own_ff : (i * n_seq + s + 1) * own_ff]
                 m.pgu[s, :, first + i * ff : first + i * ff + own_ff] = (
-                    m.gain[:, :1] * piece.astype(FULL)
+                    scale * piece.astype(FULL)
                 ).astype(LOW)
 
     swap_q.arrived()
     ring_q.step(0)
-    down.start()
     row_x.arrived()
     row_g.start()
 
@@ -574,6 +597,7 @@
         x_g.hand()
         row_g.hand()
         col_g.hand()
+        down.start()
 
     def norm():
         x_g.arrived()
@@ -602,12 +626,18 @@
         store(m.sin, m.sin_out)
         store(m.starts, m.starts_out)
 
-    interleave(
-        ring_q,
-        [lambda: pack(m.wg, 0), hand, norm, place, lambda: pack(m.wu, n_dp * ff)],
-    )
+    pack(0, m.wg, 0)
+    ring_q.step(1)
+    hand()
+    jobs = [lambda: (norm(), place()), lambda: pack(1, m.wu, n_dp * ff)]
+    for t in range(2, ring_q.steps):
+        ring_q.step(t)
+        if jobs:
+            jobs.pop(0)()
+    for job in jobs:
+        job()
     ring_q.finish()
-    ring_o.step(0)
+    ring_o.step(1)
     store(m.wq_all, m.wq_out)
 
     m.qkv[...] = sum(
@@ -628,15 +658,14 @@
             m.kv_own[...] = jnp.where(low_head(pair.shape[0]), turned, pair).astype(LOW)
     ring_kv.step(0)
     store(m.q, m.q_out)
-    ring_o.step(1)
     for t in range(1, ring_kv.steps):
         ring_kv.step(t)
     down.hand()
     ring_kv.finish()
     store(m.kv_all, m.kv_out)
-    swap_gu.start()
-
     later = list(range(2, ring_o.steps))
+    ring_o.step(later.pop(0))
+    m.lse[...] = jnp.zeros_like(m.lse)
     for r in range(n_dp):
         rows = slice(r * tok, (r + 1) * tok)
         k, v = spread_kv(m.kv_all[:, rows].reshape(length, 2 * HEAD_DIM))
@@ -653,14 +682,19 @@
             total = jnp.sum(probs, -1, keepdims=True)
             probs = (probs * (1.0 / total)).astype(LOW)
             m.o[rows, cols] = join_heads(matmul(probs, m.v2[...])).astype(LOW)
-            m.lse[r * groups + g] = top + jnp.log(total)
+            here = lanes(2 * tok) == r * groups + g
+            m.lse[...] = jnp.where(here, top + jnp.log(total), m.lse[...])
             return carry
 
         lax.fori_loop(0, groups, group, 0)
-        if later:
+        if later and r % 2:
             ring_o.step(later.pop(0))
+            if not later:
+                swap_gu.start()
     for t in later:
         ring_o.step(t)
+    if later:
+        swap_gu.start()
     store(m.o, m.o_out)
     store(m.lse, m.lse_out)
     ring_o.finish()
@@ -672,7 +706,8 @@
     back.start()
     back.across()
     back.finish(m.middle)
-    middle = m.x[...].astype(FULL) + m.middle[...]
+    loads[2].wait()
+    middle = m.x_own[...].astype(FULL) + m.middle[...]
     m.middle[...] = middle
     scale = lax.rsqrt(jnp.mean(middle * middle, -1, keepdims=True) + EPS)
     m.second[...] = (middle * scale).astype(LOW)
@@ -684,27 +719,26 @@
         copy.wait()
 
 
-def front(n_dp, n_seq, own_ff, x, seg_rows, seg_col, freqs, pq, wg, wu, gain, wo, wd):
-    tok, width = x.shape
-    rank, columns = pq.shape[1:]
-    q_width = columns - 2 * HEAD_DIM
+def front(n_dp, n_seq, own_ff, kv_of, held, small):
+    tok, width = held["x"].shape
+    rank = small["wq"].shape[0]
+    q_width = width // n_dp
     groups = q_width // (2 * HEAD_DIM)
     pair = 2 * HEAD_DIM
+    columns = q_width + pair
     length = n_seq * tok
     every = n_dp * tok
+    wd = held["wd"]
     ff = wd.shape[0]
     gu_width = 2 * n_dp * ff
-    ins = {
-        "x": x, "seg_rows": seg_rows, "seg_col": seg_col, "freqs": freqs, "pq": pq, "wg": wg, "wu": wu, "gain": gain, "wo": wo,
-    }
-    ins = {key: (value, VMEM) for key, value in ins.items()}
-    ins["wd"] = (wd, ANY)
+    ins = {key: (value, ANY) for key, value in held.items()}
+    ins |= {key: (value, VMEM) for key, value in small.items()}
     kept = {
         "n1": (LOW, n_dp, tok, width),
         "q": (LOW, every, q_width),
         "kv_all": (LOW, n_seq, every, pair),
         "o": (LOW, every, q_width),
-        "lse": (FULL, n_dp * groups, 2 * tok, 1),
+        "lse": (FULL, 2 * tok, pair),
         "cos": (FULL, every, pair),
         "sin": (FULL, every, pair),
         "starts": (jnp.int32, every, pair),
@@ -721,6 +755,13 @@
     outs["second"] = (shape_of((tok, width), LOW), VMEM)
     scratch = {key: vm(*dims) for key, dims in kept.items()}
     scratch |= {
+        "load": dma(3),
+        "wg": vm(LOW, *held["wg_in"].shape),
+        "wu": vm(LOW, *held["wg_in"].shape),
+        "x_own": vm(LOW, tok, width),
+        "pq": vm(LOW, n_dp, rank, columns),
+        "seg_rows": vm(jnp.int32, n_seq, 8, tok),
+        "seg_col": vm(jnp.int32, tok, pair),
         "landed": vm(LOW, n_dp, rank, columns),
         "xs": vm(LOW, n_dp, tok, width),
         "seg_row": vm(jnp.int32, n_seq, 8, tok),
@@ -747,7 +788,7 @@
         "down_sem": DpGather.scratch(n_dp),
     }
     return run(
-        functools.partial(front_kernel, n_dp, n_seq, own_ff, ff), "attention_forward", 1, ins, outs, scratch
+        functools.partial(front_kernel, n_dp, n_seq, own_ff, ff, kv_of), "attention_forward", 1, ins, outs, scratch
     )
 
 
@@ -764,7 +805,6 @@
     ring_dy = RingGather(at, m.dy, m.dy_all, *m.ring_dy, m.local.at[2])
     ring_h = RingScatter(at, m.part, *m.ring_h)
     side = DpScatter(at, m.wgu, *m.side)
-    down = DpScatter(at, m.wd, *m.down)
     gu.start()
     held = pltpu.make_async_copy(m.wd_all, m.wd, m.local.at[3])
     held.start()
@@ -777,6 +817,10 @@
     gu.arrived()
     held.wait()
     stores = []
+
+    def stored():
+        while stores:
+            stores.pop().wait()
 
     def forward(c):
         blocks = slice(2 * c, 2 * c + 2)
@@ -811,11 +855,6 @@
                 m.part[b, :, cols] = out[k * tok : (k + 1) * tok]
 
     jobs = [functools.partial(forward, c) for c in range(n_seq // 2)]
-
-    def stored():
-        for copy in stores:
-            copy.wait()
-
     jobs.append(stored)
     jobs.append(lambda: backward([at.seq]))
     for t in range(1, ring_dy.steps):
@@ -830,12 +869,12 @@
     if ring_dy.steps > 1:
         ring_dy.rest(ring_dy.steps - 2)
         backward([at.ring(1 - ring_dy.steps), at.ring(ring_dy.steps - 1)])
+    ring_h.early()
     ring_dy.finish()
     backward([at.ring(ring_dy.steps)])
     gu.finish()
 
     ring_h.step(0)
-    grads = m.grads[...].reshape(length, wide)
 
     def grad_gu(k):
         chip = lax.rem(at.chip + 1 + k, at.chips)
@@ -854,13 +893,14 @@
                 .astype(LOW)
                 .reshape(m.wd.shape[:2] + (step,))
             )
-        down.start()
+        held = pltpu.make_async_copy(m.wd, m.grad_d, m.local.at[3])
+        held.start()
+        stores.append(held)
 
     jobs = [functools.partial(grad_gu, 0)]
     jobs += [functools.partial(grad_gu, k) for k in range(1, at.chips)]
     jobs.insert(max(len(jobs) - 1, 1), side.across)
     jobs.append(grad_down)
-    jobs.append(down.across)
     per = -(-len(jobs) // (ring_h.steps))
     for t in range(1, ring_h.steps):
         for _ in range(per):
@@ -871,7 +911,7 @@
         job()
     ring_h.finish(m.grad_h)
     side.finish(m.fin)
-    down.finish(m.grad_d)
+    stored()
 
 
 def feed(n_dp, n_seq, second, dy, gu, wd):
@@ -884,7 +924,7 @@
         "part_y": (shape_of((n_seq, tok, width), LOW), ANY),
         "grad_h": (shape_of((tok, width), FULL), VMEM),
         "fin": (shape_of((deep, wide), LOW), VMEM),
-        "grad_d": (shape_of((ff, width), FULL), VMEM),
+        "grad_d": (shape_of(wd.shape, LOW), ANY),
     }
     scratch = {
         "local": dma(4),
@@ -903,12 +943,11 @@
         "ring_dy": Ring.semaphores(n_seq),
         "ring_h": RingScatter.scratch(n_seq, tok, width),
         "side": DpScatter.scratch(n_dp, deep, wide),
-        "down": DpScatter.scratch(n_dp, ff, width),
     }
     return run(functools.partial(feed_kernel, n_dp, n_seq), "feed_forward", 2, ins, outs, scratch)
 
 
-def back_kernel(n_dp, n_seq, own_ff, ff, m):
+def back_kernel(n_dp, n_seq, own_ff, ff, kv_of, m):
     at = Where(n_dp, n_seq)
     tok, width = m.x.shape
     q_width = m.q.shape[1]
@@ -926,8 +965,23 @@
     ring_kv = RingScatter(at, m.part_kv, *m.ring_kv)
     ring_q = RingScatter(at, m.part_q, *m.ring_q)
     ring_o = RingScatter(at, m.part_o, *m.ring_o)
+    down = DpScatter(at, m.part_d, *m.down)
     back = DpScatter(at, m.d_all, *m.back)
     swap_q = dp_exchange(at, m.sum_q, m.got_q, *m.swap_q, m.local.at[1])
+    ring_y.step(0)
+    loads = [
+        pltpu.make_async_copy(getattr(m, key + "_in"), getattr(m, key), m.load.at[2 + k])
+        for k, key in enumerate(LOADED)
+    ]
+    for copy in loads:
+        copy.start()
+
+    def load_kv(r):
+        block = m.kv.at[:, pl.ds(r * tok, tok)]
+        return pltpu.make_async_copy(block, m.kv_row.at[r % 2], m.load.at[r % 2])
+
+    load_kv(0).start()
+
     def norm_back(grad, value):
         scale = lax.rsqrt(jnp.mean(value * value, -1, keepdims=True) + EPS)
         normed = value * scale
@@ -936,19 +990,20 @@
     m.dmid[...] = m.dy[...].astype(FULL) + norm_back(m.grad_h[...], m.middle[...])
     m.d_own[...] = m.dmid[...].astype(LOW)
     d_g.start()
-    ring_y.step(0)
+    if ring_y.steps > 1:
+        ring_y.step(1)
     d_g.hand()
+    for copy in loads:
+        copy.wait()
     d_g.arrived()
+    down.start()
     m.do[...] = matmul_nt(
         m.d_all[...].reshape(n_dp * tok, width), m.wo[...].reshape(q_width, width)
     ).astype(LOW)
-    later = list(range(1, ring_y.steps))
-
-    def load_kv(r):
-        block = m.kv.at[:, pl.ds(r * tok, tok)]
-        return pltpu.make_async_copy(block, m.kv_row.at[r % 2], m.load.at[r % 2])
-
-    load_kv(0).start()
+    later = list(range(2, ring_y.steps))
+    if later:
+        ring_y.step(later.pop(0))
+    down.across()
     for r in range(n_dp):
         rows = slice(r * tok, (r + 1) * tok)
         load_kv(r).wait()
@@ -967,7 +1022,9 @@
             do2 = split_heads(m.do[rows, cols])
             raw = matmul_nt(q2, m.k2[...])
             raw = raw + jnp.concatenate([m.mask[...]] * 2, 0)
-            probs = jnp.exp(raw - m.lse[r * groups + g])
+            here = lanes(2 * tok) == r * groups + g
+            lse = jnp.sum(jnp.where(here, m.lse[...], 0.0), 1, keepdims=True)
+            probs = jnp.exp(raw - lse)
             grad_probs = matmul_nt(do2, m.v2[...])
             delta = jnp.sum(probs * grad_probs, -1, keepdims=True)
             grad_raw = (probs * (grad_probs - delta)).astype(LOW)
@@ -983,7 +1040,7 @@
             low_head(length), dk + pltpu.roll(dk, HEAD_DIM, 1), dv + pltpu.roll(dv, HEAD_DIM, 1)
         )
         m.part_kv[:, rows] = dkv.astype(LOW).reshape(n_seq, tok, pair)
-        if later:
+        if later and r % 2:
             ring_y.step(later.pop(0))
     for t in later:
         ring_y.step(t)
@@ -997,14 +1054,14 @@
     for t in range(1, ring_kv.steps):
         ring_kv.step(t)
     ring_kv.finish(m.dkv)
-    ring_y.finish(m.wide)
-    for copy in swap_gu:
-        copy.start()
-    n1 = m.ring_y[0].at[0, pl.ds(0, n_dp)]
-    fetch = pltpu.make_async_copy(m.n1, n1, m.local.at[2])
-    fetch.start()
     ring_o.step(0)
-    m.out[...] = (m.middle[...] + m.wide[...]).astype(m.out.dtype)
+    waiting = list(swap_gu)
+
+    def pace(count=1):
+        for copy in waiting[:count]:
+            copy.start()
+        del waiting[:count]
+
     factor = HEAD_DIM ** (-0.5)
     for g in range(groups + 1):
         cols = slice(g * pair, (g + 1) * pair)
@@ -1020,40 +1077,70 @@
             matmul_nt(m.dqkv[...], weight).astype(LOW).reshape(n_dp, tok, rank)
         )
     back.start()
+    pace(2)
+    ring_y.finish(m.wide)
+    n1 = m.ring_y[0].at[0, pl.ds(0, n_dp)]
+    fetch = pltpu.make_async_copy(m.n1, n1, m.local.at[2])
+    fetch.start()
+    m.out[...] = (m.middle[...] + m.wide[...]).astype(m.out.dtype)
+    down.finish(m.grad_d)
+    back.across()
+    pace()
     fetch.wait()
     for i in range(n_dp):
         cols = slice(i * rank, (i + 1) * rank)
         m.part_q[:, i] = (
-            matmul_tn(n1[:, :, cols].reshape(n_dp * tok, rank), m.dqkv[...]).astype(LOW).reshape(n_seq, rank // n_seq, q_width + pair)
+            matmul_tn(n1[:, :, cols].reshape(n_dp * tok, rank), m.dqkv[...])
+            .astype(LOW)
+            .reshape(n_seq, rank // n_seq, q_width + pair)
         )
     ring_q.step(0)
-    back.across()
-    for t in range(1, ring_q.steps):
-        ring_q.step(t)
+    pace()
+    if ring_o.steps > 1:
+        ring_o.step(1)
+    pace()
+    back.finish(m.wide)
+    pace(len(waiting))
+    m.grad_x[...] = m.dmid[...] + norm_back(m.wide[...], m.x[...].astype(FULL))
+    for t in range(2, ring_o.steps):
         ring_o.step(t)
-    back.finish(m.wide)
-    m.grad_x[...] = m.dmid[...] + norm_back(m.wide[...], m.x[...].astype(FULL))
-    ring_q.finish(m.sum_q)
-    swap_q.start()
-    ring_o.finish(m.grad_o)
     for copy in swap_gu:
         copy.wait()
     m.got_gu[at.seq] = m.fin[at.seq]
-    gain = m.gain[:, :1]
-    gain_grad = jnp.zeros(gain.shape, FULL)
-    for weight, grad, first in ((m.wg, m.grad_g, 0), (m.wu, m.grad_u, n_dp * ff)):
+
+    def unpack(grad, first):
         for s in range(n_seq):
             for i in range(n_dp):
-                raw = m.got_gu[s, :, first + i * ff : first + i * ff + own_ff].astype(FULL)
-                cols = slice((i * n_seq + s) * own_ff, (i * n_seq + s + 1) * own_ff)
-                gain_grad += jnp.sum(weight[:, cols].astype(FULL) * raw, 1, keepdims=True)
-                grad[:, cols] = gain * raw
-    m.grad_gain[...] = jnp.broadcast_to(gain_grad, m.grad_gain.shape)
+                grad[:, (i * n_seq + s) * own_ff : (i * n_seq + s + 1) * own_ff] = m.got_gu[
+                    s, :, first + i * ff : first + i * ff + own_ff
+                ]
+
+    jobs = [lambda: unpack(m.grad_g, 0), lambda: unpack(m.grad_u, n_dp * ff)]
+    for t in range(1, ring_q.steps):
+        ring_q.step(t)
+        if jobs:
+            jobs.pop(0)()
+    for job in jobs:
+        job()
+    ring_o.finish(m.grad_o)
+    ring_q.finish(m.sum_q)
+    swap_q.start()
     swap_q.arrived()
+    m.grad_kv[...] = jnp.zeros_like(m.grad_kv)
+    for i, kv in enumerate(kv_of):
+        m.grad_q[:, i * q_width : (i + 1) * q_width] = m.got_q[i, :, :q_width]
+        for k in (0, 1):
+            first = q_width + k * HEAD_DIM
+            m.grad_kv[k, :, kv * HEAD_DIM : (kv + 1) * HEAD_DIM] += m.got_q[
+                i, :, first : first + HEAD_DIM
+            ].astype(FULL)
     swap_q.finish()
 
 
-def back(n_dp, n_seq, own_ff, ff, dtype, ins):
+LOADED = ("wo", "q", "o", "lse", "cos", "sin", "starts", "wq", "part_d")
+
+
+def back(n_dp, n_seq, own_ff, ff, kv_of, dtype, ins, shapes):
     tok, width = ins["x"].shape
     every = n_dp * tok
     q_width = ins["q"].shape[1]
@@ -1064,14 +1151,25 @@
         "out": (shape_of((tok, width), dtype), VMEM),
         "grad_x": (shape_of((tok, width), FULL), VMEM),
         "grad_o": (shape_of((rank, width), FULL), VMEM),
-        "got_q": (shape_of((n_dp, rank, columns), LOW), ANY),
-        "grad_g": (shape_of(ins["wg"].shape, FULL), VMEM),
-        "grad_u": (shape_of(ins["wg"].shape, FULL), VMEM),
-        "grad_gain": (shape_of((rank, pair), FULL), VMEM),
+        "grad_d": (shape_of((ff, width), FULL), VMEM),
+        "grad_q": (shape_of(shapes["q"], LOW), VMEM),
+        "grad_kv": (shape_of((2,) + shapes["k"], FULL), VMEM),
+        "grad_g": (shape_of(shapes["gate"], LOW), VMEM),
+        "grad_u": (shape_of(shapes["gate"], LOW), VMEM),
     }
-    scratch = {
+    placed = {
+        key + "_in" if key in LOADED else key: (
+            value,
+            ANY if key in LOADED + ("part_y", "n1", "kv") else VMEM,
+        )
+        for key, value in ins.items()
+    }
+    scratch = {key: pltpu.VMEM(ins[key].shape, ins[key].dtype) for key in LOADED}
+    scratch |= {
         "local": dma(3),
-        "load": dma(2),
+        "load": dma(2 + len(LOADED)),
+        "got_q": vm(LOW, n_dp, rank, columns),
+        "down": DpScatter.scratch(n_dp, ff, width),
         "kv_row": vm(LOW, 2, n_seq, tok, pair),
         "dmid": vm(FULL, tok, width),
         "d_own": vm(LOW, tok, width),
@@ -1102,10 +1200,10 @@
         "got_gu": vm(LOW, *ins["fin"].shape),
     }
     return run(
-        functools.partial(back_kernel, n_dp, n_seq, own_ff, ff),
+        functools.partial(back_kernel, n_dp, n_seq, own_ff, ff, kv_of),
         "attention_backward",
         3,
-        {key: (value, ANY if key in ("part_y", "n1", "kv") else VMEM) for key, value in ins.items()},
+        placed,
         outs,
         scratch,
     )
@@ -1137,43 +1235,29 @@
     x_own = tokens.reshape(local, width)
     dy_own = cotangent.reshape(local, width)
 
-    gain_one = gain_attn.astype(FULL)[:, None]
-    gain_two = jnp.broadcast_to(gain_mlp.astype(FULL)[:, None], (own_rows, 2 * HEAD_DIM))
     kv_of = [i * heads // GROUP for i in range(n_dp)]
-
-    def gained(weight):
-        return (gain_one * weight.astype(FULL)).astype(LOW)
-
-    pack_q = jnp.stack(
-        [
-            jnp.concatenate(
-                [
-                    gained(w_query[:, i * q_width : (i + 1) * q_width]),
-                    gained(w_key[:, kv * HEAD_DIM : (kv + 1) * HEAD_DIM]),
-                    gained(w_value[:, kv * HEAD_DIM : (kv + 1) * HEAD_DIM]),
-                ],
-                1,
-            )
-            for i, kv in enumerate(kv_of)
-        ]
-    )
     freqs = ROPE_BASE ** (-jnp.arange(0, HEAD_DIM, 2).astype(FULL) / HEAD_DIM)
-    ids = segment_ids.reshape(local)
-    pair = 2 * HEAD_DIM
     got = front(
         n_dp,
         n_seq,
         own_ff,
-        x_own,
-        jnp.broadcast_to(ids, (n_seq, 8, local)),
-        jnp.broadcast_to(ids[:, None], (local, pair)),
-        jnp.broadcast_to(jnp.tile(freqs, 4), (8, pair)),
-        pack_q,
-        w_gate,
-        w_up,
-        gain_two,
-        w_output,
-        jnp.pad(w_down, ((0, ff - own_ff), (0, 0))),
+        kv_of,
+        {
+            "x": x_own,
+            "wg_in": w_gate,
+            "wu_in": w_up,
+            "wo": w_output,
+            "wd": jnp.pad(w_down, ((0, ff - own_ff), (0, 0))),
+        },
+        {
+            "wq": w_query,
+            "wk": w_key,
+            "wv": w_value,
+            "gain_one": gain_attn.reshape(1, own_rows),
+            "gain_two": gain_mlp.reshape(1, own_rows),
+            "ids": segment_ids.reshape(1, local),
+            "freqs": jnp.broadcast_to(jnp.tile(freqs, 4), (8, 2 * HEAD_DIM)),
+        },
     )
     fed = feed(
         n_dp,
@@ -1187,31 +1271,29 @@
         "part_y": fed["part_y"],
         "grad_h": fed["grad_h"],
         "fin": fed["fin"].reshape(got["gu"].shape),
-        "wg": w_gate,
-        "wu": w_up,
-        "gain": gain_two,
+        "part_d": fed["grad_d"],
         "x": x_own,
         "dy": dy_own,
         "middle": got["middle"],
     }
     for name in ("n1", "q", "kv", "o", "lse", "cos", "sin", "starts", "wq", "wo"):
         ins[name] = got[name + "_out"]
-    done = back(n_dp, n_seq, own_ff, ff, tokens.dtype, ins)
-    got_q = done["got_q"]
-    raw_query = jnp.concatenate([got_q[i, :, :q_width] for i in range(n_dp)], 1).astype(FULL)
-
-    def kv_join(first):
-        terms = [got_q[i, :, first : first + HEAD_DIM].astype(FULL) for i in range(n_dp)]
-        return jnp.concatenate(
-            [
-                sum(term for term, kv in zip(terms, kv_of) if kv == head)
-                for head in range(KV_HEADS)
-            ],
-            1,
-        )
-
-    raw_key = kv_join(q_width)
-    raw_value = kv_join(q_width + HEAD_DIM)
+    done = back(
+        n_dp,
+        n_seq,
+        own_ff,
+        ff,
+        kv_of,
+        tokens.dtype,
+        ins,
+        {"q": w_query.shape, "k": w_key.shape, "gate": w_gate.shape},
+    )
+    raw_query = done["grad_q"].astype(FULL)
+    raw_key, raw_value = done["grad_kv"]
+    raw_gate = done["grad_g"].astype(FULL)
+    raw_up = done["grad_u"].astype(FULL)
+    gain_one = gain_attn.astype(FULL)[:, None]
+    gain_two = gain_mlp.astype(FULL)[:, None]
 
     def gain_grad(*pairs):
         return sum(jnp.sum(weight.astype(FULL) * raw, 1) for weight, raw in pairs)
@@ -1224,10 +1306,10 @@
         gain_one * raw_key,
         gain_one * raw_value,
         done["grad_o"],
-        done["grad_gain"][:, 0],
-        done["grad_g"],
-        done["grad_u"],
-        fed["grad_d"][:own_ff],
+        gain_grad((w_gate, raw_gate), (w_up, raw_up)),
+        gain_two * raw_gate,
+        gain_two * raw_up,
+        done["grad_d"][:own_ff],
     )
 
 

time: 489 us -> 407 us (0.83)
  Pallas kernels: 456 us -> 387 us
  local copies, waits for them, and re-layouts: 15.6 us -> 4.42 us
    pallas_call x3, Pallas kernels: 456 us -> 387 us  [run(): pl.pallas_call(lambda *refs: kernel(Refs(names, refs)), name=name, out_sh...]
where the time goes in v4:
time: 407 us; the launch traced here: 399 us
  Pallas kernels  387 us (95%)
  other arithmetic  6.48 us (2%)
  local copies, waits for them, and re-layouts  4.42 us (1%)
    pallas_call x3, Pallas kernels, run(): pl.pallas_call(lambda *refs: kernel(Refs(names, refs)), name=name, out_sh...  387 us

profile of v4, /device:TPU:0, one launch (start us, length us, event | category | flops | bytes accessed | tf_op | source)
XLA Modules:
  0.0 398.8 jit_solution(7160389637347266230)
XLA Ops:
  0.7 0.1 tile.10
  0.7 0.6 broadcast_in_dim.2.refs_11_
  1.3 97.7 %attention_forward.1 = (bf16[4,128,2048]{2,1,0:T(8,128)(2,1)}, bf16[512,512]{1,0:T(8,128)(2,1)}, bf16[8,512,128]{2,1,0:T(8,128)(2,1)}, bf16[512,512]{1,0:T(8,128...) custom-call(bf16[128,2048]{1,0:T(8,128)(2,1)} %bitcast.18, ...), custom_call_target="tpu_custom_call" | custom-call | tf_op jit(solution)/shard_map/attention_forward/pallas_call | solution.py:452
  99.1 141.6 %feed_forward.1 = (bf16[8,128,2048]{2,1,0:T(8,128)(2,1)}, f32[128,2048]{1,0:T(8,128)}, bf16[512,1408]{1,0:T(8,128)(2,1)}, bf16[4,176,2048]{2,1,0:T(8,128)(2,1)}) custom-call(bf16[128,2048]{1,0:T(8,128)(2,1)} %get-tuple-element.37.refs_0_, bf16[128,2048]{1,0:T(8,128)(2,1)} %bitcast.20, bf16[512,1408]{1,0:T(8,128)(2,1)} %bitcast.22, ...), custom_call_target="tpu_custom_call" | custom-call | tf_op jit(solution)/shard_map/feed_forward/pallas_call | solution.py:452
  240.6 0.0 copy-start.11
  240.6 0.0 copy-start
  240.7 0.0 copy-start.1
  240.7 147.3 %attention_backward.1 = (bf16[128,2048]{1,0:T(8,128)(2,1)}, f32[128,2048]{1,0:T(8,128)}, f32[64,2048]{1,0:T(8,128)}, f32[176,2048]{1,0:T(8,128)}, bf16[64,2048]{...) custom-call(bf16[8,128,2048]{2,1,0:T(8,128)(2,1)} %get-tuple-element.40.refs_0_, ...), custom_call_target="tpu_custom_call" | custom-call | tf_op jit(solution)/shard_map/attention_backward/pallas_call | solution.py:452
  388.0 0.0 copy-done.11
  388.0 0.0 copy-done
  388.0 0.0 copy-done.1
  388.0 0.0 copy-start.12
  388.1 0.0 copy-start.3
  388.1 0.0 copy-start.7
  388.1 0.0 copy-start.8
  388.1 0.0 copy-start.9
  388.1 0.0 copy-start.10
  388.1 3.6 convert_multiply_fusion
  391.7 0.5 add.11
  392.2 0.0 copy-done.12
  392.2 0.0 copy-done.7
  392.3 1.0 convert_multiply_fusion.4
  393.3 0.8 bitcast_multiply_fusion
  394.1 0.5 add_add_fusion
  394.7 0.0 copy-done.6
  394.7 0.8 copy.27
  395.5 0.0 copy-done.4
  395.5 1.0 copy.28
  396.4 0.0 copy-done.5
  396.4 0.8 copy.29
  397.2 0.0 copy-done.2
  397.2 1.1 copy.30
  (12 shorter events, 0.0 us)
Async XLA Ops:
  240.6 147.4 %copy-start.11 = (bf16[64]{0:T(256)(128)(2,1)S(1)}, bf16[64]{0:T(256)(128)(2,1)}, u32[]{:S(2)}) copy-start(bf16[64]{0:T(256)(128)(2,1)} %param.19) | copy-start | bytes 388
  240.6 147.4 %copy-start = (bf16[64,5632]{1,0:T(8,128)(2,1)S(1)}, bf16[64,5632]{1,0:T(8,128)(2,1)}, u32[]{:S(2)}) copy-start(bf16[64,5632]{1,0:T(8,128)(2,1)} %refs_1_.1) | copy-start | bytes 2162692
  240.7 147.4 %copy-start.1 = (bf16[64,5632]{1,0:T(8,128)(2,1)S(1)}, bf16[64,5632]{1,0:T(8,128)(2,1)}, u32[]{:S(2)}) copy-start(bf16[64,5632]{1,0:T(8,128)(2,1)} %refs_2_.1) | copy-start | bytes 2162692
  388.0 4.2 %copy-start.12 = (bf16[64]{0:T(256)(128)(2,1)S(1)}, bf16[64]{0:T(256)(128)(2,1)}, u32[]{:S(2)}) copy-start(bf16[64]{0:T(256)(128)(2,1)} %param.14) | copy-start | bytes 388
  388.1 4.2 %copy-start.3 = (bf16[64,2048]{1,0:T(8,128)(2,1)S(1)}, bf16[64,2048]{1,0:T(8,128)(2,1)}, u32[]{:S(2)}) copy-start(bf16[64,2048]{1,0:T(8,128)(2,1)} %refs_5_.1) | copy-start | bytes 786436
  388.1 4.2 %copy-start.7 = (bf16[64,2048]{1,0:T(8,128)(2,1)S(1)}, bf16[64,2048]{1,0:T(8,128)(2,1)}, u32[]{:S(2)}) copy-start(bf16[64,2048]{1,0:T(8,128)(2,1)} %get-tuple-element.57) | copy-start | bytes 786436
  388.1 5.2 %copy-start.8 = (bf16[64,256]{1,0:T(8,128)(2,1)S(1)}, bf16[64,256]{1,0:T(8,128)(2,1)}, u32[]{:S(2)}) copy-start(bf16[64,256]{1,0:T(8,128)(2,1)} %refs_6_.1) | copy-start | bytes 98308
  388.1 5.2 %copy-start.9 = (bf16[64,256]{1,0:T(8,128)(2,1)S(1)}, bf16[64,256]{1,0:T(8,128)(2,1)}, u32[]{:S(2)}) copy-start(bf16[64,256]{1,0:T(8,128)(2,1)} %refs_7_.1) | copy-start | bytes 98308
  388.1 5.2 %copy-start.10 = (f32[2,64,256]{2,1,0:T(8,128)S(1)}, f32[2,64,256]{2,1,0:T(8,128)}, u32[]{:S(2)}) copy-start(f32[2,64,256]{2,1,0:T(8,128)} %get-tuple-element.58) | copy-start | bytes 393220
  388.1 6.5 %copy-start.6 = (bf16[128,2048]{1,0:T(8,128)(2,1)S(1)}, bf16[128,2048]{1,0:T(8,128)(2,1)}, u32[]{:S(2)}) copy-start(bf16[128,2048]{1,0:T(8,128)(2,1)} %get-tuple-element.55) | copy-start | bytes 1572868
  391.7 3.7 copy-start.4
  394.7 1.8 copy-start.5
  395.5 1.8 copy-start.2

commit v5 on v4

--- a/solution.py
+++ b/solution.py
@@ -167,8 +167,10 @@
 
 
 class RingScatter(Ring):
-    def __init__(self, at, parts, slots, send, recv, staged=None, loads=None):
-        super().__init__(at, parts.shape[1:], send, recv)
+    def __init__(self, at, parts, slots, send, recv, staged=None, loads=None, axis=0):
+        shape = parts.shape[1:] if axis == 0 else parts.shape[:1] + parts.shape[2:]
+        super().__init__(at, shape, send, recv)
+        self.axis = axis
         self.parts, self.slots, self.staged, self.loads = parts, slots, staged, loads
 
     @staticmethod
@@ -182,13 +184,17 @@
     def there(self, t, d):
         return self.at.ring(self.steps - t if d == 0 else t - self.steps)
 
+    def block(self, index, h):
+        if self.axis:
+            return self.parts.at[self.rows(h), index]
+        return self.parts.at[index, self.rows(h)]
+
     def adds(self, t, h, d):
         return t > 1 or (t == 1 and self.opposite(h, d))
 
     def load(self, t, h, d):
         rows = self.rows(h)
-        block = self.parts.at[self.there(t, d), rows]
-        return pltpu.make_async_copy(block, self.staged.at[d, rows], self.loads.at[d, h])
+        return pltpu.make_async_copy(self.block(self.there(t, d), h), self.staged.at[d, rows], self.loads.at[d, h])
 
     def load_all(self, t):
         if self.staged is not None:
@@ -201,8 +207,7 @@
     def early(self):
         for h, d in self.pieces():
             if self.steps > 1 and not self.opposite(h, d):
-                block = self.parts.at[self.there(1, d), self.rows(h)]
-                self.go(block, self.slots.at[d, 1, self.rows(h)], d, 1, h)
+                self.go(self.block(self.there(1, d), h), self.slots.at[d, 1, self.rows(h)], d, 1, h)
 
     def step(self, t):
         if t == 0:
@@ -211,7 +216,7 @@
             if (t == 0 and not self.opposite(h, d)) or (d, t, h) in self.copies:
                 continue
             rows = self.rows(h)
-            src = self.parts.at[self.there(t, d), rows]
+            src = self.block(self.there(t, d), h)
             if self.adds(t, h, d):
                 if self.staged is not None:
                     self.load(t, h, d).wait()
@@ -231,7 +236,7 @@
         for h in range(self.halves):
             rows = self.rows(h)
             if self.staged is None:
-                total = self.parts[self.at.seq, rows].astype(FULL)
+                total = self.block(self.at.seq, h)[...].astype(FULL)
             else:
                 self.load(self.steps, h, 0).wait()
                 total = self.staged[0, rows].astype(FULL)
@@ -247,6 +252,7 @@
 
 class Exchange:
     def __init__(self, me, ids, axis, packed, landing, send, recv, local):
+        self.started = 0
         self.kept = pltpu.make_async_copy(packed.at[me], landing.at[me], local)
         self.copies = [
             remote(packed.at[one[axis]], landing.at[me], send.at[k], recv.at[k], one)
@@ -257,10 +263,14 @@
     def scratch(n):
         return [pltpu.SemaphoreType.DMA((n - 1,)), pltpu.SemaphoreType.DMA((n - 1,))]
 
-    def start(self):
-        self.kept.start()
-        for copy in self.copies:
+    def start(self, count=None):
+        if not self.started:
+            self.kept.start()
+        first = self.started - 1 if self.started else 0
+        last = len(self.copies) if count is None else min(first + count, len(self.copies))
+        for copy in self.copies[first:last]:
             copy.start()
+        self.started = last + 1
 
     def arrived(self):
         self.kept.wait()
@@ -418,6 +428,8 @@
 
 
 def comm_params(number):
+    if number is None:
+        return pltpu.CompilerParams(vmem_limit_bytes=VMEM_BYTES)
     return pltpu.CompilerParams(
         collective_id=number, has_side_effects=True, vmem_limit_bytes=VMEM_BYTES
     )
@@ -522,6 +534,12 @@
     n = row.shape[1]
     here = lax.broadcasted_iota(jnp.int32, (n, n), 0) == lax.broadcasted_iota(jnp.int32, (n, n), 1)
     return jnp.sum(jnp.where(here, row.astype(FULL), 0.0), 1, keepdims=True)
+
+
+def to_row(column):
+    n = column.shape[0]
+    here = lax.broadcasted_iota(jnp.int32, (n, n), 0) == lax.broadcasted_iota(jnp.int32, (n, n), 1)
+    return jnp.sum(jnp.where(here, column, 0.0), 0, keepdims=True)
 
 
 def front_kernel(n_dp, n_seq, own_ff, ff, kv_of, m):
@@ -588,6 +606,8 @@
                     scale * piece.astype(FULL)
                 ).astype(LOW)
 
+    later = list(range(1, ring_o.steps))
+    ring_o.step(later.pop(0))
     swap_q.arrived()
     ring_q.step(0)
     row_x.arrived()
@@ -628,8 +648,7 @@
 
     pack(0, m.wg, 0)
     ring_q.step(1)
-    hand()
-    jobs = [lambda: (norm(), place()), lambda: pack(1, m.wu, n_dp * ff)]
+    jobs = [lambda: (hand(), norm(), place()), lambda: pack(1, m.wu, n_dp * ff)]
     for t in range(2, ring_q.steps):
         ring_q.step(t)
         if jobs:
@@ -637,7 +656,8 @@
     for job in jobs:
         job()
     ring_q.finish()
-    ring_o.step(1)
+    if later:
+        ring_o.step(later.pop(0))
     store(m.wq_all, m.wq_out)
 
     m.qkv[...] = sum(
@@ -660,11 +680,13 @@
     store(m.q, m.q_out)
     for t in range(1, ring_kv.steps):
         ring_kv.step(t)
+        if later and t > 1:
+            ring_o.step(later.pop(0))
+    for t in later:
+        ring_o.step(t)
     down.hand()
     ring_kv.finish()
     store(m.kv_all, m.kv_out)
-    later = list(range(2, ring_o.steps))
-    ring_o.step(later.pop(0))
     m.lse[...] = jnp.zeros_like(m.lse)
     for r in range(n_dp):
         rows = slice(r * tok, (r + 1) * tok)
@@ -687,14 +709,8 @@
             return carry
 
         lax.fori_loop(0, groups, group, 0)
-        if later and r % 2:
-            ring_o.step(later.pop(0))
-            if not later:
-                swap_gu.start()
-    for t in later:
-        ring_o.step(t)
-    if later:
-        swap_gu.start()
+        if r == 0:
+            swap_gu.start()
     store(m.o, m.o_out)
     store(m.lse, m.lse_out)
     ring_o.finish()
@@ -733,18 +749,18 @@
     gu_width = 2 * n_dp * ff
     ins = {key: (value, ANY) for key, value in held.items()}
     ins |= {key: (value, VMEM) for key, value in small.items()}
-    kept = {
-        "n1": (LOW, n_dp, tok, width),
-        "q": (LOW, every, q_width),
-        "kv_all": (LOW, n_seq, every, pair),
-        "o": (LOW, every, q_width),
-        "lse": (FULL, 2 * tok, pair),
-        "cos": (FULL, every, pair),
-        "sin": (FULL, every, pair),
-        "starts": (jnp.int32, every, pair),
-        "wq_all": (LOW, n_seq, n_dp, rank, columns),
-        "wo_all": (LOW, n_seq, rank, width),
-    }
+    kept = dict(
+        n1=(LOW, n_dp, tok, width),
+        q=(LOW, every, q_width),
+        kv_all=(LOW, n_seq, every, pair),
+        o=(LOW, every, q_width),
+        lse=(FULL, 2 * tok, pair),
+        cos=(FULL, every, pair),
+        sin=(FULL, every, pair),
+        starts=(jnp.int32, every, pair),
+        wq_all=(LOW, n_seq, n_dp, rank, columns),
+        wo_all=(LOW, n_seq, rank, width),
+    )
     outs = {
         key.replace("_all", "") + "_out": (shape_of(dims[1:], dims[0]), ANY)
         for key, dims in kept.items()
@@ -754,39 +770,39 @@
     outs["middle"] = (shape_of((tok, width), FULL), VMEM)
     outs["second"] = (shape_of((tok, width), LOW), VMEM)
     scratch = {key: vm(*dims) for key, dims in kept.items()}
-    scratch |= {
-        "load": dma(3),
-        "wg": vm(LOW, *held["wg_in"].shape),
-        "wu": vm(LOW, *held["wg_in"].shape),
-        "x_own": vm(LOW, tok, width),
-        "pq": vm(LOW, n_dp, rank, columns),
-        "seg_rows": vm(jnp.int32, n_seq, 8, tok),
-        "seg_col": vm(jnp.int32, tok, pair),
-        "landed": vm(LOW, n_dp, rank, columns),
-        "xs": vm(LOW, n_dp, tok, width),
-        "seg_row": vm(jnp.int32, n_seq, 8, tok),
-        "segs": vm(jnp.int32, n_dp, n_seq, 8, tok),
-        "seg_cols": vm(jnp.int32, n_dp, tok, pair),
-        "kv_own": vm(LOW, every, pair),
-        "mask": vm(FULL, tok, length),
-        "pgu": vm(LOW, n_seq, rank, gu_width),
-        "qkv": vm(FULL, every, columns),
-        "k2": vm(LOW, length, pair),
-        "v2": vm(LOW, length, pair),
-        "parts": vm(LOW, n_dp, tok, width),
-        "back": DpScatter.scratch(n_dp, tok, width),
-        "local": dma(10 + len(kept)),
-        "swap_q_sem": Exchange.scratch(n_dp),
-        "x_sem": DpGather.scratch(n_dp),
-        "row_x_sem": Exchange.scratch(n_seq),
-        "row_g_sem": DpGather.scratch(n_dp),
-        "col_g_sem": DpGather.scratch(n_dp),
-        "ring_q_sem": Ring.semaphores(n_seq),
-        "ring_o_sem": Ring.semaphores(n_seq),
-        "ring_kv_sem": Ring.semaphores(n_seq),
-        "swap_gu_sem": Exchange.scratch(n_seq),
-        "down_sem": DpGather.scratch(n_dp),
-    }
+    scratch |= dict(
+        load=dma(3),
+        wg=vm(LOW, *held["wg_in"].shape),
+        wu=vm(LOW, *held["wg_in"].shape),
+        x_own=vm(LOW, tok, width),
+        pq=vm(LOW, n_dp, rank, columns),
+        seg_rows=vm(jnp.int32, n_seq, 8, tok),
+        seg_col=vm(jnp.int32, tok, pair),
+        landed=vm(LOW, n_dp, rank, columns),
+        xs=vm(LOW, n_dp, tok, width),
+        seg_row=vm(jnp.int32, n_seq, 8, tok),
+        segs=vm(jnp.int32, n_dp, n_seq, 8, tok),
+        seg_cols=vm(jnp.int32, n_dp, tok, pair),
+        kv_own=vm(LOW, every, pair),
+        mask=vm(FULL, tok, length),
+        pgu=vm(LOW, n_seq, rank, gu_width),
+        qkv=vm(FULL, every, columns),
+        k2=vm(LOW, length, pair),
+        v2=vm(LOW, length, pair),
+        parts=vm(LOW, n_dp, tok, width),
+        back=DpScatter.scratch(n_dp, tok, width),
+        local=dma(10 + len(kept)),
+        swap_q_sem=Exchange.scratch(n_dp),
+        x_sem=DpGather.scratch(n_dp),
+        row_x_sem=Exchange.scratch(n_seq),
+        row_g_sem=DpGather.scratch(n_dp),
+        col_g_sem=DpGather.scratch(n_dp),
+        ring_q_sem=Ring.semaphores(n_seq),
+        ring_o_sem=Ring.semaphores(n_seq),
+        ring_kv_sem=Ring.semaphores(n_seq),
+        swap_gu_sem=Exchange.scratch(n_seq),
+        down_sem=DpGather.scratch(n_dp),
+    )
     return run(
         functools.partial(front_kernel, n_dp, n_seq, own_ff, ff, kv_of), "attention_forward", 1, ins, outs, scratch
     )
@@ -818,6 +834,11 @@
     held.wait()
     stores = []
 
+    def store(src, dst, k):
+        copy = pltpu.make_async_copy(src, dst, m.local.at[k])
+        copy.start()
+        stores.append(copy)
+
     def stored():
         while stores:
             stores.pop().wait()
@@ -858,7 +879,7 @@
     jobs.append(stored)
     jobs.append(lambda: backward([at.seq]))
     for t in range(1, ring_dy.steps):
-        for _ in range(2):
+        for _ in range(3 if t == 1 else 4):
             if jobs:
                 jobs.pop(0)()
         ring_dy.step(t)
@@ -878,10 +899,11 @@
 
     def grad_gu(k):
         chip = lax.rem(at.chip + 1 + k, at.chips)
-        for c in (0, 1):
+        for c in (1 - at.core, at.core):
             normed = m.second_all[:, :, rows_of(2 * chip + c, rank)].reshape(length, rank)
             m.wgu[2 * chip + c] = matmul_tn(normed, m.grads[...].reshape(length, wide)).astype(LOW)
-        side.to_core(chip).start()
+            if c is not at.core:
+                side.to_core(chip).start()
 
     def grad_down():
         step = width // n_dp
@@ -893,24 +915,21 @@
                 .astype(LOW)
                 .reshape(m.wd.shape[:2] + (step,))
             )
-        held = pltpu.make_async_copy(m.wd, m.grad_d, m.local.at[3])
-        held.start()
-        stores.append(held)
-
-    jobs = [functools.partial(grad_gu, 0)]
-    jobs += [functools.partial(grad_gu, k) for k in range(1, at.chips)]
-    jobs.insert(max(len(jobs) - 1, 1), side.across)
-    jobs.append(grad_down)
-    per = -(-len(jobs) // (ring_h.steps))
+        store(m.wd, m.grad_d, 3)
+
+    jobs = [functools.partial(grad_gu, k) for k in range(at.chips)]
+    jobs += [side.across, grad_down]
     for t in range(1, ring_h.steps):
-        for _ in range(per):
+        for _ in range(2):
             if jobs:
                 jobs.pop(0)()
         ring_h.step(t)
     for job in jobs:
         job()
     ring_h.finish(m.grad_h)
+    store(m.grad_h, m.grad_h_to, 4)
     side.finish(m.fin)
+    store(m.fin, m.fin_to, 5)
     stored()
 
 
@@ -919,31 +938,33 @@
     deep, wide = gu.shape
     ff = wd.shape[1]
     part = wide // 2
-    ins = {"second": (second, ANY), "dy": (dy, ANY), "gu": (gu, ANY), "wd_all": (wd, ANY)}
-    outs = {
-        "part_y": (shape_of((n_seq, tok, width), LOW), ANY),
-        "grad_h": (shape_of((tok, width), FULL), VMEM),
-        "fin": (shape_of((deep, wide), LOW), VMEM),
-        "grad_d": (shape_of(wd.shape, LOW), ANY),
-    }
-    scratch = {
-        "local": dma(4),
-        "wd": vm(LOW, *wd.shape),
-        "store": dma(n_seq // 2),
-        "second_all": vm(LOW, n_seq, tok, width),
-        "dy_all": vm(LOW, n_seq, tok, width),
-        "wgu": vm(LOW, n_dp, deep, wide),
-        "by_gate": vm(FULL, n_seq, tok, part),
-        "by_up": vm(FULL, n_seq, tok, part),
-        "hidden": vm(LOW, n_seq, tok, part),
-        "grads": vm(LOW, n_seq, tok, wide),
-        "part": vm(LOW, n_seq, tok, width),
-        "gu_sem": DpGather.scratch(n_dp),
-        "ring_n": Ring.semaphores(n_seq),
-        "ring_dy": Ring.semaphores(n_seq),
-        "ring_h": RingScatter.scratch(n_seq, tok, width),
-        "side": DpScatter.scratch(n_dp, deep, wide),
-    }
+    ins = dict(second=(second, ANY), dy=(dy, ANY), gu=(gu, ANY), wd_all=(wd, ANY))
+    outs = dict(
+        part_y=(shape_of((n_seq, tok, width), LOW), ANY),
+        grad_h_to=(shape_of((tok, width), FULL), ANY),
+        fin_to=(shape_of((deep, wide), LOW), ANY),
+        grad_d=(shape_of(wd.shape, LOW), ANY),
+    )
+    scratch = dict(
+        local=dma(6),
+        grad_h=vm(FULL, tok, width),
+        fin=vm(LOW, deep, wide),
+        wd=vm(LOW, *wd.shape),
+        store=dma(n_seq // 2),
+        second_all=vm(LOW, n_seq, tok, width),
+        dy_all=vm(LOW, n_seq, tok, width),
+        wgu=vm(LOW, n_dp, deep, wide),
+        by_gate=vm(FULL, n_seq, tok, part),
+        by_up=vm(FULL, n_seq, tok, part),
+        hidden=vm(LOW, n_seq, tok, part),
+        grads=vm(LOW, n_seq, tok, wide),
+        part=vm(LOW, n_seq, tok, width),
+        gu_sem=DpGather.scratch(n_dp),
+        ring_n=Ring.semaphores(n_seq),
+        ring_dy=Ring.semaphores(n_seq),
+        ring_h=RingScatter.scratch(n_seq, tok, width),
+        side=DpScatter.scratch(n_dp, deep, wide),
+    )
     return run(functools.partial(feed_kernel, n_dp, n_seq), "feed_forward", 2, ins, outs, scratch)
 
 
@@ -963,12 +984,29 @@
     ring_y = RingScatter(at, m.part_y, *m.ring_y, *m.staged)
     d_g = DpGather(at, m.d_own, m.d_all, *m.d_sem, m.local.at[0])
     ring_kv = RingScatter(at, m.part_kv, *m.ring_kv)
-    ring_q = RingScatter(at, m.part_q, *m.ring_q)
+    ring_q = RingScatter(at, m.landed_q, *m.ring_q, axis=1)
     ring_o = RingScatter(at, m.part_o, *m.ring_o)
     down = DpScatter(at, m.part_d, *m.down)
     back = DpScatter(at, m.d_all, *m.back)
-    swap_q = dp_exchange(at, m.sum_q, m.got_q, *m.swap_q, m.local.at[1])
+    swap_q = [
+        remote(m.part_q.at[one[0]], m.landed_q.at[at.dp], m.swap_q[0].at[k], m.swap_q[1].at[k], one)
+        for k, one in enumerate(at.dp_ids())
+    ]
     ring_y.step(0)
+    stores = []
+
+    def store(key):
+        copy = pltpu.make_async_copy(getattr(m, key), getattr(m, key + "_to"), m.store.at[len(stores)])
+        copy.start()
+        stores.append(copy)
+
+    waiting = list(swap_gu)
+
+    def pace(count=1):
+        for copy in waiting[:count]:
+            copy.start()
+        del waiting[:count]
+
     loads = [
         pltpu.make_async_copy(getattr(m, key + "_in"), getattr(m, key), m.load.at[2 + k])
         for k, key in enumerate(LOADED)
@@ -981,19 +1019,23 @@
         return pltpu.make_async_copy(block, m.kv_row.at[r % 2], m.load.at[r % 2])
 
     load_kv(0).start()
+    own_gu = pltpu.make_async_copy(m.fin.at[at.seq], m.got_gu.at[at.seq], m.local.at[3])
+    own_gu.start()
 
     def norm_back(grad, value):
         scale = lax.rsqrt(jnp.mean(value * value, -1, keepdims=True) + EPS)
         normed = value * scale
         return scale * (grad - normed * jnp.mean(grad * normed, -1, keepdims=True))
 
+    for copy in loads[:3]:
+        copy.wait()
     m.dmid[...] = m.dy[...].astype(FULL) + norm_back(m.grad_h[...], m.middle[...])
     m.d_own[...] = m.dmid[...].astype(LOW)
     d_g.start()
     if ring_y.steps > 1:
         ring_y.step(1)
     d_g.hand()
-    for copy in loads:
+    for copy in loads[3:]:
         copy.wait()
     d_g.arrived()
     down.start()
@@ -1001,9 +1043,9 @@
         m.d_all[...].reshape(n_dp * tok, width), m.wo[...].reshape(q_width, width)
     ).astype(LOW)
     later = list(range(2, ring_y.steps))
+    down.across()
     if later:
         ring_y.step(later.pop(0))
-    down.across()
     for r in range(n_dp):
         rows = slice(r * tok, (r + 1) * tok)
         load_kv(r).wait()
@@ -1053,15 +1095,9 @@
     d_g.finish()
     for t in range(1, ring_kv.steps):
         ring_kv.step(t)
+        pace()
     ring_kv.finish(m.dkv)
     ring_o.step(0)
-    waiting = list(swap_gu)
-
-    def pace(count=1):
-        for copy in waiting[:count]:
-            copy.start()
-        del waiting[:count]
-
     factor = HEAD_DIM ** (-0.5)
     for g in range(groups + 1):
         cols = slice(g * pair, (g + 1) * pair)
@@ -1070,6 +1106,28 @@
         if g == groups:
             turned = jnp.where(low_head(grad.shape[0]), turned, grad)
         m.dqkv[:, cols] = turned.astype(LOW)
+    ring_y.finish(m.wide)
+    n1 = m.ring_y[0].at[0, pl.ds(0, n_dp)]
+    fetch = pltpu.make_async_copy(m.n1, n1, m.local.at[2])
+    fetch.start()
+    m.out[...] = (m.middle[...] + m.wide[...]).astype(m.out.dtype)
+    store("out")
+    pace()
+    fetch.wait()
+    for i in range(n_dp):
+        cols = slice(i * rank, (i + 1) * rank)
+        m.part_q[i] = (
+            matmul_tn(n1[:, :, cols].reshape(n_dp * tok, rank), m.dqkv[...])
+            .astype(LOW)
+            .reshape(n_seq, rank // n_seq, q_width + pair)
+        )
+    for copy in swap_q:
+        copy.start()
+    m.landed_q[at.dp] = m.part_q[at.dp]
+    pace()
+    if ring_o.steps > 1:
+        ring_o.step(1)
+    pace()
     for i in range(n_dp):
         cols = slice(i * rank, (i + 1) * rank)
         weight = m.wq[:, i].reshape(rank, q_width + pair)
@@ -1077,36 +1135,8 @@
             matmul_nt(m.dqkv[...], weight).astype(LOW).reshape(n_dp, tok, rank)
         )
     back.start()
-    pace(2)
-    ring_y.finish(m.wide)
-    n1 = m.ring_y[0].at[0, pl.ds(0, n_dp)]
-    fetch = pltpu.make_async_copy(m.n1, n1, m.local.at[2])
-    fetch.start()
-    m.out[...] = (m.middle[...] + m.wide[...]).astype(m.out.dtype)
-    down.finish(m.grad_d)
-    back.across()
     pace()
-    fetch.wait()
-    for i in range(n_dp):
-        cols = slice(i * rank, (i + 1) * rank)
-        m.part_q[:, i] = (
-            matmul_tn(n1[:, :, cols].reshape(n_dp * tok, rank), m.dqkv[...])
-            .astype(LOW)
-            .reshape(n_seq, rank // n_seq, q_width + pair)
-        )
-    ring_q.step(0)
-    pace()
-    if ring_o.steps > 1:
-        ring_o.step(1)
-    pace()
-    back.finish(m.wide)
     pace(len(waiting))
-    m.grad_x[...] = m.dmid[...] + norm_back(m.wide[...], m.x[...].astype(FULL))
-    for t in range(2, ring_o.steps):
-        ring_o.step(t)
-    for copy in swap_gu:
-        copy.wait()
-    m.got_gu[at.seq] = m.fin[at.seq]
 
     def unpack(grad, first):
         for s in range(n_seq):
@@ -1115,7 +1145,35 @@
                     s, :, first + i * ff : first + i * ff + own_ff
                 ]
 
-    jobs = [lambda: unpack(m.grad_g, 0), lambda: unpack(m.grad_u, n_dp * ff)]
+    def unpack_gate():
+        for copy in swap_gu:
+            copy.wait()
+        own_gu.wait()
+        unpack(m.grad_g, 0)
+        store("grad_g")
+
+    def unpack_up():
+        unpack(m.grad_u, n_dp * ff)
+        store("grad_u")
+
+    def grad_inputs():
+        back.finish(m.wide)
+        m.grad_x[...] = m.dmid[...] + norm_back(m.wide[...], m.x[...].astype(FULL))
+        store("grad_x")
+
+    def finish_down():
+        down.finish(m.grad_d)
+        store("grad_d")
+
+    jobs = [finish_down, back.across]
+    for t in range(2, ring_o.steps):
+        ring_o.step(t)
+        if jobs:
+            jobs.pop(0)()
+    jobs += [unpack_gate, unpack_up, grad_inputs]
+    for copy in swap_q:
+        copy.wait()
+    ring_q.step(0)
     for t in range(1, ring_q.steps):
         ring_q.step(t)
         if jobs:
@@ -1123,9 +1181,8 @@
     for job in jobs:
         job()
     ring_o.finish(m.grad_o)
-    ring_q.finish(m.sum_q)
-    swap_q.start()
-    swap_q.arrived()
+    store("grad_o")
+    ring_q.finish(m.got_q)
     m.grad_kv[...] = jnp.zeros_like(m.grad_kv)
     for i, kv in enumerate(kv_of):
         m.grad_q[:, i * q_width : (i + 1) * q_width] = m.got_q[i, :, :q_width]
@@ -1134,10 +1191,13 @@
             m.grad_kv[k, :, kv * HEAD_DIM : (kv + 1) * HEAD_DIM] += m.got_q[
                 i, :, first : first + HEAD_DIM
             ].astype(FULL)
-    swap_q.finish()
-
-
-LOADED = ("wo", "q", "o", "lse", "cos", "sin", "starts", "wq", "part_d")
+    store("grad_q")
+    store("grad_kv")
+    for copy in stores:
+        copy.wait()
+
+
+LOADED = ("grad_h", "dy", "middle", "wo", "q", "o", "lse", "cos", "sin", "starts", "wq", "part_d", "x")
 
 
 def back(n_dp, n_seq, own_ff, ff, kv_of, dtype, ins, shapes):
@@ -1147,64 +1207,66 @@
     pair = 2 * HEAD_DIM
     length = n_seq * tok
     rank, columns = ins["wq"].shape[2:]
-    outs = {
-        "out": (shape_of((tok, width), dtype), VMEM),
-        "grad_x": (shape_of((tok, width), FULL), VMEM),
-        "grad_o": (shape_of((rank, width), FULL), VMEM),
-        "grad_d": (shape_of((ff, width), FULL), VMEM),
-        "grad_q": (shape_of(shapes["q"], LOW), VMEM),
-        "grad_kv": (shape_of((2,) + shapes["k"], FULL), VMEM),
-        "grad_g": (shape_of(shapes["gate"], LOW), VMEM),
-        "grad_u": (shape_of(shapes["gate"], LOW), VMEM),
-    }
+    outs = dict(
+        out=shape_of((tok, width), dtype),
+        grad_x=shape_of((tok, width), FULL),
+        grad_o=shape_of((rank, width), FULL),
+        grad_d=shape_of((ff, width), FULL),
+        grad_q=shape_of(shapes["q"], LOW),
+        grad_kv=shape_of((2,) + shapes["k"], FULL),
+        grad_g=shape_of(shapes["gate"], LOW),
+        grad_u=shape_of(shapes["gate"], LOW),
+    )
     placed = {
         key + "_in" if key in LOADED else key: (
             value,
-            ANY if key in LOADED + ("part_y", "n1", "kv") else VMEM,
+            ANY,
         )
         for key, value in ins.items()
     }
     scratch = {key: pltpu.VMEM(ins[key].shape, ins[key].dtype) for key in LOADED}
-    scratch |= {
-        "local": dma(3),
-        "load": dma(2 + len(LOADED)),
-        "got_q": vm(LOW, n_dp, rank, columns),
-        "down": DpScatter.scratch(n_dp, ff, width),
-        "kv_row": vm(LOW, 2, n_seq, tok, pair),
-        "dmid": vm(FULL, tok, width),
-        "d_own": vm(LOW, tok, width),
-        "d_all": vm(LOW, n_dp, tok, width),
-        "d_sem": DpGather.scratch(n_dp),
-        "do": vm(LOW, every, q_width),
-        "k2": vm(LOW, length, pair),
-        "v2": vm(LOW, length, pair),
-        "mask": vm(FULL, tok, length),
-        "dk2": vm(FULL, length, pair),
-        "dv2": vm(FULL, length, pair),
-        "dq": vm(FULL, every, q_width),
-        "dkv": vm(FULL, every, pair),
-        "dqkv": vm(LOW, every, columns),
-        "wide": vm(FULL, tok, width),
-        "sum_q": vm(LOW, n_dp, rank, columns),
-        "part_kv": vm(LOW, n_seq, every, pair),
-        "part_q": vm(LOW, n_seq, n_dp, rank, columns),
-        "part_o": vm(LOW, n_seq, rank, width),
-        "back": DpScatter.scratch(n_dp, tok, width),
-        "ring_y": RingScatter.scratch(n_seq, tok, width),
-        "staged": RingScatter.staging(tok, width),
-        "ring_kv": RingScatter.scratch(n_seq, every, pair),
-        "ring_q": RingScatter.scratch(n_seq, n_dp, rank, columns),
-        "ring_o": RingScatter.scratch(n_seq, rank, width),
-        "swap_q": Exchange.scratch(n_dp),
-        "swap_gu": Exchange.scratch(n_seq),
-        "got_gu": vm(LOW, *ins["fin"].shape),
-    }
+    scratch |= {key: pltpu.VMEM(value.shape, value.dtype) for key, value in outs.items()}
+    scratch |= dict(
+        store=dma(len(outs)),
+        local=dma(4),
+        load=dma(2 + len(LOADED)),
+        got_q=vm(LOW, n_dp, rank, columns),
+        down=DpScatter.scratch(n_dp, ff, width),
+        kv_row=vm(LOW, 2, n_seq, tok, pair),
+        dmid=vm(FULL, tok, width),
+        d_own=vm(LOW, tok, width),
+        d_all=vm(LOW, n_dp, tok, width),
+        d_sem=DpGather.scratch(n_dp),
+        do=vm(LOW, every, q_width),
+        k2=vm(LOW, length, pair),
+        v2=vm(LOW, length, pair),
+        mask=vm(FULL, tok, length),
+        dk2=vm(FULL, length, pair),
+        dv2=vm(FULL, length, pair),
+        dq=vm(FULL, every, q_width),
+        dkv=vm(FULL, every, pair),
+        dqkv=vm(LOW, every, columns),
+        wide=vm(FULL, tok, width),
+        landed_q=vm(LOW, n_dp, n_seq, rank, columns),
+        part_kv=vm(LOW, n_seq, every, pair),
+        part_q=vm(LOW, n_dp, n_seq, rank, columns),
+        part_o=vm(LOW, n_seq, rank, width),
+        back=DpScatter.scratch(n_dp, tok, width),
+        ring_y=RingScatter.scratch(n_seq, tok, width),
+        staged=RingScatter.staging(tok, width),
+        ring_kv=RingScatter.scratch(n_seq, every, pair),
+        ring_q=RingScatter.scratch(n_seq, n_dp, rank, columns),
+        ring_o=RingScatter.scratch(n_seq, rank, width),
+        swap_q=Exchange.scratch(n_dp),
+        swap_gu=Exchange.scratch(n_seq),
+        got_gu=vm(LOW, *ins["fin"].shape),
+    )
     return run(
         functools.partial(back_kernel, n_dp, n_seq, own_ff, ff, kv_of),
         "attention_backward",
         3,
         placed,
-        outs,
+        {key + "_to": (value, ANY) for key, value in outs.items()},
         scratch,
     )
 
@@ -1242,22 +1304,22 @@
         n_seq,
         own_ff,
         kv_of,
-        {
-            "x": x_own,
-            "wg_in": w_gate,
-            "wu_in": w_up,
-            "wo": w_output,
-            "wd": jnp.pad(w_down, ((0, ff - own_ff), (0, 0))),
-        },
-        {
-            "wq": w_query,
-            "wk": w_key,
-            "wv": w_value,
-            "gain_one": gain_attn.reshape(1, own_rows),
-            "gain_two": gain_mlp.reshape(1, own_rows),
-            "ids": segment_ids.reshape(1, local),
-            "freqs": jnp.broadcast_to(jnp.tile(freqs, 4), (8, 2 * HEAD_DIM)),
-        },
+        dict(
+            x=x_own,
+            wg_in=w_gate,
+            wu_in=w_up,
+            wo=w_output,
+            wd=jnp.pad(w_down, ((0, ff - own_ff), (0, 0))),
+        ),
+        dict(
+            wq=w_query,
+            wk=w_key,
+            wv=w_value,
+            gain_one=gain_attn.reshape(1, own_rows),
+            gain_two=gain_mlp.reshape(1, own_rows),
+            ids=segment_ids.reshape(1, local),
+            freqs=jnp.broadcast_to(jnp.tile(freqs, 4), (8, 2 * HEAD_DIM)),
+        ),
     )
     fed = feed(
         n_dp,
@@ -1267,15 +1329,15 @@
         got["gu"].reshape(n_seq * own_rows, 2 * n_dp * ff),
         got["wd_all"],
     )
-    ins = {
-        "part_y": fed["part_y"],
-        "grad_h": fed["grad_h"],
-        "fin": fed["fin"].reshape(got["gu"].shape),
-        "part_d": fed["grad_d"],
-        "x": x_own,
-        "dy": dy_own,
-        "middle": got["middle"],
-    }
+    ins = dict(
+        part_y=fed["part_y"],
+        grad_h=fed["grad_h_to"],
+        fin=fed["fin_to"].reshape(got["gu"].shape),
+        part_d=fed["grad_d"],
+        x=x_own,
+        dy=dy_own,
+        middle=got["middle"],
+    )
     for name in ("n1", "q", "kv", "o", "lse", "cos", "sin", "starts", "wq", "wo"):
         ins[name] = got[name + "_out"]
     done = back(
@@ -1286,31 +1348,98 @@
         kv_of,
         tokens.dtype,
         ins,
-        {"q": w_query.shape, "k": w_key.shape, "gate": w_gate.shape},
-    )
-    raw_query = done["grad_q"].astype(FULL)
-    raw_key, raw_value = done["grad_kv"]
-    raw_gate = done["grad_g"].astype(FULL)
-    raw_up = done["grad_u"].astype(FULL)
-    gain_one = gain_attn.astype(FULL)[:, None]
-    gain_two = gain_mlp.astype(FULL)[:, None]
-
-    def gain_grad(*pairs):
-        return sum(jnp.sum(weight.astype(FULL) * raw, 1) for weight, raw in pairs)
-
-    return (
-        done["out"].reshape(tokens.shape),
-        done["grad_x"].reshape(tokens.shape),
-        gain_grad((w_query, raw_query), (w_key, raw_key), (w_value, raw_value)),
-        gain_one * raw_query,
-        gain_one * raw_key,
-        gain_one * raw_value,
-        done["grad_o"],
-        gain_grad((w_gate, raw_gate), (w_up, raw_up)),
-        gain_two * raw_gate,
-        gain_two * raw_up,
-        done["grad_d"][:own_ff],
-    )
+        dict(q=w_query.shape, k=w_key.shape, gate=w_gate.shape),
+    )
+    return finish(
+        {key[: -len("_to")]: value for key, value in done.items()}
+        | dict(
+            gain_one=gain_attn.reshape(1, own_rows),
+            gain_two=gain_mlp.reshape(1, own_rows),
+            wq=w_query,
+            wk=w_key,
+            wv=w_value,
+            wg=w_gate,
+            wu=w_up,
+        ),
+        tokens.shape,
+        own_ff,
+    )
+
+
+def finish_kernel(m):
+    names = ("wg", "grad_g", "wu", "grad_u", "wq", "grad_q", "grad_x", "grad_d", "out", "grad_o")
+    loads = {
+        name: pltpu.make_async_copy(getattr(m, name), getattr(m, name + "_v"), m.load.at[k])
+        for k, name in enumerate(names)
+    }
+    for copy in loads.values():
+        copy.start()
+    stores = []
+
+    def store(src, dst):
+        copy = pltpu.make_async_copy(src, dst, m.store.at[len(stores)])
+        copy.start()
+        stores.append(copy)
+
+    def one(gain, weight, raw, into):
+        raw = raw[...].astype(FULL)
+        into[...] = gain * raw
+        return jnp.sum(weight[...].astype(FULL) * raw, 1, keepdims=True)
+
+    def whole(gain, weight, raw, into, target):
+        loads[weight].wait()
+        loads[raw].wait()
+        part = one(gain, getattr(m, weight + "_v"), getattr(m, raw + "_v"), into)
+        store(into, target)
+        return part
+
+    gain_one = to_column(m.gain_one[...])
+    gain_two = to_column(m.gain_two[...])
+    by_g = whole(gain_two, "wg", "grad_g", m.into_g, m.to_g)
+    by_u = whole(gain_two, "wu", "grad_u", m.into_u, m.to_u)
+    by_q = whole(gain_one, "wq", "grad_q", m.into_q, m.to_q)
+    by_k = one(gain_one, m.wk, m.grad_kv.at[0], m.to_k)
+    by_v = one(gain_one, m.wv, m.grad_kv.at[1], m.to_v)
+    for name, target in (("grad_x", m.to_x), ("grad_d", m.to_d), ("out", m.to_out), ("grad_o", m.to_o)):
+        loads[name].wait()
+        store(getattr(m, name + "_v"), target)
+    m.to_gain_one[...] = to_row(by_q + by_k + by_v)
+    m.to_gain_two[...] = to_row(by_g + by_u)
+    for copy in stores:
+        copy.wait()
+
+
+def finish(ins, shape, own_ff):
+    rows = ins["wq"].shape[0]
+    held = ("gain_one", "gain_two", "wk", "wv", "grad_kv")
+    placed = {key: (value, VMEM if key in held else ANY) for key, value in ins.items()}
+    outs = dict(
+        to_out=(shape_of(ins["out"].shape, ins["out"].dtype), ANY),
+        to_x=(shape_of(ins["grad_x"].shape, FULL), ANY),
+        to_gain_one=(shape_of((1, rows), FULL), VMEM),
+        to_q=(shape_of(ins["wq"].shape, FULL), ANY),
+        to_k=(shape_of(ins["wk"].shape, FULL), VMEM),
+        to_v=(shape_of(ins["wv"].shape, FULL), VMEM),
+        to_o=(shape_of(ins["grad_o"].shape, FULL), ANY),
+        to_gain_two=(shape_of((1, rows), FULL), VMEM),
+        to_g=(shape_of(ins["wg"].shape, FULL), ANY),
+        to_u=(shape_of(ins["wu"].shape, FULL), ANY),
+        to_d=(shape_of(ins["grad_d"].shape, FULL), ANY),
+    )
+    scratch = dict(load=dma(10), store=dma(7))
+    for name in ("g", "u", "q"):
+        scratch["into_" + name] = vm(FULL, *ins["w" + name].shape)
+    for key, value in ins.items():
+        if key not in held:
+            scratch[key + "_v"] = pltpu.VMEM(value.shape, value.dtype)
+    done = run(finish_kernel, "finish", None, placed, outs, scratch)
+    done = list(done.values())
+    for k in (0, 1):
+        done[k] = done[k].reshape(shape)
+    for k in (2, 7):
+        done[k] = done[k].reshape(rows)
+    done[10] = done[10][:own_ff]
+    return tuple(done)
 
 
 def solution(mesh):

time: 407 us -> 390 us (0.958)
  Pallas kernels: 387 us -> 380 us
  other arithmetic: 6.48 us -> 0.01 us
    pallas_call x3 -> x4, Pallas kernels: 387 us -> 380 us  [run(): pl.pallas_call(lambda *refs: kernel(Refs(names, refs)), name=name, out_sh...]
    mul x3 -> x0, other arithmetic: 5.43 us -> none  [the longest x1 3.59 us: body(): gain_two * raw_up]
where the time goes in v5:
time: 390 us; the launch traced here: 382 us
  Pallas kernels  380 us (97%)
    pallas_call x4, Pallas kernels, run(): pl.pallas_call(lambda *refs: kernel(Refs(names, refs)), name=name, out_sh...  380 us

profile of v5, /device:TPU:0, one launch (start us, length us, event | category | flops | bytes accessed | tf_op | source)
XLA Modules:
  0.0 382.3 jit_solution(18303750701232610460)
XLA Ops:
  0.7 0.1 tile.10
  0.7 0.6 broadcast_in_dim.3.refs_11_
  1.3 99.4 %attention_forward.1 = (bf16[4,128,2048]{2,1,0:T(8,128)(2,1)}, bf16[512,512]{1,0:T(8,128)(2,1)}, bf16[8,512,128]{2,1,0:T(8,128)(2,1)}, bf16[512,512]{1,0:T(8,128...) custom-call(bf16[128,2048]{1,0:T(8,128)(2,1)} %bitcast.10, ...), custom_call_target="tpu_custom_call" | custom-call | tf_op jit(solution)/shard_map/attention_forward/pallas_call | solution.py:464
  100.8 135.4 %feed_forward.1 = (bf16[8,128,2048]{2,1,0:T(8,128)(2,1)}, f32[128,2048]{1,0:T(8,128)}, bf16[512,1408]{1,0:T(8,128)(2,1)}, bf16[4,176,2048]{2,1,0:T(8,128)(2,1)}) custom-call(bf16[128,2048]{1,0:T(8,128)(2,1)} %get-tuple-element.48.refs_0_, bf16[128,2048]{1,0:T(8,128)(2,1)} %bitcast.12, bf16[512,1408]{1,0:T(8,128)(2,1)} %bitcast.14, ...), custom_call_target="tpu_custom_call" | custom-call | tf_op jit(solution)/shard_map/feed_forward/pallas_call | solution.py:464
  236.1 139.1 %attention_backward.1 = (bf16[128,2048]{1,0:T(8,128)(2,1)}, f32[128,2048]{1,0:T(8,128)}, f32[64,2048]{1,0:T(8,128)}, f32[176,2048]{1,0:T(8,128)}, bf16[64,2048]{...) custom-call(bf16[8,128,2048]{2,1,0:T(8,128)(2,1)} %get-tuple-element.51.refs_0_, ...), custom_call_target="tpu_custom_call" | custom-call | tf_op jit(solution)/shard_map/attention_backward/pallas_call | solution.py:464
  375.3 6.6 %finish.1 = (bf16[128,2048]{1,0:T(8,128)(2,1)}, f32[128,2048]{1,0:T(8,128)}, f32[1,64]{1,0:T(1,128)}, f32[64,2048]{1,0:T(8,128)}, f32[64,256]{1,0:T(8,128)}, /*i...) custom-call(bf16[128,2048]{1,0:T(8,128)(2,1)} %get-tuple-element.66., ...), custom_call_target="tpu_custom_call" | custom-call | tf_op jit(solution)/shard_map/finish/pallas_call | solution.py:464
  (2 shorter events, 0.0 us)

commit v6 on v5

--- a/solution.py
+++ b/solution.py
@@ -1,4 +1,5 @@
 import functools
+import math
 
 import jax
 import jax.numpy as jnp
@@ -18,7 +19,7 @@
 MESH = pl.DeviceIdType.MESH
 LOW = jnp.bfloat16
 FULL = jnp.float32
-VMEM_BYTES = 60 * 1024 * 1024
+VMEM_BYTES = 61 * 1024 * 1024
 
 
 def matmul(left, right):
@@ -575,26 +576,25 @@
     for copy in loads:
         copy.start()
 
-    gain = to_column(m.gain_one[...])
     for i, kv in enumerate(kv_of):
-        m.pq[i, :, :q_width] = (
-            gain * m.wq[:, i * q_width : (i + 1) * q_width].astype(FULL)
-        ).astype(LOW)
+        m.pq[i, :, :q_width] = m.wq[:, i * q_width : (i + 1) * q_width]
         for weight, first in ((m.wk, q_width), (m.wv, q_width + HEAD_DIM)):
-            m.pq[i, :, first : first + HEAD_DIM] = (
-                gain * weight[:, kv * HEAD_DIM : (kv + 1) * HEAD_DIM].astype(FULL)
-            ).astype(LOW)
+            m.pq[i, :, first : first + HEAD_DIM] = weight[:, kv * HEAD_DIM : (kv + 1) * HEAD_DIM]
     swap_q.start()
     x_g.start()
     ids = m.ids[...]
-    m.seg_rows[...] = jnp.broadcast_to(ids[None], m.seg_rows.shape)
-    m.seg_col[...] = jnp.broadcast_to(to_column(ids).astype(jnp.int32), m.seg_col.shape)
+    rank_own = m.pq.shape[1]
+    m.seg_rows[...] = jnp.broadcast_to(ids.astype(FULL)[None], m.seg_rows.shape)
+    for k, own_gain in ((1, m.gain_one), (2, m.gain_two)):
+        m.seg_rows[:, k : k + 1, :rank_own] = jnp.broadcast_to(
+            own_gain[...].astype(FULL)[None], (n_seq, 1, rank_own)
+        )
+    m.seg_col[...] = jnp.broadcast_to(to_column(ids), m.seg_col.shape)
     row_x.start()
     col_g.start()
 
     def pack(k, weight, first):
         loads[k].wait()
-        scale = to_column(m.gain_two[...])
         if ff > own_ff:
             m.pgu[:, :, first : first + n_dp * ff] = jnp.zeros(
                 m.pgu.shape[:2] + (n_dp * ff,), LOW
@@ -602,9 +602,7 @@
         for s in range(n_seq):
             for i in range(n_dp):
                 piece = weight[:, (i * n_seq + s) * own_ff : (i * n_seq + s + 1) * own_ff]
-                m.pgu[s, :, first + i * ff : first + i * ff + own_ff] = (
-                    scale * piece.astype(FULL)
-                ).astype(LOW)
+                m.pgu[s, :, first + i * ff : first + i * ff + own_ff] = piece
 
     later = list(range(1, ring_o.steps))
     ring_o.step(later.pop(0))
@@ -621,22 +619,33 @@
 
     def norm():
         x_g.arrived()
+        row_g.arrived()
+        m.gains[...] = jnp.zeros_like(m.gains)
+        for k in (0, 1):
+            for i in range(n_dp):
+                for s in range(n_seq):
+                    first = (i * n_seq + s) * rank_own
+                    m.gains[k : k + 1, first : first + rank_own] = m.segs[
+                        i, s, k + 1 : k + 2, :rank_own
+                    ]
+        store(m.gains, m.gains_out)
         for r in range(n_dp):
             x = m.xs[r].astype(FULL)
             scale = lax.rsqrt(jnp.mean(x * x, -1, keepdims=True) + EPS)
-            m.n1[r] = (x * scale).astype(LOW)
+            m.n1[r] = (x * scale * m.gains[:1]).astype(LOW)
         store(m.n1, m.n1_out)
 
     def place():
-        row_g.arrived()
         col_g.arrived()
         position = own_positions(at, tok)
         first = lax.rem(lanes(tok), HEAD_DIM) < HEAD_DIM // 2
+        number = lax.rem(lanes(tok), HEAD_DIM // 2).astype(FULL)
+        freqs = jnp.exp(number * (-2.0 * math.log(ROPE_BASE) / HEAD_DIM))
         for r in range(n_dp):
             segs = jnp.concatenate([m.segs[r, s, :1] for s in range(n_seq)], 1)
             own = m.seg_cols[r][:, :1]
             start = jnp.sum((segs < own).astype(jnp.int32), 1, keepdims=True)
-            turned = (position - start).astype(FULL) * m.freqs[:1]
+            turned = (position - start).astype(FULL) * freqs
             rows = slice(r * tok, (r + 1) * tok)
             m.cos[rows] = jnp.cos(turned)
             sines = jnp.sin(turned)
@@ -726,7 +735,7 @@
     middle = m.x_own[...].astype(FULL) + m.middle[...]
     m.middle[...] = middle
     scale = lax.rsqrt(jnp.mean(middle * middle, -1, keepdims=True) + EPS)
-    m.second[...] = (middle * scale).astype(LOW)
+    m.second[...] = (middle * scale * m.gains[1:2]).astype(LOW)
     swap_gu.arrived()
     down.arrived()
     for one in (swap_q, x_g, row_x, row_g, col_g, swap_gu, down):
@@ -758,6 +767,7 @@
         cos=(FULL, every, pair),
         sin=(FULL, every, pair),
         starts=(jnp.int32, every, pair),
+        gains=(FULL, 8, width),
         wq_all=(LOW, n_seq, n_dp, rank, columns),
         wo_all=(LOW, n_seq, rank, width),
     )
@@ -776,13 +786,13 @@
         wu=vm(LOW, *held["wg_in"].shape),
         x_own=vm(LOW, tok, width),
         pq=vm(LOW, n_dp, rank, columns),
-        seg_rows=vm(jnp.int32, n_seq, 8, tok),
-        seg_col=vm(jnp.int32, tok, pair),
+        seg_rows=vm(FULL, n_seq, 8, tok),
+        seg_col=vm(FULL, tok, pair),
         landed=vm(LOW, n_dp, rank, columns),
         xs=vm(LOW, n_dp, tok, width),
-        seg_row=vm(jnp.int32, n_seq, 8, tok),
-        segs=vm(jnp.int32, n_dp, n_seq, 8, tok),
-        seg_cols=vm(jnp.int32, n_dp, tok, pair),
+        seg_row=vm(FULL, n_seq, 8, tok),
+        segs=vm(FULL, n_dp, n_seq, 8, tok),
+        seg_cols=vm(FULL, n_dp, tok, pair),
         kv_own=vm(LOW, every, pair),
         mask=vm(FULL, tok, length),
         pgu=vm(LOW, n_seq, rank, gu_width),
@@ -1022,20 +1032,23 @@
     own_gu = pltpu.make_async_copy(m.fin.at[at.seq], m.got_gu.at[at.seq], m.local.at[3])
     own_gu.start()
 
-    def norm_back(grad, value):
+    def norm_back(grad, gain, value):
+        grad = grad * gain
         scale = lax.rsqrt(jnp.mean(value * value, -1, keepdims=True) + EPS)
         normed = value * scale
         return scale * (grad - normed * jnp.mean(grad * normed, -1, keepdims=True))
 
-    for copy in loads[:3]:
+    for copy in loads[:4]:
         copy.wait()
-    m.dmid[...] = m.dy[...].astype(FULL) + norm_back(m.grad_h[...], m.middle[...])
+    m.dmid[...] = m.dy[...].astype(FULL) + norm_back(
+        m.grad_h[...], m.gains[1:2], m.middle[...]
+    )
     m.d_own[...] = m.dmid[...].astype(LOW)
     d_g.start()
     if ring_y.steps > 1:
         ring_y.step(1)
     d_g.hand()
-    for copy in loads[3:]:
+    for copy in loads[4:]:
         copy.wait()
     d_g.arrived()
     down.start()
@@ -1158,7 +1171,9 @@
 
     def grad_inputs():
         back.finish(m.wide)
-        m.grad_x[...] = m.dmid[...] + norm_back(m.wide[...], m.x[...].astype(FULL))
+        m.grad_x[...] = m.dmid[...] + norm_back(
+            m.wide[...], m.gains[:1], m.x[...].astype(FULL)
+        )
         store("grad_x")
 
     def finish_down():
@@ -1197,7 +1212,7 @@
         copy.wait()
 
 
-LOADED = ("grad_h", "dy", "middle", "wo", "q", "o", "lse", "cos", "sin", "starts", "wq", "part_d", "x")
+LOADED = ("grad_h", "dy", "middle", "gains", "wo", "q", "o", "lse", "cos", "sin", "starts", "wq", "part_d", "x")
 
 
 def back(n_dp, n_seq, own_ff, ff, kv_of, dtype, ins, shapes):
@@ -1298,7 +1313,6 @@
     dy_own = cotangent.reshape(local, width)
 
     kv_of = [i * heads // GROUP for i in range(n_dp)]
-    freqs = ROPE_BASE ** (-jnp.arange(0, HEAD_DIM, 2).astype(FULL) / HEAD_DIM)
     got = front(
         n_dp,
         n_seq,
@@ -1318,7 +1332,6 @@
             gain_one=gain_attn.reshape(1, own_rows),
             gain_two=gain_mlp.reshape(1, own_rows),
             ids=segment_ids.reshape(1, local),
-            freqs=jnp.broadcast_to(jnp.tile(freqs, 4), (8, 2 * HEAD_DIM)),
         ),
     )
     fed = feed(
@@ -1338,7 +1351,7 @@
         dy=dy_own,
         middle=got["middle"],
     )
-    for name in ("n1", "q", "kv", "o", "lse", "cos", "sin", "starts", "wq", "wo"):
+    for name in ("n1", "q", "kv", "o", "lse", "cos", "sin", "starts", "gains", "wq", "wo"):
         ins[name] = got[name + "_out"]
     done = back(
         n_dp,
@@ -1367,7 +1380,7 @@
 
 
 def finish_kernel(m):
-    names = ("wg", "grad_g", "wu", "grad_u", "wq", "grad_q", "grad_x", "grad_d", "out", "grad_o")
+    names = ("wg", "grad_g", "grad_x", "grad_d", "out", "grad_o", "wu", "grad_u", "wq", "grad_q")
     loads = {
         name: pltpu.make_async_copy(getattr(m, name), getattr(m, name + "_v"), m.load.at[k])
         for k, name in enumerate(names)
@@ -1381,30 +1394,28 @@
         copy.start()
         stores.append(copy)
 
-    def one(gain, weight, raw, into):
+    def one(weight, raw, into):
         raw = raw[...].astype(FULL)
-        into[...] = gain * raw
+        into[...] = raw
         return jnp.sum(weight[...].astype(FULL) * raw, 1, keepdims=True)
 
-    def whole(gain, weight, raw, into, target):
+    def whole(weight, raw, into, target):
         loads[weight].wait()
         loads[raw].wait()
-        part = one(gain, getattr(m, weight + "_v"), getattr(m, raw + "_v"), into)
+        part = one(getattr(m, weight + "_v"), getattr(m, raw + "_v"), into)
         store(into, target)
         return part
 
-    gain_one = to_column(m.gain_one[...])
-    gain_two = to_column(m.gain_two[...])
-    by_g = whole(gain_two, "wg", "grad_g", m.into_g, m.to_g)
-    by_u = whole(gain_two, "wu", "grad_u", m.into_u, m.to_u)
-    by_q = whole(gain_one, "wq", "grad_q", m.into_q, m.to_q)
-    by_k = one(gain_one, m.wk, m.grad_kv.at[0], m.to_k)
-    by_v = one(gain_one, m.wv, m.grad_kv.at[1], m.to_v)
+    by_g = whole("wg", "grad_g", m.into_g, m.to_g)
     for name, target in (("grad_x", m.to_x), ("grad_d", m.to_d), ("out", m.to_out), ("grad_o", m.to_o)):
         loads[name].wait()
         store(getattr(m, name + "_v"), target)
-    m.to_gain_one[...] = to_row(by_q + by_k + by_v)
-    m.to_gain_two[...] = to_row(by_g + by_u)
+    by_u = whole("wu", "grad_u", m.into_u, m.to_u)
+    by_q = whole("wq", "grad_q", m.into_q, m.to_q)
+    by_k = one(m.wk, m.grad_kv.at[0], m.to_k)
+    by_v = one(m.wv, m.grad_kv.at[1], m.to_v)
+    m.to_gain_one[...] = to_row(by_q + by_k + by_v) / m.gain_one[...].astype(FULL)
+    m.to_gain_two[...] = to_row(by_g + by_u) / m.gain_two[...].astype(FULL)
     for copy in stores:
         copy.wait()
 

time: 390 us -> 389 us (level)
  no operation moved by 1% of the time
where the time goes in v6:
time: 389 us; the launch traced here: 382 us
  Pallas kernels  381 us (98%)
    pallas_call x4, Pallas kernels, run(): pl.pallas_call(lambda *refs: kernel(Refs(names, refs)), name=name, out_sh...  381 us

profile of v6, /device:TPU:0, one launch (start us, length us, event | category | flops | bytes accessed | tf_op | source)
XLA Modules:
  0.0 382.0 jit_solution(12544475028639696021)
XLA Ops:
  0.6 99.6 %attention_forward.1 = (bf16[4,128,2048]{2,1,0:T(8,128)(2,1)}, bf16[512,512]{1,0:T(8,128)(2,1)}, bf16[8,512,128]{2,1,0:T(8,128)(2,1)}, bf16[512,512]{1,0:T(8,128...) custom-call(bf16[128,2048]{1,0:T(8,128)(2,1)} %bitcast.10, ...), custom_call_target="tpu_custom_call" | custom-call | tf_op jit(solution)/shard_map/attention_forward/pallas_call | solution.py:465
  100.2 135.2 %feed_forward.1 = (bf16[8,128,2048]{2,1,0:T(8,128)(2,1)}, f32[128,2048]{1,0:T(8,128)}, bf16[512,1408]{1,0:T(8,128)(2,1)}, bf16[4,176,2048]{2,1,0:T(8,128)(2,1)}) custom-call(bf16[128,2048]{1,0:T(8,128)(2,1)} %get-tuple-element.49.refs_0_, bf16[128,2048]{1,0:T(8,128)(2,1)} %bitcast.12, bf16[512,1408]{1,0:T(8,128)(2,1)} %bitcast.14, ...), custom_call_target="tpu_custom_call" | custom-call | tf_op jit(solution)/shard_map/feed_forward/pallas_call | solution.py:465
  235.4 139.1 %attention_backward.1 = (bf16[128,2048]{1,0:T(8,128)(2,1)}, f32[128,2048]{1,0:T(8,128)}, f32[64,2048]{1,0:T(8,128)}, f32[176,2048]{1,0:T(8,128)}, bf16[64,2048]{...) custom-call(bf16[8,128,2048]{2,1,0:T(8,128)(2,1)} %get-tuple-element.52.refs_0_, ...), custom_call_target="tpu_custom_call" | custom-call | tf_op jit(solution)/shard_map/attention_backward/pallas_call | solution.py:465
  374.6 7.0 %finish.1 = (bf16[128,2048]{1,0:T(8,128)(2,1)}, f32[128,2048]{1,0:T(8,128)}, f32[1,64]{1,0:T(1,128)}, f32[64,2048]{1,0:T(8,128)}, f32[64,256]{1,0:T(8,128)}, /*i...) custom-call(bf16[128,2048]{1,0:T(8,128)(2,1)} %get-tuple-element.68., ...), custom_call_target="tpu_custom_call" | custom-call | tf_op jit(solution)/shard_map/finish/pallas_call | solution.py:465

commit v7 on v6

--- a/solution.py
+++ b/solution.py
@@ -695,6 +695,7 @@
         ring_o.step(t)
     down.hand()
     ring_kv.finish()
+    swap_gu.start(2)
     store(m.kv_all, m.kv_out)
     m.lse[...] = jnp.zeros_like(m.lse)
     for r in range(n_dp):

time: 389 us -> 387 us (level)
  no operation moved by 1% of the time
where the time goes in v7:
time: 387 us; the launch traced here: 379 us
  Pallas kernels  378 us (98%)
    pallas_call x4, Pallas kernels, run(): pl.pallas_call(lambda *refs: kernel(Refs(names, refs)), name=name, out_sh...  378 us

profile of v7, /device:TPU:0, one launch (start us, length us, event | category | flops | bytes accessed | tf_op | source)
XLA Modules:
  0.0 379.3 jit_solution(3671501696605941983)
XLA Ops:
  0.6 99.6 %attention_forward.1 = (bf16[4,128,2048]{2,1,0:T(8,128)(2,1)}, bf16[512,512]{1,0:T(8,128)(2,1)}, bf16[8,512,128]{2,1,0:T(8,128)(2,1)}, bf16[512,512]{1,0:T(8,128...) custom-call(bf16[128,2048]{1,0:T(8,128)(2,1)} %bitcast.10, ...), custom_call_target="tpu_custom_call" | custom-call | tf_op jit(solution)/shard_map/attention_forward/pallas_call | solution.py:465
  100.2 132.7 %feed_forward.1 = (bf16[8,128,2048]{2,1,0:T(8,128)(2,1)}, f32[128,2048]{1,0:T(8,128)}, bf16[512,1408]{1,0:T(8,128)(2,1)}, bf16[4,176,2048]{2,1,0:T(8,128)(2,1)}) custom-call(bf16[128,2048]{1,0:T(8,128)(2,1)} %get-tuple-element.49.refs_0_, bf16[128,2048]{1,0:T(8,128)(2,1)} %bitcast.12, bf16[512,1408]{1,0:T(8,128)(2,1)} %bitcast.14, ...), custom_call_target="tpu_custom_call" | custom-call | tf_op jit(solution)/shard_map/feed_forward/pallas_call | solution.py:465
  232.9 138.9 %attention_backward.1 = (bf16[128,2048]{1,0:T(8,128)(2,1)}, f32[128,2048]{1,0:T(8,128)}, f32[64,2048]{1,0:T(8,128)}, f32[176,2048]{1,0:T(8,128)}, bf16[64,2048]{...) custom-call(bf16[8,128,2048]{2,1,0:T(8,128)(2,1)} %get-tuple-element.52.refs_0_, ...), custom_call_target="tpu_custom_call" | custom-call | tf_op jit(solution)/shard_map/attention_backward/pallas_call | solution.py:465
  371.8 7.0 %finish.1 = (bf16[128,2048]{1,0:T(8,128)(2,1)}, f32[128,2048]{1,0:T(8,128)}, f32[1,64]{1,0:T(1,128)}, f32[64,2048]{1,0:T(8,128)}, f32[64,256]{1,0:T(8,128)}, /*i...) custom-call(bf16[128,2048]{1,0:T(8,128)(2,1)} %get-tuple-element.68., ...), custom_call_target="tpu_custom_call" | custom-call | tf_op jit(solution)/shard_map/finish/pallas_call | solution.py:465

commit v8 on v7

--- a/solution.py
+++ b/solution.py
@@ -698,8 +698,11 @@
     swap_gu.start(2)
     store(m.kv_all, m.kv_out)
     m.lse[...] = jnp.zeros_like(m.lse)
-    for r in range(n_dp):
-        rows = slice(r * tok, (r + 1) * tok)
+    back = DpScatter(at, m.parts, *m.back)
+    chips = [lax.rem(at.chip + k, at.chips) for k in range(1, at.chips)] + [at.chip]
+    order = [2 * chip + c for chip in chips for c in (1 - at.core, at.core)]
+    for place_of, r in enumerate(order):
+        rows = rows_of(r, tok)
         k, v = spread_kv(m.kv_all[:, rows].reshape(length, 2 * HEAD_DIM))
         m.k2[...] = k
         m.v2[...] = v
@@ -719,18 +722,17 @@
             return carry
 
         lax.fori_loop(0, groups, group, 0)
-        if r == 0:
+        if place_of == 0:
             swap_gu.start()
+            ring_o.finish()
+            store(m.wo_all, m.wo_out)
+        m.parts[r] = matmul(m.o[rows], m.wo_all[...].reshape(q_width, width)).astype(LOW)
+        if place_of % 2 == 0:
+            back.to_core(chips[place_of // 2]).start()
+        if place_of == n_dp - 2:
+            back.across()
     store(m.o, m.o_out)
     store(m.lse, m.lse_out)
-    ring_o.finish()
-    store(m.wo_all, m.wo_out)
-    full = m.wo_all[...].reshape(q_width, width)
-    for r in range(n_dp):
-        m.parts[r] = matmul(m.o[r * tok : (r + 1) * tok], full).astype(LOW)
-    back = DpScatter(at, m.parts, *m.back)
-    back.start()
-    back.across()
     back.finish(m.middle)
     loads[2].wait()
     middle = m.x_own[...].astype(FULL) + m.middle[...]

time: 387 us -> 387 us (level)
  no operation moved by 1% of the time
where the time goes in v8:
time: 387 us; the launch traced here: 380 us
  Pallas kernels  378 us (98%)
    pallas_call x4, Pallas kernels, run(): pl.pallas_call(lambda *refs: kernel(Refs(names, refs)), name=name, out_sh...  378 us

profile of v8, /device:TPU:0, one launch (start us, length us, event | category | flops | bytes accessed | tf_op | source)
XLA Modules:
  0.0 379.6 jit_solution(12967752385614219835)
XLA Ops:
  0.6 93.9 %attention_forward.1 = (bf16[4,128,2048]{2,1,0:T(8,128)(2,1)}, bf16[512,512]{1,0:T(8,128)(2,1)}, bf16[8,512,128]{2,1,0:T(8,128)(2,1)}, bf16[512,512]{1,0:T(8,128...) custom-call(bf16[128,2048]{1,0:T(8,128)(2,1)} %bitcast.10, ...), custom_call_target="tpu_custom_call" | custom-call | tf_op jit(solution)/shard_map/attention_forward/pallas_call | solution.py:465
  94.5 138.4 %feed_forward.1 = (bf16[8,128,2048]{2,1,0:T(8,128)(2,1)}, f32[128,2048]{1,0:T(8,128)}, bf16[512,1408]{1,0:T(8,128)(2,1)}, bf16[4,176,2048]{2,1,0:T(8,128)(2,1)}) custom-call(bf16[128,2048]{1,0:T(8,128)(2,1)} %get-tuple-element.49.refs_0_, bf16[128,2048]{1,0:T(8,128)(2,1)} %bitcast.12, bf16[512,1408]{1,0:T(8,128)(2,1)} %bitcast.14, ...), custom_call_target="tpu_custom_call" | custom-call | tf_op jit(solution)/shard_map/feed_forward/pallas_call | solution.py:465
  233.0 139.2 %attention_backward.1 = (bf16[128,2048]{1,0:T(8,128)(2,1)}, f32[128,2048]{1,0:T(8,128)}, f32[64,2048]{1,0:T(8,128)}, f32[176,2048]{1,0:T(8,128)}, bf16[64,2048]{...) custom-call(bf16[8,128,2048]{2,1,0:T(8,128)(2,1)} %get-tuple-element.52.refs_0_, ...), custom_call_target="tpu_custom_call" | custom-call | tf_op jit(solution)/shard_map/attention_backward/pallas_call | solution.py:465
  372.1 7.0 %finish.1 = (bf16[128,2048]{1,0:T(8,128)(2,1)}, f32[128,2048]{1,0:T(8,128)}, f32[1,64]{1,0:T(1,128)}, f32[64,2048]{1,0:T(8,128)}, f32[64,256]{1,0:T(8,128)}, /*i...) custom-call(bf16[128,2048]{1,0:T(8,128)(2,1)} %get-tuple-element.68., ...), custom_call_target="tpu_custom_call" | custom-call | tf_op jit(solution)/shard_map/finish/pallas_call | solution.py:465
